TPU v7x, 32 devices: a whole 2x2x4 slice. The times are simulated.
32 devices in a mesh: dp: 8 (over y, x, core), tm: 4 (over z).
Axes of the slice: x: 2, y: 2, z: 4, core: 2. Of those that a mesh axis runs over, the one named last changes fastest.
Arguments:
- tokens: bfloat16 [32, 2048, 512], P('dp', 'tm'), may hold values from -6 to 6
- lengths: int32 [32, 3], P('dp'), may hold values from 128 to 1791, as said below
- style: bfloat16 [32, 3, 128], P('dp'), may hold values from -6 to 6
- fc1_weight: bfloat16 [128, 1024], replicated, may hold values from -0.375 to 0.375
- fc1_bias: bfloat16 [1024], replicated, may hold values from -3 to 3
- conv1_kernel: bfloat16 [3, 512, 512], replicated, may hold values from -0.15625 to 0.15625
- fc2_weight: bfloat16 [128, 1024], replicated, may hold values from -0.375 to 0.375
- fc2_bias: bfloat16 [1024], replicated, may hold values from -3 to 3
- conv2_kernel: bfloat16 [3, 512, 512], replicated, may hold values from -0.15625 to 0.15625
- conv2_bias: bfloat16 [512], replicated, may hold values from -3 to 3
- out_grad: bfloat16 [32, 2048, 512], P('dp', 'tm'), may hold values from -6 to 6
Outputs:
- block_out: bfloat16 [32, 2048, 512], P('dp', 'tm')
- input_grad: bfloat16 [32, 2048, 512], P('dp', 'tm')
- style_grad: float32 [32, 3, 128], P('dp')
- fc1_weight_grad: float32 [128, 1024], replicated
- fc1_bias_grad: float32 [1024], replicated
- conv1_kernel_grad: float32 [3, 512, 512], replicated
- fc2_weight_grad: float32 [128, 1024], replicated
- fc2_bias_grad: float32 [1024], replicated
- conv2_kernel_grad: float32 [3, 512, 512], replicated
- conv2_bias_grad: float32 [512], replicated
Inputs may be any that keep to these rules, and one draw needn't show every extreme that they name: `lengths`: every row ends in at least one frame of padding. Of each row's 3 utterances all but one have 512 // 4 to 170 frames, one of them exactly 128; the remaining one begins among the row's first 512 frames and ends among its last 512 frames.
All inputs are finite; a program needn't handle non-finite values.
Results may differ from a plain program's by a relative error of at most 0.0078.
Values may be sent and summed in bfloat16 or wider, within the bound.
No kernel may reach another device: no remote copies, remote signals or barrier semaphores. Data moves between devices by JAX's collectives and lax.ppermute only.
A program may use at most 128 MiB of HBM per device.

v0:
```python
import functools

import jax
import jax.numpy as jnp
from jax import lax
from jax.experimental import pallas as pl
from jax.experimental.pallas import tpu as pltpu
from jax.sharding import Mesh, PartitionSpec as P

EPSILON = 1e-05
ROOT_HALF = 0.7071067811865476
SEGS = 3
PAD = 16
CHUNK = 64
EDGE = 8 + 16
F32 = jnp.float32
BF16 = jnp.bfloat16
VMEM_MIB = 32


class Row:
    def __init__(self, len_ref, r, frames):
        self.frames = frames
        self.z = lax.axis_index("tm")
        self.counts = [len_ref[r, s] for s in range(SEGS)]
        l0, l1, l2 = self.counts
        start = -self.z * frames
        e0 = start + l0
        e1 = e0 + l1
        e2 = e1 + l2
        self.begins = [start, e0, e1]
        self.ends = [e0, e1, e2]
        self.long_at = jnp.where(l0 >= jnp.maximum(l1, l2), 0, jnp.where(l1 >= l2, 1, 2))
        self.long_begin = self.of_long(self.begins)
        self.long_end = self.of_long(self.ends)

    def of_long(self, values):
        return jnp.where(
            self.long_at == 0, values[0], jnp.where(self.long_at == 1, values[1], values[2])
        )

    def segment(self, t):
        return sum((t >= e).astype(jnp.int32) for e in self.ends)

    def chunks(self, uniform_fn, mixed_fn):
        def body(i, carry):
            t0 = pl.multiple_of(i * CHUNK, CHUNK)
            first, last = self.segment(t0), self.segment(t0 + CHUNK - 1)
            uniform = jnp.logical_and(first == last, first < SEGS)

            @pl.when(uniform)
            def _():
                uniform_fn(t0, first)

            @pl.when(jnp.logical_not(uniform))
            def _():
                mixed_fn(t0)

            return carry

        lax.fori_loop(0, self.frames // CHUNK, body, 0)


def frame_ids(t0, rows, width):
    return t0 + lax.broadcasted_iota(jnp.int32, (rows, width), 0)


def pick(tab_ref, base, t, row):
    value = jnp.where(t >= row.ends[0], tab_ref[base + 1 : base + 2, :], tab_ref[base : base + 1, :])
    return jnp.where(t >= row.ends[1], tab_ref[base + 2 : base + 3, :], value)


def row_of(tab_ref, base, s):
    return tab_ref[pl.ds(base + s, 1), :]


def fold(x):
    return jnp.sum(x.reshape(x.shape[0] // 8, 8, x.shape[1]), axis=0)


def add_sums(acc_ref, s, first, second):
    acc_ref[s] += fold(first)
    acc_ref[4 + s] += fold(second)


def add_masked_sums(acc_ref, t, row, first, second):
    for s in range(SEGS):
        inside = jnp.logical_and(t >= row.begins[s], t < row.ends[s])
        add_sums(acc_ref, s, jnp.where(inside, first, 0.0), jnp.where(inside, second, 0.0))


def put_sums(acc_ref, st_ref, msg_ref, row, r):
    for s in range(SEGS):
        st_ref[s : s + 1, :] = jnp.sum(acc_ref[s], axis=0, keepdims=True)
        st_ref[SEGS + s : SEGS + s + 1, :] = jnp.sum(acc_ref[4 + s], axis=0, keepdims=True)
    st_ref[6:8, :] = jnp.zeros((2, st_ref.shape[1]), F32)
    for k in range(2):
        value = jnp.sum(acc_ref[4 * k + row.long_at], axis=0, keepdims=True)
        for d in range(msg_ref.shape[0]):
            msg_ref[d, pl.ds(2 * r + k, 1), :] = value


def sums_of(row, r, st_ref, rx_ref, s):
    out = []
    for k in range(2):
        total = rx_ref[0, pl.ds(2 * r + k, 1), :]
        for d in range(1, rx_ref.shape[0]):
            total = total + rx_ref[d, pl.ds(2 * r + k, 1), :]
        local = st_ref[SEGS * k + s : SEGS * k + s + 1, :]
        out.append(jnp.where(row.long_at == s, total, local))
    return out


def norm_of(row, r, st_ref, rx_ref, aff_ref, s):
    width = st_ref.shape[1]
    first, second = sums_of(row, r, st_ref, rx_ref, s)
    count = jnp.full((1, width), row.counts[s].astype(F32))
    mean = first / count
    rstd = lax.rsqrt(second / count - mean * mean + EPSILON)
    affine = aff_ref[pl.ds(SEGS * r + s, 1), :]
    return mean, rstd, 1.0 + affine[:, :width], affine[:, width:], count


def put_forward(row, r, st_ref, rx_ref, aff_ref, tab_ref):
    scales, shifts = [], []
    for s in range(SEGS):
        mean, rstd, gain, beta, _ = norm_of(row, r, st_ref, rx_ref, aff_ref, s)
        scales.append(gain * rstd)
        shifts.append(beta - mean * scales[-1])
        tab_ref[s : s + 1, :] = scales[s]
        tab_ref[SEGS + s : SEGS + s + 1, :] = shifts[s]
    tab_ref[6:7, :] = row.of_long(scales)
    tab_ref[7:8, :] = row.of_long(shifts)


def put_backward(row, r, st_ref, rx_ref, gst_ref, grx_ref, aff_ref, tab_ref):
    parts = [[], [], []]
    for s in range(SEGS):
        mean, rstd, gain, _, count = norm_of(row, r, st_ref, rx_ref, aff_ref, s)
        shift, scale = sums_of(row, r, gst_ref, grx_ref, s)
        scale = rstd * (scale - mean * shift)
        mean_g = gain * shift / count
        slope = rstd * rstd * (gain * scale / count)
        parts[0].append(gain * rstd)
        parts[1].append(-slope)
        parts[2].append(slope * mean - rstd * mean_g)
    for k in range(3):
        for s in range(SEGS):
            tab_ref[SEGS * k + s : SEGS * k + s + 1, :] = parts[k][s]
        tab_ref[9 + k : 10 + k, :] = row.of_long(parts[k])


def put_affine_grads(row, r, st_ref, rx_ref, gst_ref, aff_ref, out_ref, at):
    width = st_ref.shape[1]
    for s in range(SEGS):
        mean, rstd, _, _, _ = norm_of(row, r, st_ref, rx_ref, aff_ref, s)
        shift = gst_ref[s : s + 1, :]
        scale = rstd * (gst_ref[SEGS + s : SEGS + s + 1, :] - mean * shift)
        out_ref[pl.ds(4 * r + s, 1), at : at + width] = scale
        out_ref[pl.ds(4 * r + s, 1), at + width : at + 2 * width] = shift


def silu(a):
    half = 0.5 * a
    return half + half * jnp.tanh(half)


def silu_and_slope(a):
    gate = 0.5 + 0.5 * jnp.tanh(0.5 * a)
    low = a * gate
    return low, gate + low * (1.0 - gate)


def halo_tile(row, frames, width, left):
    t = frame_ids(-PAD if left else frames, PAD, width)
    near = jnp.logical_and(t >= -2, t < frames + 2)
    inside = jnp.logical_and(t >= row.long_begin, t < row.long_end)
    return t, jnp.logical_and(near, inside)


def edge_tile(rx_ref, row, r, t, at, left):
    last = rx_ref.shape[0] - 1
    source = jnp.maximum(row.z - 1, 0) if left else jnp.minimum(row.z + 1, last)
    e0 = rx_ref[source, pl.ds(8 + 4 * r + at, 1), :]
    e1 = rx_ref[source, pl.ds(8 + 4 * r + at + 1, 1), :]
    second = -1 if left else row.frames + 1
    return jnp.where(t == second, e1, e0)


def stack_taps(buf_ref, xs_ref, row, frames, forward, halo, low_ref=None):
    width = buf_ref.shape[1]
    before_at, after_at = (0, 2 * width) if forward else (2 * width, 0)
    base = PAD if halo else 0
    for i in range(frames // CHUNK):
        o, d = PAD + i * CHUNK, base + i * CHUNK
        centre = buf_ref[o : o + CHUNK, :].astype(BF16)
        xs_ref[d : d + CHUNK, width : 2 * width] = centre
        xs_ref[d : d + CHUNK, before_at : before_at + width] = buf_ref[o - 1 : o - 1 + CHUNK, :].astype(BF16)
        xs_ref[d : d + CHUNK, after_at : after_at + width] = buf_ref[o + 1 : o + 1 + CHUNK, :].astype(BF16)
        if low_ref is not None:
            low_ref[0, i * CHUNK : (i + 1) * CHUNK, :] = centre
    if halo:
        end = PAD + frames
        left, right = buf_ref[0:PAD, :], buf_ref[end : end + PAD, :]
        xs_ref[0:PAD, width : 2 * width] = left.astype(BF16)
        xs_ref[end : end + PAD, width : 2 * width] = right.astype(BF16)
        xs_ref[0:PAD, before_at : before_at + width] = pltpu.roll(left, 1, 0).astype(BF16)
        xs_ref[end : end + PAD, before_at : before_at + width] = buf_ref[end - 1 : end - 1 + PAD, :].astype(BF16)
        xs_ref[0:PAD, after_at : after_at + width] = buf_ref[1 : 1 + PAD, :].astype(BF16)
        xs_ref[end : end + PAD, after_at : after_at + width] = pltpu.roll(right, PAD - 1, 0).astype(BF16)
    for end in row.ends[:2]:
        for at, t in ((before_at, end), (after_at, end - 1)):

            @pl.when(jnp.logical_and(t >= 0, t < frames))
            def _(at=at, t=t):
                tile = pl.multiple_of((t // PAD) * PAD, PAD)
                rows = pl.ds(base + tile, PAD)
                value = xs_ref[rows, at : at + width].astype(F32)
                keep = frame_ids(tile, PAD, width) != t
                xs_ref[rows, at : at + width] = jnp.where(keep, value, 0.0).astype(BF16)


def times_transposed(xs, w_ref, width):
    out = None
    for k in range(3):
        part = lax.dot_general(
            xs[:, k * width : (k + 1) * width],
            w_ref[k * width : (k + 1) * width, :],
            (((1,), (1,)), ((), ())),
            preferred_element_type=F32,
        )
        out = part if out is None else out + part
    return out


def token_sums_kernel(len_ref, tok_ref, tok_head, tok_tail, og_head, og_tail, st_ref, msg_ref, acc_ref):
    r = pl.program_id(0)
    frames, width = tok_ref.shape[1:]
    row = Row(len_ref, r, frames)
    acc_ref[...] = jnp.zeros_like(acc_ref)

    def uniform(t0, s):
        v = tok_ref[0, pl.ds(t0, CHUNK), :].astype(F32)
        add_sums(acc_ref, s, v, v * v)

    def mixed(t0):
        v = tok_ref[0, pl.ds(t0, CHUNK), :].astype(F32)
        add_masked_sums(acc_ref, frame_ids(t0, CHUNK, width), row, v, v * v)

    row.chunks(uniform, mixed)
    put_sums(acc_ref, st_ref, msg_ref, row, r)
    for j, (head, tail) in enumerate(((tok_head, tok_tail), (og_head, og_tail))):
        first, last = head[0].astype(F32), tail[0].astype(F32)
        for i in range(2):
            to_left, to_right = first[i : i + 1, :], last[PAD - 2 + i : PAD - 1 + i, :]
            for d in range(msg_ref.shape[0]):
                msg_ref[d, pl.ds(8 + 4 * r + 2 * j + i, 1), :] = jnp.where(row.z < d, to_right, to_left)


def first_half_kernel(len_ref, tok_ref, st_ref, rx_ref, aff_ref, w_ref, low_ref, hid_ref, st2_ref, msg_ref,
                      buf_ref, xs_ref, tab_ref, acc_ref):
    r = pl.program_id(0)
    frames, width = tok_ref.shape[1:]
    row = Row(len_ref, r, frames)
    put_forward(row, r, st_ref, rx_ref, aff_ref, tab_ref)

    def uniform(t0, s):
        v = tok_ref[0, pl.ds(t0, CHUNK), :].astype(F32)
        buf_ref[pl.ds(PAD + t0, CHUNK), :] = silu(v * row_of(tab_ref, 0, s) + row_of(tab_ref, SEGS, s))

    def mixed(t0):
        t = frame_ids(t0, CHUNK, width)
        v = tok_ref[0, pl.ds(t0, CHUNK), :].astype(F32)
        low = silu(v * pick(tab_ref, 0, t, row) + pick(tab_ref, SEGS, t, row))
        buf_ref[pl.ds(PAD + t0, CHUNK), :] = jnp.where(t < row.ends[2], low, 0.0)

    row.chunks(uniform, mixed)
    for left in (True, False):
        t, valid = halo_tile(row, frames, width, left)
        low = silu(edge_tile(rx_ref, row, r, t, 0, left) * tab_ref[6:7, :] + tab_ref[7:8, :])
        at = 0 if left else PAD + frames
        buf_ref[at : at + PAD, :] = jnp.where(valid, low, 0.0)
    stack_taps(buf_ref, xs_ref, row, frames, True, True, low_ref)
    hid_ref[0] = jnp.dot(xs_ref[...], w_ref[...], preferred_element_type=F32)

    acc_ref[...] = jnp.zeros_like(acc_ref)

    def uniform_sums(t0, s):
        v = hid_ref[0, pl.ds(PAD + t0, CHUNK), :]
        add_sums(acc_ref, s, v, v * v)

    def mixed_sums(t0):
        v = hid_ref[0, pl.ds(PAD + t0, CHUNK), :]
        add_masked_sums(acc_ref, frame_ids(t0, CHUNK, width), row, v, v * v)

    row.chunks(uniform_sums, mixed_sums)
    put_sums(acc_ref, st2_ref, msg_ref, row, r)


def branch_grad_kernel(len_ref, og_ref, rx_ref, w_ref, gs_ref, q_ref, bias_ref, buf_ref, xs_ref):
    r = pl.program_id(0)
    frames, width = og_ref.shape[1:]
    row = Row(len_ref, r, frames)

    @pl.when(r == 0)
    def _():
        bias_ref[...] = jnp.zeros_like(bias_ref)

    def put(t0, g):
        g = g.astype(BF16).astype(F32)
        buf_ref[pl.ds(PAD + t0, CHUNK), :] = g
        bias_ref[...] += fold(g)

    def uniform(t0, s):
        put(t0, og_ref[0, pl.ds(t0, CHUNK), :].astype(F32) * ROOT_HALF)

    def mixed(t0):
        t = frame_ids(t0, CHUNK, width)
        g = og_ref[0, pl.ds(t0, CHUNK), :].astype(F32) * ROOT_HALF
        put(t0, jnp.where(t < row.ends[2], g, 0.0))

    row.chunks(uniform, mixed)
    for left in (True, False):
        t, valid = halo_tile(row, frames, width, left)
        at = 0 if left else PAD + frames
        g = edge_tile(rx_ref, row, r, t, 2, left) * ROOT_HALF
        buf_ref[at : at + PAD, :] = jnp.where(valid, g, 0.0)
    stack_taps(buf_ref, xs_ref, row, frames, False, True)
    gs_ref[0] = xs_ref[PAD : PAD + frames, :]
    q_ref[0] = times_transposed(xs_ref[...], w_ref, width).astype(BF16)


def second_norm_kernel(len_ref, hid_ref, q_ref, st_ref, rx_ref, aff_ref, low_ref, da_ref, gst_ref, msg_ref,
                       tab_ref, acc_ref):
    r = pl.program_id(0)
    padded, width = hid_ref.shape[1:]
    frames = padded - 2 * PAD
    row = Row(len_ref, r, frames)
    put_forward(row, r, st_ref, rx_ref, aff_ref, tab_ref)
    acc_ref[...] = jnp.zeros_like(acc_ref)

    def uniform(t0, s):
        rows = pl.ds(PAD + t0, CHUNK)
        v = hid_ref[0, rows, :]
        low, slope = silu_and_slope(v * row_of(tab_ref, 0, s) + row_of(tab_ref, SEGS, s))
        da = slope * q_ref[0, rows, :].astype(F32)
        low_ref[0, rows, :] = low.astype(BF16)
        da_ref[0, rows, :] = da.astype(BF16)
        add_sums(acc_ref, s, da, da * v)

    def mixed(t0):
        rows = pl.ds(PAD + t0, CHUNK)
        t = frame_ids(t0, CHUNK, width)
        live = t < row.ends[2]
        v = hid_ref[0, rows, :]
        low, slope = silu_and_slope(v * pick(tab_ref, 0, t, row) + pick(tab_ref, SEGS, t, row))
        da = slope * q_ref[0, rows, :].astype(F32)
        low_ref[0, rows, :] = jnp.where(live, low, 0.0).astype(BF16)
        da_ref[0, rows, :] = jnp.where(live, da, 0.0).astype(BF16)
        add_masked_sums(acc_ref, t, row, da, da * v)

    row.chunks(uniform, mixed)
    for left in (True, False):
        t, valid = halo_tile(row, frames, width, left)
        at = 0 if left else PAD + frames
        v = hid_ref[0, at : at + PAD, :]
        low, slope = silu_and_slope(v * tab_ref[6:7, :] + tab_ref[7:8, :])
        da = slope * q_ref[0, at : at + PAD, :].astype(F32)
        low_ref[0, at : at + PAD, :] = jnp.where(valid, low, 0.0).astype(BF16)
        da_ref[0, at : at + PAD, :] = jnp.where(valid, da, 0.0).astype(BF16)
    put_sums(acc_ref, gst_ref, msg_ref, row, r)


def block_out_kernel(len_ref, low_ref, tok_ref, w_ref, bias_ref, out_ref, buf_ref, xs_ref):
    r = pl.program_id(0)
    frames, width = tok_ref.shape[1:]
    row = Row(len_ref, r, frames)
    buf_ref[...] = low_ref[0].astype(F32)
    stack_taps(buf_ref, xs_ref, row, frames, True, False)
    branch = jnp.dot(xs_ref[...], w_ref[...], preferred_element_type=F32) + bias_ref[...].astype(F32)
    live = frame_ids(0, frames, width) < row.ends[2]
    out = (tok_ref[0].astype(F32) + jnp.where(live, branch, 0.0)) * ROOT_HALF
    out_ref[0] = out.astype(BF16)


def add_kernel_grad(r, u, gs, acc_ref, send_ref, keep_ref):
    width = u.shape[1]
    part = lax.dot_general(u, gs, (((0,), (0,)), ((), ())), preferred_element_type=F32)

    @pl.when(r == 0)
    def _():
        acc_ref[...] = part

    @pl.when(r > 0)
    def _():
        acc_ref[...] += part

    @pl.when(r == pl.num_programs(0) - 1)
    def _():
        core, half = lax.axis_index("core"), width // 2
        for ref, which in ((send_ref, 1 - core), (keep_ref, core)):
            rows = pl.ds(pl.multiple_of(which * half, half), half)
            for k in range(3):
                ref[k * half : (k + 1) * half, :] = acc_ref[rows, k * width : (k + 1) * width].astype(BF16)


def second_kernel_grad_kernel(low_ref, gs_ref, send_ref, keep_ref, acc_ref):
    frames = gs_ref.shape[1]
    add_kernel_grad(pl.program_id(0), low_ref[0, PAD : PAD + frames, :], gs_ref[0], acc_ref, send_ref, keep_ref)


def hidden_grad_kernel(len_ref, low_ref, da_ref, hid_ref, st_ref, rx_ref, gst_ref, grx_ref, aff_ref,
                       gs_ref, send_ref, keep_ref, part_ref, buf_ref, tab_ref, acc_ref):
    r = pl.program_id(0)
    frames, width = low_ref.shape[1:]
    row = Row(len_ref, r, frames)

    @pl.when(r == 0)
    def _():
        part_ref[...] = jnp.zeros_like(part_ref)

    put_affine_grads(row, r, st_ref, rx_ref, gst_ref, aff_ref, part_ref, 0)
    put_backward(row, r, st_ref, rx_ref, gst_ref, grx_ref, aff_ref, tab_ref)

    def uniform(t0, s):
        rows = pl.ds(PAD + t0, CHUNK)
        buf_ref[rows, :] = (
            da_ref[0, rows, :].astype(F32) * row_of(tab_ref, 0, s)
            + hid_ref[0, rows, :] * row_of(tab_ref, SEGS, s)
            + row_of(tab_ref, 2 * SEGS, s)
        )

    def mixed(t0):
        rows = pl.ds(PAD + t0, CHUNK)
        t = frame_ids(t0, CHUNK, width)
        grad = (
            da_ref[0, rows, :].astype(F32) * pick(tab_ref, 0, t, row)
            + hid_ref[0, rows, :] * pick(tab_ref, SEGS, t, row)
            + pick(tab_ref, 2 * SEGS, t, row)
        )
        buf_ref[rows, :] = jnp.where(t < row.ends[2], grad, 0.0)

    row.chunks(uniform, mixed)
    for left in (True, False):
        t, valid = halo_tile(row, frames, width, left)
        at = 0 if left else PAD + frames
        grad = (
            da_ref[0, at : at + PAD, :].astype(F32) * tab_ref[9:10, :]
            + hid_ref[0, at : at + PAD, :] * tab_ref[10:11, :]
            + tab_ref[11:12, :]
        )
        buf_ref[at : at + PAD, :] = jnp.where(valid, grad, 0.0)
    stack_taps(buf_ref, gs_ref.at[0], row, frames, False, False)
    add_kernel_grad(r, low_ref[0], gs_ref[0], acc_ref, send_ref, keep_ref)


def first_norm_grad_kernel(len_ref, gs_ref, w_ref, tok_ref, st_ref, rx_ref, aff_ref, part2_ref, bias_ref,
                           da_ref, gst_ref, msg_ref, part_ref, q_ref, tab_ref, acc_ref, sums_ref):
    r = pl.program_id(0)
    frames, width = tok_ref.shape[1:]
    row = Row(len_ref, r, frames)

    @pl.when(r == 0)
    def _():
        sums_ref[:, : 2 * width] = jnp.zeros((sums_ref.shape[0], 2 * width), F32)
        sums_ref[:, 2 * width :] = part2_ref[...]
        sums_ref[SEGS : SEGS + 1, :width] = jnp.sum(bias_ref[...], axis=0, keepdims=True)

    put_forward(row, r, st_ref, rx_ref, aff_ref, tab_ref)
    q_ref[...] = times_transposed(gs_ref[0], w_ref, width)
    acc_ref[...] = jnp.zeros_like(acc_ref)

    def uniform(t0, s):
        rows = pl.ds(t0, CHUNK)
        v = tok_ref[0, rows, :].astype(F32)
        _, slope = silu_and_slope(v * row_of(tab_ref, 0, s) + row_of(tab_ref, SEGS, s))
        da = slope * q_ref[rows, :]
        da_ref[0, rows, :] = da.astype(BF16)
        add_sums(acc_ref, s, da, da * v)

    def mixed(t0):
        rows = pl.ds(t0, CHUNK)
        t = frame_ids(t0, CHUNK, width)
        v = tok_ref[0, rows, :].astype(F32)
        _, slope = silu_and_slope(v * pick(tab_ref, 0, t, row) + pick(tab_ref, SEGS, t, row))
        da = slope * q_ref[rows, :]
        da_ref[0, rows, :] = jnp.where(t < row.ends[2], da, 0.0).astype(BF16)
        add_masked_sums(acc_ref, t, row, da, da * v)

    row.chunks(uniform, mixed)
    put_sums(acc_ref, gst_ref, msg_ref, row, r)
    put_affine_grads(row, r, st_ref, rx_ref, gst_ref, aff_ref, sums_ref, 0)

    @pl.when(r == pl.num_programs(0) - 1)
    def _():
        for d in range(part_ref.shape[0]):
            part_ref[d] = sums_ref[...].astype(BF16)


def input_grad_kernel(len_ref, og_ref, da_ref, tok_ref, st_ref, rx_ref, gst_ref, grx_ref, aff_ref, out_ref, tab_ref):
    r = pl.program_id(0)
    frames, width = tok_ref.shape[1:]
    row = Row(len_ref, r, frames)
    put_backward(row, r, st_ref, rx_ref, gst_ref, grx_ref, aff_ref, tab_ref)

    def uniform(t0, s):
        rows = pl.ds(t0, CHUNK)
        out = (
            og_ref[0, rows, :].astype(F32) * ROOT_HALF
            + da_ref[0, rows, :].astype(F32) * row_of(tab_ref, 0, s)
            + tok_ref[0, rows, :].astype(F32) * row_of(tab_ref, SEGS, s)
            + row_of(tab_ref, 2 * SEGS, s)
        )
        out_ref[0, rows, :] = out.astype(BF16)

    def mixed(t0):
        rows = pl.ds(t0, CHUNK)
        t = frame_ids(t0, CHUNK, width)
        grad = (
            da_ref[0, rows, :].astype(F32) * pick(tab_ref, 0, t, row)
            + tok_ref[0, rows, :].astype(F32) * pick(tab_ref, SEGS, t, row)
            + pick(tab_ref, 2 * SEGS, t, row)
        )
        out = og_ref[0, rows, :].astype(F32) * ROOT_HALF + jnp.where(t < row.ends[2], grad, 0.0)
        out_ref[0, rows, :] = out.astype(BF16)

    row.chunks(uniform, mixed)


def per_row(*shape):
    return pl.BlockSpec((1, *shape), lambda r, *_: (r,) + (0,) * len(shape))


def sums_block(width):
    return pl.BlockSpec((8, width), lambda r, *_: (r, 0))


def whole(*shape):
    return pl.BlockSpec(shape, lambda r, *_: (0,) * len(shape))


def call(kernel, rows, lengths, arrays, in_specs, outs, out_specs, scratch, flops=0, nbytes=8 << 20):
    prefetch = () if lengths is None else (lengths,)
    return pl.pallas_call(
        kernel,
        out_shape=[jax.ShapeDtypeStruct(s, d) for s, d in outs],
        grid_spec=pltpu.PrefetchScalarGridSpec(
            num_scalar_prefetch=len(prefetch),
            grid=(rows,),
            in_specs=in_specs,
            out_specs=out_specs,
            scratch_shapes=[pltpu.VMEM(s, d) for s, d in scratch],
        ),
        compiler_params=pltpu.CompilerParams(
            dimension_semantics=("arbitrary",), vmem_limit_bytes=VMEM_MIB << 20
        ),
        cost_estimate=pl.CostEstimate(flops=flops, bytes_accessed=nbytes, transcendentals=0),
    )(*prefetch, *arrays)


def exchange(message):
    return lax.all_to_all(message, "tm", 0, 0)


def spread(block, axis):
    count = lax.axis_size(axis)
    return lax.all_to_all(jnp.broadcast_to(block[None], (count, *block.shape)), axis, 0, 0)


def scatter_sum(blocks, axis):
    count = lax.axis_size(axis)
    got = lax.all_to_all(blocks.reshape(count, -1, blocks.shape[1]), axis, 0, 0)
    return jnp.sum(got.astype(F32), axis=0).astype(BF16)


def swap_cores(block):
    return lax.ppermute(block, "core", [(0, 1), (1, 0)])


def total(send, keep):
    width = send.shape[1]
    mine = (swap_cores(send).astype(F32) + keep.astype(F32)).astype(BF16)
    part = scatter_sum(scatter_sum(mine, "chip"), "tm")
    mine = spread(spread(part, "tm").reshape(-1, width), "chip").reshape(-1, width)
    other = swap_cores(mine)
    first = lax.axis_index("core") == 0
    low = jnp.where(first, mine, other).reshape(3, -1, width)
    high = jnp.where(first, other, mine).reshape(3, -1, width)
    return jnp.concatenate([low, high], axis=1).astype(F32)


def per_device(tokens, lengths, style, fc1_weight, fc1_bias, conv1_kernel, fc2_weight, fc2_bias, conv2_kernel,
               conv2_bias, out_grad):
    rows, frames, width = tokens.shape
    count = lax.axis_size("tm")
    padded = frames + 2 * PAD
    style_rows = style.reshape(rows * SEGS, -1)
    affine1 = jnp.dot(style_rows, fc1_weight, preferred_element_type=F32) + fc1_bias.astype(F32)
    affine2 = jnp.dot(style_rows, fc2_weight, preferred_element_type=F32) + fc2_bias.astype(F32)
    kernel1 = conv1_kernel.reshape(3 * width, width)
    kernel2 = conv2_kernel.reshape(3 * width, width)

    own, wide = per_row(frames, width), per_row(padded, width)
    taps = per_row(frames, 3 * width)
    head = pl.BlockSpec((1, PAD, width), lambda r, *_: (r, 0, 0))
    tail = pl.BlockSpec((1, PAD, width), lambda r, *_: (r, frames // PAD - 1, 0))
    sums, affine, kernel = sums_block(width), whole(rows * SEGS, 2 * width), whole(3 * width, width)
    msg, msg_edges = whole(count, 2 * rows, width), whole(count, EDGE, width)
    halves = whole(3 * width // 2, width)
    sums_shape = ((8 * rows, width), F32)
    msg_shape = ((count, 2 * rows, width), F32)
    half_shape = ((3 * width // 2, width), BF16)
    acc, tab = ((8, 8, width), F32), ((16, width), F32)
    buf, xs_wide, xs_own = ((padded, width), F32), ((padded, 3 * width), BF16), ((frames, 3 * width), BF16)
    flops = 2 * rows * frames * 3 * width * width

    st1, msg1 = call(
        token_sums_kernel, rows, lengths, (tokens, tokens, tokens, out_grad, out_grad),
        [own, head, tail, head, tail], [sums_shape, ((count, EDGE, width), F32)], [sums, msg_edges], [acc],
    )
    rx1 = exchange(msg1)
    low1, hidden, st2, msg2 = call(
        first_half_kernel, rows, lengths, (tokens, st1, rx1, affine1, kernel1),
        [own, sums, msg_edges, affine, kernel],
        [((rows, frames, width), BF16), ((rows, padded, width), F32), sums_shape, msg_shape],
        [own, wide, sums, msg], [buf, xs_wide, tab, acc], flops,
    )
    rx2 = exchange(msg2)
    gs2, grad_low2, bias_part = call(
        branch_grad_kernel, rows, lengths, (out_grad, rx1, kernel2), [own, msg_edges, kernel],
        [((rows, frames, 3 * width), BF16), ((rows, padded, width), BF16), ((8, width), F32)],
        [taps, wide, whole(8, width)], [buf, xs_wide], flops,
    )
    low2, da2, gst2, msg3 = call(
        second_norm_kernel, rows, lengths, (hidden, grad_low2, st2, rx2, affine2), [wide, wide, sums, msg, affine],
        [((rows, padded, width), BF16), ((rows, padded, width), BF16), sums_shape, msg_shape],
        [wide, wide, sums, msg], [tab, acc],
    )
    rx3 = exchange(msg3)
    send2, keep2 = call(
        second_kernel_grad_kernel, rows, None, (low2, gs2), [wide, taps], [half_shape, half_shape], [halves, halves],
        [((width, 3 * width), F32)], flops,
    )
    gs1, send1, keep1, part2 = call(
        hidden_grad_kernel, rows, lengths, (low1, da2, hidden, st2, rx2, gst2, rx3, affine2),
        [own, wide, wide, sums, msg, sums, msg, affine],
        [((rows, frames, 3 * width), BF16), half_shape, half_shape, ((4 * rows, 2 * width), F32)],
        [taps, halves, halves, whole(4 * rows, 2 * width)], [buf, tab, ((width, 3 * width), F32)], flops,
    )
    da1, gst1, msg4, parts = call(
        first_norm_grad_kernel, rows, lengths, (gs1, kernel1, tokens, st1, rx1, affine1, part2, bias_part),
        [taps, kernel, own, sums, msg_edges, affine, whole(4 * rows, 2 * width), whole(8, width)],
        [((rows, frames, width), BF16), sums_shape, msg_shape, ((count, 4 * rows, 4 * width), BF16)],
        [own, sums, msg, whole(count, 4 * rows, 4 * width)],
        [((frames, width), F32), tab, acc, ((4 * rows, 4 * width), F32)], flops,
    )
    rx4 = exchange(msg4)
    (block_out,) = call(
        block_out_kernel, rows, lengths, (low2, tokens, kernel2, conv2_bias.reshape(1, width)),
        [wide, own, kernel, whole(1, width)], [((rows, frames, width), BF16)], [own], [buf, xs_own], flops,
    )
    (input_grad,) = call(
        input_grad_kernel, rows, lengths, (out_grad, da1, tokens, st1, rx1, gst1, rx4, affine1),
        [own, own, own, sums, msg_edges, sums, msg, affine], [((rows, frames, width), BF16)], [own], [tab],
    )

    conv2_sum, conv1_sum = total(send2, keep2), total(send1, keep1)

    affine_grads = jnp.sum(exchange(parts).astype(F32), axis=0).astype(BF16)
    mine = affine_grads.reshape(rows, 4, 4 * width)[:, :SEGS].reshape(rows * SEGS, 4 * width)
    style_grad = lax.dot_general(
        mine[:, : 2 * width], fc1_weight, (((1,), (1,)), ((), ())), preferred_element_type=F32
    ) + lax.dot_general(mine[:, 2 * width :], fc2_weight, (((1,), (1,)), ((), ())), preferred_element_type=F32)
    style_pad = jnp.pad(style, ((0, 0), (0, 1), (0, 0))).reshape(rows * 4, -1)
    gathered = spread(jnp.concatenate([affine_grads, style_pad], axis=1), ("chip", "core"))
    gathered = gathered.reshape(-1, gathered.shape[-1])
    grads, styles = gathered[:, : 4 * width], gathered[:, 4 * width :]
    fc_grads = lax.dot_general(styles, grads, (((0,), (0,)), ((), ())), preferred_element_type=F32)
    by_segment = jnp.sum(grads.reshape(-1, 4, 4 * width).astype(F32), axis=0)
    fc_bias_grads = jnp.sum(by_segment[:SEGS], axis=0)
    return (
        block_out,
        input_grad,
        style_grad.reshape(style.shape),
        fc_grads[:, : 2 * width],
        fc_bias_grads[: 2 * width],
        conv1_sum,
        fc_grads[:, 2 * width :],
        fc_bias_grads[2 * width :],
        conv2_sum,
        by_segment[SEGS, :width],
    )


def solution(mesh):
    chips = mesh.shape["dp"] // 2
    mesh = Mesh(mesh.devices.reshape(chips, 2, mesh.shape["tm"]), ("chip", "core", "tm"))
    dp = ("chip", "core")
    return jax.shard_map(
        per_device,
        mesh=mesh,
        in_specs=(
            P(dp, "tm", None),
            P(dp, None),
            P(dp, None, None),
            P(),
            P(),
            P(),
            P(),
            P(),
            P(),
            P(),
            P(dp, "tm", None),
        ),
        out_specs=(
            P(dp, "tm", None),
            P(dp, "tm", None),
            P(dp, None, None),
            P(),
            P(),
            P(),
            P(),
            P(),
            P(),
            P(),
        ),
        check_vma=False,
    )
```

profile of v0, /device:TPU:0, one launch (start us, length us, event | category | flops | bytes accessed | tf_op | source)
XLA Modules:
  0.0 252.0 jit_solution(11842319739050441871)
XLA Ops:
  4.6 2.7 %shard_map.186 = (f32[32,512]{1,0:T(8,128)S(1)}, f32[4,24,512]{2,1,0:T(8,128)}) custom-call(s32[4,3]{1,0:T(4,128)S(1)} %copy-done.21, bf16[4,512,512]{2,1,0:T(8,128)(2,1)S(1)} %copy-done.1, bf16[4,512,512]{2,1,0:T(8,128)(2,1)S(1)} %copy-done.1, bf16[4,512,512]{2,1,0:T(8,128)(2,1)S(1)} %copy-done.1, bf16[4,512,512]{2,1,0:T(8,128)(2,1)S(1)} %copy-done.3, ...), custom_call_target="tpu_custom_call" | custom-call | bytes 8388608 | tf_op jit(solution)/shard_map/pallas_call | solution.py:544
  7.3 6.7 %all-to-all-start = ((f32[4,24,512]{2,1,0:T(8,128)}), f32[4,24,512]{2,1,0:T(8,128)S(1)}, u32[]{:S(2)}, u32[]{:S(2)}) async-start(f32[4,24,512]{2,1,0:T(8,128)} %get-tuple-element.34), calls=%async_computation | async-start | bytes 393216 | tf_op jit(solution)/shard_map/all_to_all | solution.py:562
  14.4 7.3 %all-to-all-done.rx_ref = f32[4,24,512]{2,1,0:T(8,128)S(1)} async-done(((f32[4,24,512]{2,1,0:T(8,128)}), f32[4,24,512]{2,1,0:T(8,128)S(1)}, u32[]{:S(2)}, u32[]{:S(2)}) %all-to-all-start) | async-done | bytes 196640 | tf_op jit(solution)/shard_map/all_to_all | solution.py:562
  23.1 10.0 %shard_map.187 = (bf16[4,512,512]{2,1,0:T(8,128)(2,1)S(1)}, f32[4,544,512]{2,1,0:T(8,128)S(1)}, f32[32,512]{1,0:T(8,128)S(1)}, f32[4,8,512]{2,1,0:T(8,128)}) custom-call(s32[4,3]{1,0:T(4,128)S(1)} %copy-done.22, bf16[4,512,512]{2,1,0:T(8,128)(2,1)S(1)} %copy-done.2, f32[32,512]{1,0:T(8,128)S(1)} %get-tuple-element.33.st_ref, ...), custom_call_target="tpu_custom_call" | custom-call | flops 3221225472 | bytes 8388608 | tf_op jit(solution)/shard_map/pallas_call | solution.py:544
  36.6 3.3 %all-to-all-start.1 = ((f32[4,8,512]{2,1,0:T(8,128)}), f32[4,8,512]{2,1,0:T(8,128)S(1)}, u32[]{:S(2)}, u32[]{:S(2)}) async-start(f32[4,8,512]{2,1,0:T(8,128)} %get-tuple-element.38), calls=%async_computation.1 | async-start | bytes 131072 | tf_op jit(solution)/shard_map/all_to_all | solution.py:562
  42.9 8.1 %shard_map.188 = (bf16[4,512,1536]{2,1,0:T(8,128)(2,1)S(1)}, bf16[4,544,512]{2,1,0:T(8,128)(2,1)S(1)}, f32[8,512]{1,0:T(8,128)S(1)}) custom-call(s32[4,3]{1,0:T(4,128)S(1)} %copy-done.22, bf16[4,512,512]{2,1,0:T(8,128)(2,1)S(1)} %copy-done.4, f32[4,24,512]{2,1,0:T(8,128)S(1)} %all-to-all-done.rx_ref, bf16[1536,512]{1,0:T(8,128)(2,1)S(1)} %bitcast.30), custom_call_target="tpu_custom_call" | custom-call | flops 3221225472 | bytes 8388608 | tf_op jit(solution)/shard_map/pallas_call | solution.py:544
  59.5 4.1 %shard_map.189 = (bf16[4,544,512]{2,1,0:T(8,128)(2,1)S(1)}, bf16[4,544,512]{2,1,0:T(8,128)(2,1)S(1)}, f32[32,512]{1,0:T(8,128)S(1)}, f32[4,8,512]{2,1,0:T(8,128)S(1)}) custom-call(s32[4,3]{1,0:T(4,128)S(1)} %copy-done.22, f32[4,544,512]{2,1,0:T(8,128)S(1)} %copy-done.7, bf16[4,544,512]{2,1,0:T(8,128)(2,1)S(1)} %copy-done.10, ...), custom_call_target="tpu_custom_call" | custom-call | bytes 8388608 | tf_op jit(solution)/shard_map/pallas_call | solution.py:544
  65.0 11.1 %all_to_all.70.grx_ref = f32[4,8,512]{2,1,0:T(8,128)S(1)} all-to-all(f32[4,8,512]{2,1,0:T(8,128)S(1)} %get-tuple-element.43), channel_id=1, replica_groups=mesh['chip'=4,'core'=2,'tm'=4] {'tm'}, dimensions={0} | all-to-all | bytes 131072 | tf_op jit(solution)/shard_map/all_to_all | solution.py:562
  76.9 8.9 %shard_map.191 = (bf16[4,512,1536]{2,1,0:T(8,128)(2,1)S(1)}, bf16[768,512]{1,0:T(8,128)(2,1)S(1)}, bf16[768,512]{1,0:T(8,128)(2,1)S(1)}, f32[16,1024]{1,0:T(8,128)S(1)}) custom-call(s32[4,3]{1,0:T(4,128)S(1)} %copy-done.22, bf16[4,512,512]{2,1,0:T(8,128)(2,1)S(1)} %copy-done.34, bf16[4,544,512]{2,1,0:T(8,128)(2,1)S(1)} %get-tuple-element.41.da_ref, ...), custom_call_target="tpu_custom_call" | custom-call | flops 3221225472 | bytes 8388608 | tf_op jit(solution)/shard_map/pallas_call | solution.py:544
  85.9 8.0 %shard_map.192 = (bf16[4,512,512]{2,1,0:T(8,128)(2,1)S(1)}, f32[32,512]{1,0:T(8,128)S(1)}, f32[4,8,512]{2,1,0:T(8,128)S(1)}, bf16[4,16,2048]{2,1,0:T(8,128)(2,1)S(1)}) custom-call(s32[4,3]{1,0:T(4,128)S(1)} %copy-done.22, bf16[4,512,1536]{2,1,0:T(8,128)(2,1)S(1)} %get-tuple-element.44.gs_ref, bf16[1536,512]{1,0:T(8,128)(2,1)S(1)} %bitcast.29, ...), custom_call_target="tpu_custom_call" | custom-call | flops 3221225472 | bytes 8388608 | tf_op jit(solution)/shard_map/pallas_call | solution.py:544
  96.6 4.0 %all-to-all-start.4 = ((bf16[4,16,2048]{2,1,0:T(8,128)(2,1)}), bf16[4,16,2048]{2,1,0:T(8,128)(2,1)}, u32[]{:S(2)}, u32[]{:S(2)}) async-start(bf16[4,16,2048]{2,1,0:T(8,128)(2,1)} %copy-done.14), calls=%async_computation.4 | async-start | bytes 524288 | tf_op jit(solution)/shard_map/all_to_all | solution.py:562
  102.2 2.8 %copy-done.32 = bf16[4,512,1536]{2,1,0:T(8,128)(2,1)S(1)} copy-done((bf16[4,512,1536]{2,1,0:T(8,128)(2,1)S(1)}, bf16[4,512,1536]{2,1,0:T(8,128)(2,1)}, u32[]{:S(2)}) %copy-start.32) | copy-done | bytes 6291480
  105.0 6.2 %shard_map.194 = (bf16[768,512]{1,0:T(8,128)(2,1)}, bf16[768,512]{1,0:T(8,128)(2,1)S(1)}) custom-call(bf16[4,544,512]{2,1,0:T(8,128)(2,1)S(1)} %copy-done.24, bf16[4,512,1536]{2,1,0:T(8,128)(2,1)S(1)} %copy-done.32), custom_call_target="tpu_custom_call" | custom-call | flops 3221225472 | bytes 8388608 | tf_op jit(solution)/shard_map/pallas_call | solution.py:544
  112.1 5.1 %all-to-all-start.3 = ((f32[4,8,512]{2,1,0:T(8,128)}), f32[4,8,512]{2,1,0:T(8,128)S(1)}, u32[]{:S(2)}, u32[]{:S(2)}) async-start(f32[4,8,512]{2,1,0:T(8,128)} %copy-done.20), calls=%async_computation.3 | async-start | bytes 131072 | tf_op jit(solution)/shard_map/all_to_all | solution.py:562
  124.6 4.2 %all-to-all-start.5 = ((bf16[8,16,2176]{2,1,0:T(8,128)(2,1)}), bf16[8,16,2176]{2,1,0:T(8,128)(2,1)}, u32[]{:S(2)}, u32[]{:S(2)}) async-start(bf16[8,16,2176]{2,1,0:T(8,128)(2,1)} %broadcast_in_dim.14), calls=%async_computation.5 | async-start | bytes 1114112 | tf_op jit(solution)/shard_map/all_to_all | solution.py:567
  131.7 7.3 %all-to-all-done.5 = bf16[8,16,2176]{2,1,0:T(8,128)(2,1)} async-done(((bf16[8,16,2176]{2,1,0:T(8,128)(2,1)}), bf16[8,16,2176]{2,1,0:T(8,128)(2,1)}, u32[]{:S(2)}, u32[]{:S(2)}) %all-to-all-start.5) | async-done | bytes 557088 | tf_op jit(solution)/shard_map/all_to_all | solution.py:567
  138.9 4.2 %all-to-all-start.10 = ((bf16[4,192,512]{2,1,0:T(8,128)(2,1)}), bf16[4,192,512]{2,1,0:T(8,128)(2,1)}, u32[]{:S(2)}, u32[]{:S(2)}) async-start(bf16[4,192,512]{2,1,0:T(8,128)(2,1)} %bitcast.37), calls=%async_computation.10 | async-start | bytes 1572864 | tf_op jit(solution)/shard_map/all_to_all | solution.py:572
  145.4 7.9 %all-to-all-done.10 = bf16[4,192,512]{2,1,0:T(8,128)(2,1)} async-done(((bf16[4,192,512]{2,1,0:T(8,128)(2,1)}), bf16[4,192,512]{2,1,0:T(8,128)(2,1)}, u32[]{:S(2)}, u32[]{:S(2)}) %all-to-all-start.10) | async-done | bytes 786464 | tf_op jit(solution)/shard_map/all_to_all | solution.py:572
  153.3 3.5 %all-to-all-start.6 = ((bf16[4,192,512]{2,1,0:T(8,128)(2,1)}), bf16[4,192,512]{2,1,0:T(8,128)(2,1)S(1)}, u32[]{:S(2)}, u32[]{:S(2)}) async-start(bf16[4,192,512]{2,1,0:T(8,128)(2,1)} %bitcast.38), calls=%async_computation.6 | async-start | bytes 1572864 | tf_op jit(solution)/shard_map/all_to_all | solution.py:572
  158.8 7.6 %all-to-all-done.6 = bf16[4,192,512]{2,1,0:T(8,128)(2,1)S(1)} async-done(((bf16[4,192,512]{2,1,0:T(8,128)(2,1)}), bf16[4,192,512]{2,1,0:T(8,128)(2,1)S(1)}, u32[]{:S(2)}, u32[]{:S(2)}) %all-to-all-start.6) | async-done | bytes 786464 | tf_op jit(solution)/shard_map/all_to_all | solution.py:572
  166.4 4.0 %all-to-all-start.11 = ((bf16[4,48,512]{2,1,0:T(8,128)(2,1)}), bf16[4,48,512]{2,1,0:T(8,128)(2,1)}, u32[]{:S(2)}, u32[]{:S(2)}) async-start(bf16[4,48,512]{2,1,0:T(8,128)(2,1)} %bitcast.39), calls=%async_computation.11 | async-start | bytes 393216 | tf_op jit(solution)/shard_map/all_to_all | solution.py:572
  171.3 6.5 %all-to-all-done.11 = bf16[4,48,512]{2,1,0:T(8,128)(2,1)} async-done(((bf16[4,48,512]{2,1,0:T(8,128)(2,1)}), bf16[4,48,512]{2,1,0:T(8,128)(2,1)}, u32[]{:S(2)}, u32[]{:S(2)}) %all-to-all-start.11) | async-done | bytes 196640 | tf_op jit(solution)/shard_map/all_to_all | solution.py:572
  177.8 3.4 %all-to-all-start.7 = ((bf16[4,48,512]{2,1,0:T(8,128)(2,1)}), bf16[4,48,512]{2,1,0:T(8,128)(2,1)S(1)}, u32[]{:S(2)}, u32[]{:S(2)}) async-start(bf16[4,48,512]{2,1,0:T(8,128)(2,1)} %bitcast.40), calls=%async_computation.7 | async-start | bytes 393216 | tf_op jit(solution)/shard_map/all_to_all | solution.py:572
  182.1 5.2 %all-to-all-done.7 = bf16[4,48,512]{2,1,0:T(8,128)(2,1)S(1)} async-done(((bf16[4,48,512]{2,1,0:T(8,128)(2,1)}), bf16[4,48,512]{2,1,0:T(8,128)(2,1)S(1)}, u32[]{:S(2)}, u32[]{:S(2)}) %all-to-all-start.7) | async-done | bytes 196640 | tf_op jit(solution)/shard_map/all_to_all | solution.py:572
  188.1 3.4 %all-to-all-start.12 = ((bf16[4,48,512]{2,1,0:T(8,128)(2,1)}), bf16[4,48,512]{2,1,0:T(8,128)(2,1)S(1)}, u32[]{:S(2)}, u32[]{:S(2)}) async-start(bf16[4,48,512]{2,1,0:T(8,128)(2,1)} %broadcast_in_dim.18), calls=%async_computation.12 | async-start | bytes 393216 | tf_op jit(solution)/shard_map/all_to_all | solution.py:567
  191.5 6.2 %all-to-all-done.12 = bf16[4,48,512]{2,1,0:T(8,128)(2,1)S(1)} async-done(((bf16[4,48,512]{2,1,0:T(8,128)(2,1)}), bf16[4,48,512]{2,1,0:T(8,128)(2,1)S(1)}, u32[]{:S(2)}, u32[]{:S(2)}) %all-to-all-start.12) | async-done | bytes 196640 | tf_op jit(solution)/shard_map/all_to_all | solution.py:567
  197.7 9.9 %all_to_all.71 = bf16[4,48,512]{2,1,0:T(8,128)(2,1)} all-to-all(bf16[4,48,512]{2,1,0:T(8,128)(2,1)S(1)} %broadcast_in_dim.15), channel_id=1, replica_groups=mesh['chip'=4,'core'=2,'tm'=4] {'tm'}, dimensions={0} | all-to-all | bytes 393216 | tf_op jit(solution)/shard_map/all_to_all | solution.py:567
  208.6 3.7 %all-to-all-start.13 = ((bf16[4,192,512]{2,1,0:T(8,128)(2,1)}), bf16[4,192,512]{2,1,0:T(8,128)(2,1)S(1)}, u32[]{:S(2)}, u32[]{:S(2)}) async-start(bf16[4,192,512]{2,1,0:T(8,128)(2,1)} %broadcast_in_dim.40), calls=%async_computation.13 | async-start | bytes 1572864 | tf_op jit(solution)/shard_map/all_to_all | solution.py:567
  215.3 7.1 %shard_map.190 = bf16[4,512,512]{2,1,0:T(8,128)(2,1)} custom-call(s32[4,3]{1,0:T(4,128)S(1)} %copy-done.22, bf16[4,544,512]{2,1,0:T(8,128)(2,1)S(1)} %copy-done.25, bf16[4,512,512]{2,1,0:T(8,128)(2,1)S(1)} %copy-done.2, bf16[1536,512]{1,0:T(8,128)(2,1)S(1)} %bitcast.31, bf16[1,512]{1,0:T(2,128)(2,1)S(1)} %reshape.90.bias_ref), custom_call_target="tpu_custom_call" | custom-call | flops 3221225472 | bytes 8388608 | tf_op jit(solution)/shard_map/pallas_call | solution.py:544
  222.5 3.9 %shard_map.193 = bf16[4,512,512]{2,1,0:T(8,128)(2,1)} custom-call(s32[4,3]{1,0:T(4,128)S(1)} %copy-done.22, bf16[4,512,512]{2,1,0:T(8,128)(2,1)S(1)} %copy-done.5, bf16[4,512,512]{2,1,0:T(8,128)(2,1)S(1)} %copy-done.12, bf16[4,512,512]{2,1,0:T(8,128)(2,1)S(1)} %copy-done.2, f32[32,512]{1,0:T(8,128)S(1)} %copy-done.17, ...), custom_call_target="tpu_custom_call" | custom-call | bytes 8388608 | tf_op jit(solution)/shard_map/pallas_call | solution.py:544
  229.4 4.2 %all-to-all-start.9 = ((bf16[4,192,512]{2,1,0:T(8,128)(2,1)}), bf16[4,192,512]{2,1,0:T(8,128)(2,1)}, u32[]{:S(2)}, u32[]{:S(2)}) async-start(bf16[4,192,512]{2,1,0:T(8,128)(2,1)} %broadcast_in_dim.17), calls=%async_computation.9 | async-start | bytes 1572864 | tf_op jit(solution)/shard_map/all_to_all | solution.py:567
  236.1 5.6 %all-to-all-done.9 = bf16[4,192,512]{2,1,0:T(8,128)(2,1)} async-done(((bf16[4,192,512]{2,1,0:T(8,128)(2,1)}), bf16[4,192,512]{2,1,0:T(8,128)(2,1)}, u32[]{:S(2)}, u32[]{:S(2)}) %all-to-all-start.9) | async-done | bytes 786464 | tf_op jit(solution)/shard_map/all_to_all | solution.py:567
  (137 shorter events, 64.9 us)
Async XLA Ops:
  0.6 13.4 %copy-start = (bf16[128,1024]{1,0:T(8,128)(2,1)S(1)}, bf16[128,1024]{1,0:T(8,128)(2,1)}, u32[]{:S(2)}) copy-start(bf16[128,1024]{1,0:T(8,128)(2,1)} %param.14) | copy-start | bytes 786436
  4.6 9.4 %copy-start.40 = (bf16[4,3,128]{2,0,1:T(4,128)(2,1)S(1)}, bf16[4,3,128]{2,0,1:T(4,128)(2,1)}, u32[]{:S(2)}) copy-start(bf16[4,3,128]{2,0,1:T(4,128)(2,1)} %param.13) | copy-start | bytes 9220
  4.6 9.5 %copy-start.41 = (bf16[1024]{0:T(1024)(128)(2,1)S(1)}, bf16[1024]{0:T(1024)(128)(2,1)}, u32[]{:S(2)}) copy-start(bf16[1024]{0:T(1024)(128)(2,1)} %param.15) | copy-start | bytes 6148
  4.6 9.6 %copy-start.42 = (bf16[1024]{0:T(1024)(128)(2,1)S(1)}, bf16[1024]{0:T(1024)(128)(2,1)}, u32[]{:S(2)}) copy-start(bf16[1024]{0:T(1024)(128)(2,1)} %param.18) | copy-start | bytes 6148
  4.6 9.6 %copy-start.37 = (bf16[128,1024]{1,0:T(8,128)(2,1)S(1)}, bf16[128,1024]{1,0:T(8,128)(2,1)}, u32[]{:S(2)}) copy-start(bf16[128,1024]{1,0:T(8,128)(2,1)} %param.17) | copy-start | bytes 786436
  4.6 17.1 %copy-start.2 = (bf16[4,512,512]{2,1,0:T(8,128)(2,1)S(1)}, bf16[4,512,512]{2,1,0:T(8,128)(2,1)}, u32[]{:S(2)}) copy-start(bf16[4,512,512]{2,1,0:T(8,128)(2,1)} %tok_ref.9) | copy-start | bytes 6291460
  4.6 17.1 %copy-start.22 = (s32[4,3]{1,0:T(4,128)S(1)}, s32[4,3]{1,0:T(4,128)}, u32[]{:S(2)}) copy-start(s32[4,3]{1,0:T(4,128)} %len_ref.15) | copy-start | bytes 148
  7.3 25.8 %copy-start.15 = (f32[32,512]{1,0:T(8,128)}, f32[32,512]{1,0:T(8,128)S(1)}, u32[]{:S(2)}) copy-start(f32[32,512]{1,0:T(8,128)S(1)} %get-tuple-element.33.st_ref) | copy-start | bytes 196612
  7.3 14.3 %all-to-all-start = ((f32[4,24,512]{2,1,0:T(8,128)}), f32[4,24,512]{2,1,0:T(8,128)S(1)}, u32[]{:S(2)}, u32[]{:S(2)}) async-start(f32[4,24,512]{2,1,0:T(8,128)} %get-tuple-element.34), calls=%async_computation | async-start | bytes 393216 | tf_op jit(solution)/shard_map/all_to_all | solution.py:562
  36.6 19.0 %copy-start.18 = (f32[32,512]{1,0:T(8,128)}, f32[32,512]{1,0:T(8,128)S(1)}, u32[]{:S(2)}) copy-start(f32[32,512]{1,0:T(8,128)S(1)} %get-tuple-element.37.st_ref) | copy-start | bytes 196612
  36.6 19.0 %all-to-all-start.1 = ((f32[4,8,512]{2,1,0:T(8,128)}), f32[4,8,512]{2,1,0:T(8,128)S(1)}, u32[]{:S(2)}, u32[]{:S(2)}) async-start(f32[4,8,512]{2,1,0:T(8,128)} %get-tuple-element.38), calls=%async_computation.1 | async-start | bytes 131072 | tf_op jit(solution)/shard_map/all_to_all | solution.py:562
  59.5 16.6 %copy-start.8 = (f32[4,544,512]{2,1,0:T(8,128)S(1)}, f32[4,544,512]{2,1,0:T(8,128)}, u32[]{:S(2)}) copy-start(f32[4,544,512]{2,1,0:T(8,128)} %copy-done.6) | copy-start | bytes 13369348
  59.5 16.6 %copy-start.34 = (bf16[4,512,512]{2,1,0:T(8,128)(2,1)S(1)}, bf16[4,512,512]{2,1,0:T(8,128)(2,1)}, u32[]{:S(2)}) copy-start(bf16[4,512,512]{2,1,0:T(8,128)(2,1)} %copy-done.33) | copy-start | bytes 6291460
  76.9 8.9 %copy-start.16 = (f32[32,512]{1,0:T(8,128)S(1)}, f32[32,512]{1,0:T(8,128)}, u32[]{:S(2)}) copy-start(f32[32,512]{1,0:T(8,128)} %copy-done.15) | copy-start | bytes 196612
  76.9 8.9 %copy-start.27 = (bf16[3,512,512]{2,1,0:T(8,128)(2,1)S(1)}, bf16[3,512,512]{2,1,0:T(8,128)(2,1)}, u32[]{:S(2)}) copy-start(bf16[3,512,512]{2,1,0:T(8,128)(2,1)} %param.16) | copy-start | bytes 4718596
  76.9 9.0 %copy-start.36 = (f32[8,512]{1,0:T(8,128)S(1)}, f32[8,512]{1,0:T(8,128)}, u32[]{:S(2)}) copy-start(f32[8,512]{1,0:T(8,128)} %copy-done.35) | copy-start | bytes 49156
  85.8 8.1 %copy-start.30 = (bf16[768,512]{1,0:T(8,128)(2,1)}, bf16[768,512]{1,0:T(8,128)(2,1)S(1)}, u32[]{:S(2)}) copy-start(bf16[768,512]{1,0:T(8,128)(2,1)S(1)} %get-tuple-element.51) | copy-start | bytes 2359300
  96.6 15.6 %all-to-all-start.4 = ((bf16[4,16,2048]{2,1,0:T(8,128)(2,1)}), bf16[4,16,2048]{2,1,0:T(8,128)(2,1)}, u32[]{:S(2)}, u32[]{:S(2)}) async-start(bf16[4,16,2048]{2,1,0:T(8,128)(2,1)} %copy-done.14), calls=%async_computation.4 | async-start | bytes 524288 | tf_op jit(solution)/shard_map/all_to_all | solution.py:562
  112.1 17.1 %collective-permute-start.2 = (bf16[768,512]{1,0:T(8,128)(2,1)}, bf16[768,512]{1,0:T(8,128)(2,1)}, u32[]{:S(2)}, u32[]{:S(2)}) collective-permute-start(bf16[768,512]{1,0:T(8,128)(2,1)} %get-tuple-element.54), channel_id=1, source_target_pairs={{0,4},{4,0},{1,5},{5,1},{2,6},{6,2},{3,7},{7,3},{8,12},{12,8},{9,1... | collective-permute-start | bytes 2359304 | tf_op jit(solution)/shard_map/ppermute | solution.py:577
  112.1 10.8 %all-to-all-start.3 = ((f32[4,8,512]{2,1,0:T(8,128)}), f32[4,8,512]{2,1,0:T(8,128)S(1)}, u32[]{:S(2)}, u32[]{:S(2)}) async-start(f32[4,8,512]{2,1,0:T(8,128)} %copy-done.20), calls=%async_computation.3 | async-start | bytes 131072 | tf_op jit(solution)/shard_map/all_to_all | solution.py:562
  124.6 14.3 %all-to-all-start.5 = ((bf16[8,16,2176]{2,1,0:T(8,128)(2,1)}), bf16[8,16,2176]{2,1,0:T(8,128)(2,1)}, u32[]{:S(2)}, u32[]{:S(2)}) async-start(bf16[8,16,2176]{2,1,0:T(8,128)(2,1)} %broadcast_in_dim.14), calls=%async_computation.5 | async-start | bytes 1114112 | tf_op jit(solution)/shard_map/all_to_all | solution.py:567
  128.8 14.3 %collective-permute-start = (bf16[768,512]{1,0:T(8,128)(2,1)}, bf16[768,512]{1,0:T(8,128)(2,1)}, u32[]{:S(2)}, u32[]{:S(2)}) collective-permute-start(bf16[768,512]{1,0:T(8,128)(2,1)} %copy-done.30), channel_id=1, source_target_pairs={{0,4},{4,0},{1,5},{5,1},{2,6},{6,2},{3,7},{7,3},{8,12},{12,8},{9,1... | collective-permute-start | bytes 2359304 | tf_op jit(solution)/shard_map/ppermute | solution.py:577
  138.9 14.4 %all-to-all-start.10 = ((bf16[4,192,512]{2,1,0:T(8,128)(2,1)}), bf16[4,192,512]{2,1,0:T(8,128)(2,1)}, u32[]{:S(2)}, u32[]{:S(2)}) async-start(bf16[4,192,512]{2,1,0:T(8,128)(2,1)} %bitcast.37), calls=%async_computation.10 | async-start | bytes 1572864 | tf_op jit(solution)/shard_map/all_to_all | solution.py:572
  153.3 13.1 %all-to-all-start.6 = ((bf16[4,192,512]{2,1,0:T(8,128)(2,1)}), bf16[4,192,512]{2,1,0:T(8,128)(2,1)S(1)}, u32[]{:S(2)}, u32[]{:S(2)}) async-start(bf16[4,192,512]{2,1,0:T(8,128)(2,1)} %bitcast.38), calls=%async_computation.6 | async-start | bytes 1572864 | tf_op jit(solution)/shard_map/all_to_all | solution.py:572
  166.4 11.3 %all-to-all-start.11 = ((bf16[4,48,512]{2,1,0:T(8,128)(2,1)}), bf16[4,48,512]{2,1,0:T(8,128)(2,1)}, u32[]{:S(2)}, u32[]{:S(2)}) async-start(bf16[4,48,512]{2,1,0:T(8,128)(2,1)} %bitcast.39), calls=%async_computation.11 | async-start | bytes 393216 | tf_op jit(solution)/shard_map/all_to_all | solution.py:572
  177.8 9.6 %all-to-all-start.7 = ((bf16[4,48,512]{2,1,0:T(8,128)(2,1)}), bf16[4,48,512]{2,1,0:T(8,128)(2,1)S(1)}, u32[]{:S(2)}, u32[]{:S(2)}) async-start(bf16[4,48,512]{2,1,0:T(8,128)(2,1)} %bitcast.40), calls=%async_computation.7 | async-start | bytes 393216 | tf_op jit(solution)/shard_map/all_to_all | solution.py:572
  182.1 30.1 %copy-start.43 = (bf16[512]{0:T(512)(128)(2,1)S(1)}, bf16[512]{0:T(512)(128)(2,1)}, u32[]{:S(2)}) copy-start(bf16[512]{0:T(512)(128)(2,1)} %param.20) | copy-start | bytes 3076
  188.1 9.6 %all-to-all-start.12 = ((bf16[4,48,512]{2,1,0:T(8,128)(2,1)}), bf16[4,48,512]{2,1,0:T(8,128)(2,1)S(1)}, u32[]{:S(2)}, u32[]{:S(2)}) async-start(bf16[4,48,512]{2,1,0:T(8,128)(2,1)} %broadcast_in_dim.18), calls=%async_computation.12 | async-start | bytes 393216 | tf_op jit(solution)/shard_map/all_to_all | solution.py:567
  208.6 18.9 %all-to-all-start.13 = ((bf16[4,192,512]{2,1,0:T(8,128)(2,1)}), bf16[4,192,512]{2,1,0:T(8,128)(2,1)S(1)}, u32[]{:S(2)}, u32[]{:S(2)}) async-start(bf16[4,192,512]{2,1,0:T(8,128)(2,1)} %broadcast_in_dim.40), calls=%async_computation.13 | async-start | bytes 1572864 | tf_op jit(solution)/shard_map/all_to_all | solution.py:567
  229.4 12.3 %all-to-all-start.9 = ((bf16[4,192,512]{2,1,0:T(8,128)(2,1)}), bf16[4,192,512]{2,1,0:T(8,128)(2,1)}, u32[]{:S(2)}, u32[]{:S(2)}) async-start(bf16[4,192,512]{2,1,0:T(8,128)(2,1)} %broadcast_in_dim.17), calls=%async_computation.9 | async-start | bytes 1572864 | tf_op jit(solution)/shard_map/all_to_all | solution.py:567
  236.0 9.3 %collective-permute-start.3 = (bf16[768,512]{1,0:T(8,128)(2,1)S(1)}, bf16[768,512]{1,0:T(8,128)(2,1)S(1)}, u32[]{:S(2)}, u32[]{:S(2)}) collective-permute-start(bf16[768,512]{1,0:T(8,128)(2,1)S(1)} %bitcast.36), channel_id=1, source_target_pairs={{0,4},{4,0},{1,5},{5,1},{2,6},{6,2},{3,7},{7,3},{8,12},{12,8},{9,1... | collective-permute-start | bytes 2359304 | tf_op jit(solution)/shard_map/ppermute | solution.py:577
  241.7 4.6 %collective-permute-start.1 = (bf16[768,512]{1,0:T(8,128)(2,1)}, bf16[768,512]{1,0:T(8,128)(2,1)S(1)}, u32[]{:S(2)}, u32[]{:S(2)}) collective-permute-start(bf16[768,512]{1,0:T(8,128)(2,1)} %bitcast.7), channel_id=1, source_target_pairs={{0,4},{4,0},{1,5},{5,1},{2,6},{6,2},{3,7},{7,3},{8,12},{12,8},{9,1... | collective-permute-start | bytes 2359304 | tf_op jit(solution)/shard_map/ppermute | solution.py:577
  (28 other events, 63.0 us)
where the time goes:
time: 254 us; the launch traced here: 252 us
  Pallas kernels  59.1 us (23%)
  waiting for transfers between devices  56.3 us (22%)
  starting transfers between devices  49.9 us (20%)
  local copies, waits for them, and re-layouts  43.8 us (17%)
  blocking collectives  21 us (8%)
  other arithmetic  18.7 us (7%)
    pallas_call x9, Pallas kernels, call(): pl.pallas_call(kernel, out_shape=[jax.ShapeDtypeStruct(s, d) for s, d in...  59.1 us
    unnamed x90, local copies, waits for them, and re-layouts  35 us
    all_to_all x4, waiting for transfers between devices, scatter_sum(): got = lax.all_to_all(blocks.reshape(count, -1, blocks.shape[1]), axis, 0, 0)  27.3 us
    all_to_all x4, starting transfers between devices, exchange(): return lax.all_to_all(message, 'tm', 0, 0)  19 us
    all_to_all x4, waiting for transfers between devices, spread(): lax.all_to_all(jnp.broadcast_to(block[None], (count, *block.shape)), axis...  19 us
    all_to_all x4, starting transfers between devices, spread(): lax.all_to_all(jnp.broadcast_to(block[None], (count, *block.shape)), axis...  15.4 us
    all_to_all x4, starting transfers between devices, scatter_sum(): got = lax.all_to_all(blocks.reshape(count, -1, blocks.shape[1]), axis, 0, 0)  15 us
    all_to_all x1, blocking collectives, exchange(): return lax.all_to_all(message, 'tm', 0, 0)  11.1 us
  transfers between devices with their start and end apart: 16, of which 9 were waited for; matrix products, arithmetic and copies ran while one was open for 8% of the time, Pallas kernels for 10%

commit v1 on v0

v1 whole, which is shorter than its diff:
```python
import functools

import jax
import jax.numpy as jnp
from jax import lax
from jax.experimental import pallas as pl
from jax.experimental.pallas import tpu as pltpu
from jax.sharding import Mesh, PartitionSpec as P

EPSILON = 1e-05
ROOT_HALF = 0.7071067811865476
SEGS = 3
PAD = 16
CHUNK = 64
EDGE = 8 + 16
F32 = jnp.float32
BF16 = jnp.bfloat16
SMALL, LARGE = 20, 30


class Row:
    def __init__(self, len_ref, r, frames):
        self.frames = frames
        self.z = lax.axis_index("tm")
        self.counts = [len_ref[r, s] for s in range(SEGS)]
        l0, l1, l2 = self.counts
        start = -self.z * frames
        e0 = start + l0
        e1 = e0 + l1
        e2 = e1 + l2
        self.begins = [start, e0, e1]
        self.ends = [e0, e1, e2]
        self.long_at = jnp.where(l0 >= jnp.maximum(l1, l2), 0, jnp.where(l1 >= l2, 1, 2))
        self.long_begin = self.of_long(self.begins)
        self.long_end = self.of_long(self.ends)

    def of_long(self, values):
        return jnp.where(
            self.long_at == 0, values[0], jnp.where(self.long_at == 1, values[1], values[2])
        )

    def segment(self, t):
        return sum((t >= e).astype(jnp.int32) for e in self.ends)

    def chunks(self, uniform_fn, mixed_fn):
        def body(i, carry):
            t0 = pl.multiple_of(i * CHUNK, CHUNK)
            first, last = self.segment(t0), self.segment(t0 + CHUNK - 1)
            uniform = jnp.logical_and(first == last, first < SEGS)

            @pl.when(uniform)
            def _():
                uniform_fn(t0, first)

            @pl.when(jnp.logical_not(uniform))
            def _():
                mixed_fn(t0)

            return carry

        lax.fori_loop(0, self.frames // CHUNK, body, 0)


def frame_ids(t0, rows, width):
    return t0 + lax.broadcasted_iota(jnp.int32, (rows, width), 0)


def pick(tab_ref, base, t, row):
    value = jnp.where(t >= row.ends[0], tab_ref[base + 1 : base + 2, :], tab_ref[base : base + 1, :])
    return jnp.where(t >= row.ends[1], tab_ref[base + 2 : base + 3, :], value)


def row_of(tab_ref, base, s):
    return tab_ref[pl.ds(base + s, 1), :]


def fold(x):
    return jnp.sum(x.reshape(x.shape[0] // 8, 8, x.shape[1]), axis=0)


def add_sums(acc_ref, s, first, second):
    acc_ref[s] += fold(first)
    acc_ref[4 + s] += fold(second)


def add_masked_sums(acc_ref, t, row, first, second):
    for s in range(SEGS):
        inside = jnp.logical_and(t >= row.begins[s], t < row.ends[s])
        add_sums(acc_ref, s, jnp.where(inside, first, 0.0), jnp.where(inside, second, 0.0))


def put_sums(acc_ref, st_ref, msg_refs, row, r):
    for s in range(SEGS):
        for k in range(2):
            st_ref[r, pl.ds(SEGS * k + s, 1), :] = jnp.sum(acc_ref[4 * k + s], axis=0, keepdims=True)
    for k in range(2):
        value = jnp.sum(acc_ref[4 * k + row.long_at], axis=0, keepdims=True)
        for ref in msg_refs:
            ref[pl.ds(2 * r + k, 1), :] = value


def sums_of(row, r, st_ref, rx_refs, s):
    out = []
    for k in range(2):
        total = sum(ref[pl.ds(2 * r + k, 1), :] for ref in rx_refs)
        local = st_ref[r, SEGS * k + s : SEGS * k + s + 1, :]
        out.append(jnp.where(row.long_at == s, total, local))
    return out


def norm_of(row, r, st_ref, rx_ref, aff_ref, s):
    width = st_ref.shape[2]
    first, second = sums_of(row, r, st_ref, rx_ref, s)
    count = jnp.full((1, width), row.counts[s].astype(F32))
    mean = first / count
    rstd = lax.rsqrt(second / count - mean * mean + EPSILON)
    affine = aff_ref[r, s : s + 1, :]
    return mean, rstd, 1.0 + affine[:, :width], affine[:, width:], count


def put_forward(row, r, st_ref, rx_ref, aff_ref, tab_ref):
    scales, shifts = [], []
    for s in range(SEGS):
        mean, rstd, gain, beta, _ = norm_of(row, r, st_ref, rx_ref, aff_ref, s)
        scales.append(gain * rstd)
        shifts.append(beta - mean * scales[-1])
        tab_ref[s : s + 1, :] = scales[s]
        tab_ref[SEGS + s : SEGS + s + 1, :] = shifts[s]
    tab_ref[6:7, :] = row.of_long(scales)
    tab_ref[7:8, :] = row.of_long(shifts)


def put_backward(row, r, st_ref, rx_ref, gst_ref, grx_ref, aff_ref, tab_ref):
    parts = [[], [], []]
    for s in range(SEGS):
        mean, rstd, gain, _, count = norm_of(row, r, st_ref, rx_ref, aff_ref, s)
        shift, scale = sums_of(row, r, gst_ref, grx_ref, s)
        scale = rstd * (scale - mean * shift)
        mean_g = gain * shift / count
        slope = rstd * rstd * (gain * scale / count)
        parts[0].append(gain * rstd)
        parts[1].append(-slope)
        parts[2].append(slope * mean - rstd * mean_g)
    for k in range(3):
        for s in range(SEGS):
            tab_ref[SEGS * k + s : SEGS * k + s + 1, :] = parts[k][s]
        tab_ref[9 + k : 10 + k, :] = row.of_long(parts[k])


def put_affine_grads(row, r, st_ref, rx_ref, gst_ref, aff_ref, out_ref, at):
    width = st_ref.shape[2]
    for s in range(SEGS):
        mean, rstd, _, _, _ = norm_of(row, r, st_ref, rx_ref, aff_ref, s)
        shift = gst_ref[r, s : s + 1, :]
        scale = rstd * (gst_ref[r, SEGS + s : SEGS + s + 1, :] - mean * shift)
        out_ref[pl.ds(4 * r + s, 1), at : at + width] = scale
        out_ref[pl.ds(4 * r + s, 1), at + width : at + 2 * width] = shift


def silu(a):
    half = 0.5 * a
    return half + half * jnp.tanh(half)


def silu_and_slope(a):
    gate = 0.5 + 0.5 * jnp.tanh(0.5 * a)
    low = a * gate
    return low, gate + low * (1.0 - gate)


def halo_tile(row, frames, width, left):
    t = frame_ids(-PAD if left else frames, PAD, width)
    near = jnp.logical_and(t >= -2, t < frames + 2)
    inside = jnp.logical_and(t >= row.long_begin, t < row.long_end)
    return t, jnp.logical_and(near, inside)


def edge_tile(rx_refs, row, r, t, at, left):
    last = len(rx_refs) - 1
    neighbour = jnp.maximum(row.z - 1, 0) if left else jnp.minimum(row.z + 1, last)
    edges = []
    for i in range(2):
        value, k = rx_refs[1][pl.ds(8 + 4 * r + at + i, 1), :], 3
        while k <= last:
            value = jnp.where((row.z ^ neighbour) == k, rx_refs[k][pl.ds(8 + 4 * r + at + i, 1), :], value)
            k = 2 * k + 1
        edges.append(value)
    second = -1 if left else row.frames + 1
    return jnp.where(t == second, edges[1], edges[0])


def stack_taps(buf_ref, xs_ref, row, frames, forward, halo, low_ref=None, r=None):
    width = buf_ref.shape[1]
    before_at, after_at = (0, 2 * width) if forward else (2 * width, 0)
    base = PAD if halo else 0
    for i in range(frames // CHUNK):
        o, d = PAD + i * CHUNK, base + i * CHUNK
        centre = buf_ref[o : o + CHUNK, :].astype(BF16)
        xs_ref[d : d + CHUNK, width : 2 * width] = centre
        xs_ref[d : d + CHUNK, before_at : before_at + width] = buf_ref[o - 1 : o - 1 + CHUNK, :].astype(BF16)
        xs_ref[d : d + CHUNK, after_at : after_at + width] = buf_ref[o + 1 : o + 1 + CHUNK, :].astype(BF16)
        if low_ref is not None:
            low_ref[r, i * CHUNK : (i + 1) * CHUNK, :] = centre
    if halo:
        end = PAD + frames
        left, right = buf_ref[0:PAD, :], buf_ref[end : end + PAD, :]
        xs_ref[0:PAD, width : 2 * width] = left.astype(BF16)
        xs_ref[end : end + PAD, width : 2 * width] = right.astype(BF16)
        xs_ref[0:PAD, before_at : before_at + width] = pltpu.roll(left, 1, 0).astype(BF16)
        xs_ref[end : end + PAD, before_at : before_at + width] = buf_ref[end - 1 : end - 1 + PAD, :].astype(BF16)
        xs_ref[0:PAD, after_at : after_at + width] = buf_ref[1 : 1 + PAD, :].astype(BF16)
        xs_ref[end : end + PAD, after_at : after_at + width] = pltpu.roll(right, PAD - 1, 0).astype(BF16)
    for end in row.ends[:2]:
        for at, t in ((before_at, end), (after_at, end - 1)):

            @pl.when(jnp.logical_and(t >= 0, t < frames))
            def _(at=at, t=t):
                tile = pl.multiple_of((t // PAD) * PAD, PAD)
                rows = pl.ds(base + tile, PAD)
                value = xs_ref[rows, at : at + width].astype(F32)
                keep = frame_ids(tile, PAD, width) != t
                xs_ref[rows, at : at + width] = jnp.where(keep, value, 0.0).astype(BF16)


def times_transposed(xs, w_ref, width):
    out = None
    for k in range(3):
        part = lax.dot_general(
            xs[:, k * width : (k + 1) * width],
            w_ref[k * width : (k + 1) * width, :],
            (((1,), (1,)), ((), ())),
            preferred_element_type=F32,
        )
        out = part if out is None else out + part
    return out


def for_rows(len_ref, rows, frames, body):
    def step(r, carry):
        body(r, Row(len_ref, r, frames))
        return carry

    lax.fori_loop(0, rows, step, 0)


def token_sums_kernel(len_ref, tok_hbm, og_hbm, w_hbm, tok_ref, w_ref, st_ref, msg_refs, head_ref, tail_ref, acc_ref,
                      sems, row_sems):
    rows, frames, width = tok_ref.shape

    def row_copy(r):
        return pltpu.make_async_copy(tok_hbm.at[r], tok_ref.at[r], row_sems.at[r])

    for r in range(rows):
        row_copy(r).start()
    edges = (
        pltpu.make_async_copy(og_hbm.at[:, pl.ds(0, PAD), :], head_ref, sems.at[0]),
        pltpu.make_async_copy(og_hbm.at[:, pl.ds(frames - PAD, PAD), :], tail_ref, sems.at[1]),
    )
    for copy in edges:
        copy.start()
    kernel_copy = pltpu.make_async_copy(w_hbm, w_ref, sems.at[2])
    kernel_copy.start()
    for copy in edges:
        copy.wait()

    def body(r, row):
        row_copy(r).wait()
        acc_ref[...] = jnp.zeros_like(acc_ref)

        def uniform(t0, s):
            v = tok_ref[r, pl.ds(t0, CHUNK), :].astype(F32)
            add_sums(acc_ref, s, v, v * v)

        def mixed(t0):
            v = tok_ref[r, pl.ds(t0, CHUNK), :].astype(F32)
            add_masked_sums(acc_ref, frame_ids(t0, CHUNK, width), row, v, v * v)

        row.chunks(uniform, mixed)
        put_sums(acc_ref, st_ref, msg_refs, row, r)
        for j, (head, tail) in enumerate(
            ((tok_ref[r, 0:PAD, :], tok_ref[r, frames - PAD : frames, :]), (head_ref[r], tail_ref[r]))
        ):
            first, last = head.astype(F32), tail.astype(F32)
            for i in range(2):
                to_left, to_right = first[i : i + 1, :], last[PAD - 2 + i : PAD - 1 + i, :]
                for k, ref in enumerate(msg_refs):
                    value = jnp.where(row.z < row.z ^ k, to_right, to_left)
                    ref[pl.ds(8 + 4 * r + 2 * j + i, 1), :] = value

    for_rows(len_ref, rows, frames, body)
    kernel_copy.wait()


def first_half_kernel(len_ref, tok_ref, st_ref, rx_ref, aff_ref, w_ref, og_hbm, w2_hbm, low_hbm, hid_hbm,
                      hid_ref, st2_ref, msg_ref, og_ref, w2_ref, low_ref, buf_ref, xs_ref, tab_ref, acc_ref,
                      sems, row_sems):
    rows, frames, width = tok_ref.shape

    def row_copies(r):
        return (
            pltpu.make_async_copy(low_ref.at[r], low_hbm.at[r], row_sems.at[r]),
            pltpu.make_async_copy(hid_ref.at[r], hid_hbm.at[r], row_sems.at[rows + r]),
        )

    copies = (
        pltpu.make_async_copy(og_hbm, og_ref, sems.at[0]),
        pltpu.make_async_copy(w2_hbm, w2_ref, sems.at[1]),
    )
    for copy in copies:
        copy.start()

    def body(r, row):
        put_forward(row, r, st_ref, rx_ref, aff_ref, tab_ref)

        def uniform(t0, s):
            v = tok_ref[r, pl.ds(t0, CHUNK), :].astype(F32)
            buf_ref[pl.ds(PAD + t0, CHUNK), :] = silu(v * row_of(tab_ref, 0, s) + row_of(tab_ref, SEGS, s))

        def mixed(t0):
            t = frame_ids(t0, CHUNK, width)
            v = tok_ref[r, pl.ds(t0, CHUNK), :].astype(F32)
            low = silu(v * pick(tab_ref, 0, t, row) + pick(tab_ref, SEGS, t, row))
            buf_ref[pl.ds(PAD + t0, CHUNK), :] = jnp.where(t < row.ends[2], low, 0.0)

        row.chunks(uniform, mixed)
        for left in (True, False):
            t, valid = halo_tile(row, frames, width, left)
            low = silu(edge_tile(rx_ref, row, r, t, 0, left) * tab_ref[6:7, :] + tab_ref[7:8, :])
            at = 0 if left else PAD + frames
            buf_ref[at : at + PAD, :] = jnp.where(valid, low, 0.0)
        stack_taps(buf_ref, xs_ref, row, frames, True, True, low_ref, r)
        hid_ref[r] = jnp.dot(xs_ref[...], w_ref[...], preferred_element_type=F32)
        for copy in row_copies(r):
            copy.start()

        acc_ref[...] = jnp.zeros_like(acc_ref)

        def uniform_sums(t0, s):
            v = hid_ref[r, pl.ds(PAD + t0, CHUNK), :]
            add_sums(acc_ref, s, v, v * v)

        def mixed_sums(t0):
            v = hid_ref[r, pl.ds(PAD + t0, CHUNK), :]
            add_masked_sums(acc_ref, frame_ids(t0, CHUNK, width), row, v, v * v)

        row.chunks(uniform_sums, mixed_sums)
        put_sums(acc_ref, st2_ref, [msg_ref], row, r)

    for_rows(len_ref, rows, frames, body)
    for r in range(rows):
        copies += row_copies(r)
    for copy in copies:
        copy.wait()


def branch_grad_kernel(len_ref, og_ref, rx_ref, w_ref, gs_ref, q_ref, bias_ref, buf_ref, xs_ref):
    rows, frames, width = og_ref.shape
    bias_ref[...] = jnp.zeros_like(bias_ref)

    def body(r, row):
        def put(t0, g):
            g = g.astype(BF16).astype(F32)
            buf_ref[pl.ds(PAD + t0, CHUNK), :] = g
            bias_ref[...] += fold(g)

        def uniform(t0, s):
            put(t0, og_ref[r, pl.ds(t0, CHUNK), :].astype(F32) * ROOT_HALF)

        def mixed(t0):
            t = frame_ids(t0, CHUNK, width)
            g = og_ref[r, pl.ds(t0, CHUNK), :].astype(F32) * ROOT_HALF
            put(t0, jnp.where(t < row.ends[2], g, 0.0))

        row.chunks(uniform, mixed)
        for left in (True, False):
            t, valid = halo_tile(row, frames, width, left)
            at = 0 if left else PAD + frames
            g = edge_tile(rx_ref, row, r, t, 2, left) * ROOT_HALF
            buf_ref[at : at + PAD, :] = jnp.where(valid, g, 0.0)
        stack_taps(buf_ref, xs_ref, row, frames, False, True)
        gs_ref[r] = xs_ref[PAD : PAD + frames, :]
        q_ref[r] = times_transposed(xs_ref[...], w_ref, width).astype(BF16)

    for_rows(len_ref, rows, frames, body)


def second_norm_kernel(len_ref, hid_ref, q_ref, st_ref, rx_ref, aff_ref, low_ref, low_hbm, da_hbm, gst_ref, msg_ref,
                       da_ref, tab_ref, acc_ref, row_sems):
    rows, padded, width = hid_ref.shape
    frames = padded - 2 * PAD

    def row_copies(r):
        return (
            pltpu.make_async_copy(low_ref.at[r], low_hbm.at[r], row_sems.at[r]),
            pltpu.make_async_copy(da_ref.at[r], da_hbm.at[r], row_sems.at[rows + r]),
        )

    def body(r, row):
        put_forward(row, r, st_ref, rx_ref, aff_ref, tab_ref)
        acc_ref[...] = jnp.zeros_like(acc_ref)

        def uniform(t0, s):
            at = pl.ds(PAD + t0, CHUNK)
            v = hid_ref[r, at, :]
            low, slope = silu_and_slope(v * row_of(tab_ref, 0, s) + row_of(tab_ref, SEGS, s))
            da = slope * q_ref[r, at, :].astype(F32)
            low_ref[r, at, :] = low.astype(BF16)
            da_ref[r, at, :] = da.astype(BF16)
            add_sums(acc_ref, s, da, da * v)

        def mixed(t0):
            at = pl.ds(PAD + t0, CHUNK)
            t = frame_ids(t0, CHUNK, width)
            live = t < row.ends[2]
            v = hid_ref[r, at, :]
            low, slope = silu_and_slope(v * pick(tab_ref, 0, t, row) + pick(tab_ref, SEGS, t, row))
            da = slope * q_ref[r, at, :].astype(F32)
            low_ref[r, at, :] = jnp.where(live, low, 0.0).astype(BF16)
            da_ref[r, at, :] = jnp.where(live, da, 0.0).astype(BF16)
            add_masked_sums(acc_ref, t, row, da, da * v)

        row.chunks(uniform, mixed)
        for left in (True, False):
            t, valid = halo_tile(row, frames, width, left)
            at = 0 if left else PAD + frames
            v = hid_ref[r, at : at + PAD, :]
            low, slope = silu_and_slope(v * tab_ref[6:7, :] + tab_ref[7:8, :])
            da = slope * q_ref[r, at : at + PAD, :].astype(F32)
            low_ref[r, at : at + PAD, :] = jnp.where(valid, low, 0.0).astype(BF16)
            da_ref[r, at : at + PAD, :] = jnp.where(valid, da, 0.0).astype(BF16)
        for copy in row_copies(r):
            copy.start()
        put_sums(acc_ref, gst_ref, [msg_ref], row, r)

    for_rows(len_ref, rows, frames, body)
    for r in range(rows):
        for copy in row_copies(r):
            copy.wait()


class Loads:
    def __init__(self, rows, sems, whole, by_row):
        count = len(whole)
        self.whole = [pltpu.make_async_copy(a, b, sems.at[i]) for i, (a, b) in enumerate(whole)]
        self.row = lambda r: [
            pltpu.make_async_copy(a.at[r], b.at[r], sems.at[count + i * rows + r]) for i, (a, b) in enumerate(by_row)
        ]
        for r in range(rows):
            for copy in self.row(r):
                copy.start()
            if r == 0:
                for copy in self.whole:
                    copy.start()

    def wait(self, r):
        for copy in self.row(r):
            copy.wait()

        @pl.when(r == 0)
        def _():
            for copy in self.whole:
                copy.wait()


def block_out_kernel(len_ref, low_hbm, tok_hbm, w_hbm, bias_ref, out_hbm, low_ref, tok_ref, w_ref, buf_ref, xs_ref,
                     out_ref, sems, row_sems):
    rows, frames, width = tok_ref.shape
    loads = Loads(rows, sems, [(w_hbm, w_ref)], [(low_hbm, low_ref), (tok_hbm, tok_ref)])

    def row_copy(r):
        return pltpu.make_async_copy(out_ref.at[r], out_hbm.at[r], row_sems.at[r])

    def body(r, row):
        loads.wait(r)
        buf_ref[...] = low_ref[r].astype(F32)
        stack_taps(buf_ref, xs_ref, row, frames, True, False)
        branch = jnp.dot(xs_ref[...], w_ref[...], preferred_element_type=F32) + bias_ref[...].astype(F32)
        live = frame_ids(0, frames, width) < row.ends[2]
        out = (tok_ref[r].astype(F32) + jnp.where(live, branch, 0.0)) * ROOT_HALF
        out_ref[r] = out.astype(BF16)
        row_copy(r).start()

    for_rows(len_ref, rows, frames, body)
    for r in range(rows):
        row_copy(r).wait()


def half_of_grad(low_ref, gs_ref, r, half, first_frame):
    frames, width = gs_ref.shape[1], low_ref.shape[2] // 2
    u = low_ref[r, first_frame : first_frame + frames, pl.ds(pl.multiple_of(half * width, width), width)]
    return lax.dot_general(u, gs_ref[r], (((0,), (0,)), ((), ())), preferred_element_type=F32)


def put_half(acc_ref, out_ref):
    half, width = acc_ref.shape[0], acc_ref.shape[1] // 3
    for k in range(3):
        out_ref[k * half : (k + 1) * half, :] = acc_ref[:, k * width : (k + 1) * width].astype(BF16)


def kernel_grad_kernel(own, first_frame, low_ref, gs_ref, out_ref, acc_ref):
    core = lax.axis_index("core")
    half = core if own else 1 - core
    acc_ref[...] = half_of_grad(low_ref, gs_ref, 0, half, first_frame)

    def step(r, carry):
        acc_ref[...] += half_of_grad(low_ref, gs_ref, r, half, first_frame)
        return carry

    lax.fori_loop(1, low_ref.shape[0], step, 0)
    put_half(acc_ref, out_ref)


def hidden_grad_kernel(len_ref, low_hbm, da_hbm, hid_hbm, st_ref, rx_ref, gst_ref, grx_ref, aff_ref,
                       gs_hbm, send_ref, keep_ref, part_ref, low_ref, da_ref, hid_ref, gs_ref, buf_ref, tab_ref, acc_ref,
                       sems, row_sems):
    rows, frames, width = low_ref.shape
    loads = Loads(rows, sems, [], [(da_hbm, da_ref), (hid_hbm, hid_ref), (low_hbm, low_ref)])
    part_ref[...] = jnp.zeros_like(part_ref)
    acc_ref[...] = jnp.zeros_like(acc_ref)

    def row_copy(r):
        return pltpu.make_async_copy(gs_ref.at[r], gs_hbm.at[r], row_sems.at[r])

    def body(r, row):
        put_affine_grads(row, r, st_ref, rx_ref, gst_ref, aff_ref, part_ref, 0)
        put_backward(row, r, st_ref, rx_ref, gst_ref, grx_ref, aff_ref, tab_ref)
        loads.wait(r)

        def uniform(t0, s):
            at = pl.ds(PAD + t0, CHUNK)
            buf_ref[at, :] = (
                da_ref[r, at, :].astype(F32) * row_of(tab_ref, 0, s)
                + hid_ref[r, at, :] * row_of(tab_ref, SEGS, s)
                + row_of(tab_ref, 2 * SEGS, s)
            )

        def mixed(t0):
            at = pl.ds(PAD + t0, CHUNK)
            t = frame_ids(t0, CHUNK, width)
            grad = (
                da_ref[r, at, :].astype(F32) * pick(tab_ref, 0, t, row)
                + hid_ref[r, at, :] * pick(tab_ref, SEGS, t, row)
                + pick(tab_ref, 2 * SEGS, t, row)
            )
            buf_ref[at, :] = jnp.where(t < row.ends[2], grad, 0.0)

        row.chunks(uniform, mixed)
        for left in (True, False):
            t, valid = halo_tile(row, frames, width, left)
            at = 0 if left else PAD + frames
            grad = (
                da_ref[r, at : at + PAD, :].astype(F32) * tab_ref[9:10, :]
                + hid_ref[r, at : at + PAD, :] * tab_ref[10:11, :]
                + tab_ref[11:12, :]
            )
            buf_ref[at : at + PAD, :] = jnp.where(valid, grad, 0.0)
        stack_taps(buf_ref, gs_ref.at[r], row, frames, False, False)
        row_copy(r).start()
        acc_ref[...] += lax.dot_general(
            low_ref[r], gs_ref[r], (((0,), (0,)), ((), ())), preferred_element_type=F32
        )

    for_rows(len_ref, rows, frames, body)
    core, half = lax.axis_index("core"), width // 2
    for ref, which in ((send_ref, 1 - core), (keep_ref, core)):
        put_half(acc_ref.at[pl.ds(pl.multiple_of(which * half, half), half), :], ref)
    for r in range(rows):
        row_copy(r).wait()


def first_norm_grad_kernel(len_ref, gs_hbm, w_hbm, tok_hbm, st_ref, rx_ref, aff_ref, part2_ref, bias_ref,
                           da_hbm, gst_ref, msg_ref, out_ref, gs_ref, w_ref, tok_ref, da_ref, q_ref, tab_ref, acc_ref,
                           part_ref, sems, row_sems):
    rows, frames, width = tok_ref.shape
    loads = Loads(rows, sems, [(w_hbm, w_ref)], [(gs_hbm, gs_ref), (tok_hbm, tok_ref)])
    part_ref[:, : 2 * width] = jnp.zeros((part_ref.shape[0], 2 * width), F32)
    part_ref[:, 2 * width :] = part2_ref[...]
    part_ref[SEGS : SEGS + 1, :width] = jnp.sum(bias_ref[...], axis=0, keepdims=True)

    def row_copy(r):
        return pltpu.make_async_copy(da_ref.at[r], da_hbm.at[r], row_sems.at[r])

    def body(r, row):
        put_forward(row, r, st_ref, rx_ref, aff_ref, tab_ref)
        loads.wait(r)
        q_ref[...] = times_transposed(gs_ref[r], w_ref, width)
        acc_ref[...] = jnp.zeros_like(acc_ref)

        def uniform(t0, s):
            at = pl.ds(t0, CHUNK)
            v = tok_ref[r, at, :].astype(F32)
            _, slope = silu_and_slope(v * row_of(tab_ref, 0, s) + row_of(tab_ref, SEGS, s))
            da = slope * q_ref[at, :]
            da_ref[r, at, :] = da.astype(BF16)
            add_sums(acc_ref, s, da, da * v)

        def mixed(t0):
            at = pl.ds(t0, CHUNK)
            t = frame_ids(t0, CHUNK, width)
            v = tok_ref[r, at, :].astype(F32)
            _, slope = silu_and_slope(v * pick(tab_ref, 0, t, row) + pick(tab_ref, SEGS, t, row))
            da = slope * q_ref[at, :]
            da_ref[r, at, :] = jnp.where(t < row.ends[2], da, 0.0).astype(BF16)
            add_masked_sums(acc_ref, t, row, da, da * v)

        row.chunks(uniform, mixed)
        row_copy(r).start()
        put_sums(acc_ref, gst_ref, [msg_ref], row, r)
        put_affine_grads(row, r, st_ref, rx_ref, gst_ref, aff_ref, part_ref, 0)

    for_rows(len_ref, rows, frames, body)
    out_ref[...] = part_ref[...].astype(BF16)
    for r in range(rows):
        row_copy(r).wait()


def input_grad_kernel(len_ref, og_hbm, da_hbm, tok_hbm, st_ref, rx_ref, gst_ref, grx_ref, aff_ref, out_hbm,
                      og_ref, da_ref, tok_ref, tab_ref, out_ref, sems, row_sems):
    rows, frames, width = tok_ref.shape
    loads = Loads(rows, sems, [], [(og_hbm, og_ref), (da_hbm, da_ref), (tok_hbm, tok_ref)])

    def row_copy(r):
        return pltpu.make_async_copy(out_ref.at[r], out_hbm.at[r], row_sems.at[r])

    def body(r, row):
        put_backward(row, r, st_ref, rx_ref, gst_ref, grx_ref, aff_ref, tab_ref)
        loads.wait(r)

        def uniform(t0, s):
            at = pl.ds(t0, CHUNK)
            out = (
                og_ref[r, at, :].astype(F32) * ROOT_HALF
                + da_ref[r, at, :].astype(F32) * row_of(tab_ref, 0, s)
                + tok_ref[r, at, :].astype(F32) * row_of(tab_ref, SEGS, s)
                + row_of(tab_ref, 2 * SEGS, s)
            )
            out_ref[r, at, :] = out.astype(BF16)

        def mixed(t0):
            at = pl.ds(t0, CHUNK)
            t = frame_ids(t0, CHUNK, width)
            grad = (
                da_ref[r, at, :].astype(F32) * pick(tab_ref, 0, t, row)
                + tok_ref[r, at, :].astype(F32) * pick(tab_ref, SEGS, t, row)
                + pick(tab_ref, 2 * SEGS, t, row)
            )
            out = og_ref[r, at, :].astype(F32) * ROOT_HALF + jnp.where(t < row.ends[2], grad, 0.0)
            out_ref[r, at, :] = out.astype(BF16)

        row.chunks(uniform, mixed)
        row_copy(r).start()

    for_rows(len_ref, rows, frames, body)
    for r in range(rows):
        row_copy(r).wait()


def assemble_kernel(mine_ref, other_ref, out2_hbm, out1_hbm, buf_ref, sems):
    chips, count, _, rows, width = mine_ref.shape
    half = chips * count * rows // 3
    first = lax.axis_index("core") == 0
    copies = []
    for which, out_hbm in enumerate((out2_hbm, out1_hbm)):
        for b in range(chips * count):
            for j in range(rows // PAD):
                at = b * rows + j * PAD
                tap, channel = at // half, at % half
                block = (b // count, b % count, which, slice(j * PAD, (j + 1) * PAD))
                mine, other = mine_ref[block].astype(F32), other_ref[block].astype(F32)
                buf_ref[which, tap, channel : channel + PAD, :] = jnp.where(first, mine, other)
                buf_ref[which, tap, half + channel : half + channel + PAD, :] = jnp.where(first, other, mine)
        copies.append(pltpu.make_async_copy(buf_ref.at[which], out_hbm, sems.at[which]))
        copies[-1].start()
    for copy in copies:
        copy.wait()


SPACES = {"s": pltpu.SMEM, "v": pltpu.VMEM, "h": pltpu.HBM}


def call(kernel, spaces, arrays, outs, scratch, vmem_mib, flops=0, nbytes=8 << 20):
    arrays = [
        pltpu.with_memory_space_constraint(a, pltpu.HBM) if c == "h" else a for c, a in zip(spaces, arrays)
    ]
    letters = list(zip(spaces, [*arrays, *outs]))
    specs = [jax.tree.map(lambda _, c=c: pl.BlockSpec(memory_space=SPACES[c]), a) for c, a in letters[: len(arrays)]]

    def shape_of(c, out):
        return pltpu.HBM(*out) if c == "h" else jax.ShapeDtypeStruct(*out)

    def spec_of(c, out):
        return pl.BlockSpec(memory_space=SPACES[c])

    shapes, out_specs = (
        [[f(c, o) for o in out] if isinstance(out, list) else f(c, out) for c, out in letters[len(arrays) :]]
        for f in (shape_of, spec_of)
    )
    return pl.pallas_call(
        kernel,
        out_shape=shapes,
        in_specs=specs,
        out_specs=out_specs,
        scratch_shapes=[pltpu.SemaphoreType.DMA(s) if len(s) == 1 else pltpu.VMEM(*s) for s in scratch],
        compiler_params=pltpu.CompilerParams(vmem_limit_bytes=vmem_mib << 20),
        cost_estimate=pl.CostEstimate(flops=flops, bytes_accessed=nbytes, transcendentals=0),
    )(*arrays)


def after(x, *others):
    return lax.optimization_barrier((x, *others))[0]


def exchange(messages):
    return [messages[0]] + [swap(m, "tm", k) for k, m in enumerate(messages) if k > 0]


def scatter_sum(blocks, axis):
    return jnp.sum(lax.all_to_all(blocks, axis, 0, 0).astype(F32), axis=0).astype(BF16)


def spread(block, axis):
    return lax.all_to_all(jnp.broadcast_to(block[None], (lax.axis_size(axis), *block.shape)), axis, 0, 0)


def swap(x, axis, bit):
    return lax.ppermute(x, axis, [(i, i ^ bit) for i in range(lax.axis_size(axis))])


def sum_over_tm(x):
    count = lax.axis_size("tm")
    parts = [x.astype(F32)] + [swap(x, "tm", k).astype(F32) for k in range(1, count)]
    while len(parts) > 1:
        half = len(parts) // 2
        parts = [a + b for a, b in zip(parts[:half], parts[half:])]
    return parts[0]


def gather_rows(x):
    steps = [("core", 1)] + [("chip", 1 << b) for b in range((lax.axis_size("chip") - 1).bit_length())]
    for axis, bit in steps:
        other = swap(x, axis, bit)
        upper = (lax.axis_index(axis) & bit) != 0
        x = jnp.where(upper, jnp.concatenate([other, x]), jnp.concatenate([x, other]))
    return x


def per_device(tokens, lengths, style, fc1_weight, fc1_bias, conv1_kernel, fc2_weight, fc2_bias, conv2_kernel,
               conv2_bias, out_grad):
    rows, frames, width = tokens.shape
    count, chips = lax.axis_size("tm"), lax.axis_size("chip")
    padded = frames + 2 * PAD
    affine1 = jnp.einsum("rsk,kc->rsc", style, fc1_weight, preferred_element_type=F32) + fc1_bias.astype(F32)
    affine2 = jnp.einsum("rsk,kc->rsc", style, fc2_weight, preferred_element_type=F32) + fc2_bias.astype(F32)
    kernel1, kernel2 = (k.reshape(3 * width, width) for k in (conv1_kernel, conv2_kernel))

    own, wide = ((rows, frames, width), BF16), ((rows, padded, width), BF16)
    hid, taps, kernel = ((rows, padded, width), F32), ((rows, frames, 3 * width), BF16), ((3 * width, width), BF16)
    sums, msg, half = ((rows, 8, width), F32), ((2 * rows, width), F32), ((3 * width // 2, width), BF16)
    acc, tab = ((8, 8, width), F32), ((16, width), F32)
    buf, xs = ((padded, width), F32), ((padded, 3 * width), BF16)
    flops = 2 * rows * frames * 3 * width * width

    tok, w1, st1, msg1 = call(
        token_sums_kernel, "shhh" + "vvvv", (lengths, tokens, out_grad, kernel1),
        [own, kernel, sums, [((EDGE, width), F32)] * count],
        [((rows, PAD, width), BF16), ((rows, PAD, width), BF16), acc, (3,), (rows,)], SMALL,
    )
    rx1 = exchange(msg1)
    low1, hidden_hbm, hidden, st2, msg2, og, w2 = call(
        first_half_kernel, "svvvvvhh" + "hhvvvvv", (lengths, tok, st1, rx1, affine1, w1, out_grad, kernel2),
        [own, hid, hid, sums, msg, own, kernel], [own, buf, xs, tab, acc, (2,), (2 * rows,)], SMALL, flops,
    )
    rx2 = exchange([msg2] * count)
    gs2, grad_low2, bias_part = call(
        branch_grad_kernel, "svvv" + "vvv", (lengths, og, rx1, w2), [taps, wide, ((8, width), F32)], [buf, xs],
        SMALL, flops,
    )
    low2, low2_hbm, da2, gst2, msg3 = call(
        second_norm_kernel, "svvvvv" + "vhhvv", (lengths, hidden, grad_low2, st2, rx2, affine2),
        [wide, wide, wide, sums, msg], [wide, tab, acc, (2 * rows,)], SMALL,
    )
    rx3 = exchange([msg3] * count)

    def kernel_grad(own_half, first_frame, low, gs):
        return call(
            functools.partial(kernel_grad_kernel, own_half, first_frame), "vvv", (low, gs), [half],
            [((width // 2, 3 * width), F32)], SMALL, flops // 2,
        )[0]

    send2 = kernel_grad(False, PAD, low2, gs2)
    got2 = swap(send2, "core", 1)
    keep2 = kernel_grad(True, PAD, low2, after(gs2, send2, *rx3))
    half2 = (got2.astype(F32) + keep2.astype(F32)).astype(BF16)
    part2 = scatter_sum(half2.reshape(chips, -1, width), "chip")

    gs1, send1, keep1, affine_part2 = call(
        hidden_grad_kernel, "shhhvvvvv" + "hvvv",
        (lengths, low1, after(da2, half2), hidden_hbm, st2, rx2, gst2, rx3, affine2),
        [taps, half, half, ((4 * rows, 2 * width), F32)],
        [own, wide, hid, taps, buf, tab, ((width, 3 * width), F32), (3 * rows,), (rows,)], LARGE, flops,
    )
    got1 = swap(after(send1, part2), "core", 1)
    half1 = (got1.astype(F32) + keep1.astype(F32)).astype(BF16)
    part1 = scatter_sum(half1.reshape(chips, -1, width), "chip")

    da1, gst1, msg4, affine_part = call(
        first_norm_grad_kernel, "shhhvvvvv" + "hvvv",
        (lengths, after(gs1, half1), kernel1, tokens, st1, rx1, affine1, affine_part2, bias_part),
        [own, sums, msg, ((4 * rows, 4 * width), BF16)],
        [taps, kernel, own, own, ((frames, width), F32), tab, acc, ((4 * rows, 4 * width), F32), (1 + 2 * rows,), (rows,)],
        LARGE, flops,
    )
    both = jnp.concatenate([part2.reshape(count, -1, width), part1.reshape(count, -1, width)], axis=1)
    both = scatter_sum(after(both, da1), "tm")
    rx4 = exchange([after(msg4, part1)] * count)
    affine_grads = sum_over_tm(after(affine_part, part1)).astype(BF16)
    (block_out,) = call(
        block_out_kernel, "shhhv" + "h", (lengths, low2_hbm, after(tokens, da1), kernel2, conv2_bias.reshape(1, width)), [own],
        [wide, own, kernel, buf, ((frames, 3 * width), BF16), own, (1 + 2 * rows,), (rows,)], LARGE, flops,
    )
    both = spread(after(both, block_out), "tm")
    (input_grad,) = call(
        input_grad_kernel, "shhhvvvvv" + "h", (lengths, out_grad, da1, tokens, st1, rx1, gst1, rx4, affine1), [own],
        [own, own, own, tab, own, (3 * rows,), (rows,)], LARGE,
    )
    both = spread(after(both, input_grad), "chip")

    mine = affine_grads.reshape(rows, 4, 4 * width)[:, :SEGS].reshape(rows * SEGS, 4 * width)
    style_grad = lax.dot_general(
        mine[:, : 2 * width], fc1_weight, (((1,), (1,)), ((), ())), preferred_element_type=F32
    ) + lax.dot_general(mine[:, 2 * width :], fc2_weight, (((1,), (1,)), ((), ())), preferred_element_type=F32)
    style_pad = jnp.pad(style, ((0, 0), (0, 1), (0, 0))).reshape(rows * 4, -1)
    gathered = gather_rows(jnp.concatenate([affine_grads, style_pad], axis=1))
    grads, styles = gathered[:, : 4 * width], gathered[:, 4 * width :]
    fc_grads = lax.dot_general(styles, grads, (((0,), (0,)), ((), ())), preferred_element_type=F32)
    by_segment = jnp.sum(grads.reshape(-1, 4, 4 * width).astype(F32), axis=0)
    fc_bias_grads = jnp.sum(by_segment[:SEGS], axis=0)

    both = both.reshape(chips, count, 2, -1, width)
    other = swap(after(both, fc_grads, fc_bias_grads, style_grad), "core", 1)
    if both.shape[3] % PAD == 0:
        conv_shape = ((3, width, width), F32)
        conv2_sum, conv1_sum = call(
            assemble_kernel, "vv" + "hh", (both, other), [conv_shape, conv_shape], [((2, 3, width, width), F32), (2,)], SMALL,
        )
    else:
        first = lax.axis_index("core") == 0
        halves = [jnp.where(first, both, other), jnp.where(first, other, both)]
        halves = [jnp.moveaxis(h, 2, 0).reshape(2, 3, width // 2, width) for h in halves]
        conv2_sum, conv1_sum = jnp.concatenate(halves, axis=2).astype(F32)
    return (
        block_out,
        input_grad,
        style_grad.reshape(style.shape),
        fc_grads[:, : 2 * width],
        fc_bias_grads[: 2 * width],
        conv1_sum,
        fc_grads[:, 2 * width :],
        fc_bias_grads[2 * width :],
        conv2_sum,
        by_segment[SEGS, :width],
    )


def solution(mesh):
    chips = mesh.shape["dp"] // 2
    mesh = Mesh(mesh.devices.reshape(chips, 2, mesh.shape["tm"]), ("chip", "core", "tm"))
    dp = ("chip", "core")
    return jax.shard_map(
        per_device,
        mesh=mesh,
        in_specs=(
            P(dp, "tm", None),
            P(dp, None),
            P(dp, None, None),
            P(),
            P(),
            P(),
            P(),
            P(),
            P(),
            P(),
            P(dp, "tm", None),
        ),
        out_specs=(
            P(dp, "tm", None),
            P(dp, "tm", None),
            P(dp, None, None),
            P(),
            P(),
            P(),
            P(),
            P(),
            P(),
            P(),
        ),
        check_vma=False,
    )
```

time: 254 us -> 171 us (0.67)
  local copies, waits for them, and re-layouts: 43.8 us -> 8.52 us
  blocking collectives: 21 us -> 0 us
  waiting for transfers between devices: 56.3 us -> 36.7 us
  other arithmetic: 18.7 us -> 5.47 us
  Pallas kernels: 59.1 us -> 69.7 us
  starting transfers between devices: 49.9 us -> 47.3 us
    unnamed x90 -> x22, local copies, waits for them, and re-layouts: 35 us -> 1.37 us
    all_to_all x12 -> x5, waiting for transfers between devices: 56.3 us -> 24.6 us  [the longest x2 24.2 us: spread(): lax.all_to_all(jnp.broadcast_to(block[None], (lax.axis_size(axis), *block...]
    all_to_all x12 -> x5, starting transfers between devices: 49.5 us -> 19.8 us  [the longest x3 11.1 us: scatter_sum(): lax.all_to_all(blocks, axis, 0, 0).astype(F32)]
    ppermute x4 -> x21, starting transfers between devices: 0.45 us -> 27.4 us  [swap(): lax.ppermute(x, axis, [(i, i ^ bit) for i in range(lax.axis_size(axis))])]
    all_to_all x2 -> x0, blocking collectives: 21 us -> none  [the longest x1 11.1 us: exchange(): return lax.all_to_all(message, 'tm', 0, 0)]
    ppermute x4 -> x21, waiting for transfers between devices: 0.01 us -> 12 us  [swap(): lax.ppermute(x, axis, [(i, i ^ bit) for i in range(lax.axis_size(axis))])]
    pallas_call x9 -> x11, Pallas kernels: 59.1 us -> 69.7 us  [call(): pl.pallas_call(kernel, out_shape=shapes, in_specs=specs, out_specs=out_sp...]
    convert_element_type x4 -> x3, other arithmetic: 8.92 us -> 2.22 us  [the longest x1 1.09 us: per_device(): half2 = (got2.astype(F32) + keep2.astype(F32)).astype(BF16)]
  transfers between devices with their start and end apart: 16 -> 26, of which waited for: 9 -> 10; matrix products, arithmetic and copies ran while one was open for 8% -> 7% of each run, Pallas kernels for 10% -> 26%
where the time goes in v1:
time: 171 us
  Pallas kernels  69.7 us (41%)
  starting transfers between devices  47.3 us (28%)
  waiting for transfers between devices  36.7 us (21%)
  local copies, waits for them, and re-layouts  8.52 us (5%)
  other arithmetic  5.47 us (3%)
  matrix products  1.96 us (1%)
    pallas_call x11, Pallas kernels, call(): pl.pallas_call(kernel, out_shape=shapes, in_specs=specs, out_specs=out_sp...  69.7 us
    ppermute x21, starting transfers between devices, swap(): lax.ppermute(x, axis, [(i, i ^ bit) for i in range(lax.axis_size(axis))])  27.4 us
    all_to_all x2, waiting for transfers between devices, spread(): lax.all_to_all(jnp.broadcast_to(block[None], (lax.axis_size(axis), *block...  24.2 us
    ppermute x21, waiting for transfers between devices, swap(): lax.ppermute(x, axis, [(i, i ^ bit) for i in range(lax.axis_size(axis))])  12 us
    all_to_all x3, starting transfers between devices, scatter_sum(): lax.all_to_all(blocks, axis, 0, 0).astype(F32)  11.1 us
    all_to_all x2, starting transfers between devices, spread(): lax.all_to_all(jnp.broadcast_to(block[None], (lax.axis_size(axis), *block...  8.76 us
  transfers between devices with their start and end apart: 26, of which 10 were waited for; matrix products, arithmetic and copies ran while one was open for 7% of the time, Pallas kernels for 26%

profile of v1, /device:TPU:0, one launch (start us, length us, event | category | flops | bytes accessed | tf_op | source)
XLA Modules:
  0.0 170.8 jit_solution(8588251872301218210)
XLA Ops:
  1.4 3.6 %shard_map.186 = (bf16[4,512,512]{2,1,0:T(8,128)(2,1)S(1)}, bf16[1536,512]{1,0:T(8,128)(2,1)S(1)}, f32[4,8,512]{2,1,0:T(8,128)S(1)}, f32[24,512]{1,0:T(8,128)S(1...) custom-call(s32[4,3]{1,0:T(4,128)S(1)} %copy-done.1, bf16[4,512,512]{2,1,0:T(8,128)(2,1)} %tok_hbm.6, ...), custom_call_target="tpu_custom_call" | custom-call | bytes 8388608 | tf_op jit(solution)/shard_map/pallas_call | solution.py:698
  5.0 3.0 %collective-permute-start = (f32[24,512]{1,0:T(8,128)S(1)}, f32[24,512]{1,0:T(8,128)S(1)}, u32[]{:S(2)}, u32[]{:S(2)}) collective-permute-start(f32[24,512]{1,0:T(8,128)S(1)} %get-tuple-element.56), channel_id=1, source_target_pairs={{0,1},{1,0},{2,3},{3,2},{4,5},{5,4},{6,7},{7,6},{8,9},{9,8},{10,11... | collective-permute-start | bytes 147464 | tf_op jit(solution)/shard_map/ppermute | solution.py:726
  7.9 3.1 %collective-permute-start.1 = (f32[24,512]{1,0:T(8,128)S(1)}, f32[24,512]{1,0:T(8,128)S(1)}, u32[]{:S(2)}, u32[]{:S(2)}) collective-permute-start(f32[24,512]{1,0:T(8,128)S(1)} %get-tuple-element.57), channel_id=1, source_target_pairs={{0,2},{1,3},{2,0},{3,1},{4,6},{5,7},{6,4},{7,5},{8,10},{9,11},{10,... | collective-permute-start | bytes 147464 | tf_op jit(solution)/shard_map/ppermute | solution.py:726
  11.4 2.6 %collective-permute-done.1.rx_ref_2_ = f32[24,512]{1,0:T(8,128)S(1)} collective-permute-done((f32[24,512]{1,0:T(8,128)S(1)}, f32[24,512]{1,0:T(8,128)S(1)}, u32[]{:S(2)}, u32[]{:S(2)}) %collective-permute-start.1) | collective-permute-done | bytes 49184 | tf_op jit(solution)/shard_map/ppermute | solution.py:726
  14.0 2.9 %collective-permute-done.2.rx_ref_3_ = f32[24,512]{1,0:T(8,128)S(1)} collective-permute-done((f32[24,512]{1,0:T(8,128)S(1)}, f32[24,512]{1,0:T(8,128)S(1)}, u32[]{:S(2)}, u32[]{:S(2)}) %collective-permute-start.2) | collective-permute-done | bytes 49184 | tf_op jit(solution)/shard_map/ppermute | solution.py:726
  16.9 10.3 %shard_map.187 = (bf16[4,512,512]{2,1,0:T(8,128)(2,1)}, f32[4,544,512]{2,1,0:T(8,128)}, f32[4,544,512]{2,1,0:T(8,128)S(1)}, f32[4,8,512]{2,1,0:T(8,128)S(1)}, f3...) custom-call(s32[4,3]{1,0:T(4,128)S(1)} %copy-done.1, ...), custom_call_target="tpu_custom_call" | custom-call | flops 3221225472 | bytes 8388608 | tf_op jit(solution)/shard_map/pallas_call | solution.py:698
  27.3 1.8 %collective-permute-start.4 = (f32[8,512]{1,0:T(8,128)S(1)}, f32[8,512]{1,0:T(8,128)S(1)}, u32[]{:S(2)}, u32[]{:S(2)}) collective-permute-start(f32[8,512]{1,0:T(8,128)S(1)} %get-tuple-element.65.rx_ref_0_), channel_id=1, source_target_pairs={{0,2},{1,3},{2,0},{3,1},{4,6},{5,7},{6,4},{7,5},{8,10},{9,11},{10,... | collective-permute-start | bytes 49160 | tf_op jit(solution)/shard_map/ppermute | solution.py:726
  29.2 2.5 %collective-permute-start.5 = (f32[8,512]{1,0:T(8,128)S(1)}, f32[8,512]{1,0:T(8,128)S(1)}, u32[]{:S(2)}, u32[]{:S(2)}) collective-permute-start(f32[8,512]{1,0:T(8,128)S(1)} %get-tuple-element.65.rx_ref_0_), channel_id=1, source_target_pairs={{0,3},{1,2},{2,1},{3,0},{4,7},{5,6},{6,5},{7,4},{8,11},{9,10},{10,... | collective-permute-start | bytes 49160 | tf_op jit(solution)/shard_map/ppermute | solution.py:726
  31.7 8.0 %shard_map.188 = (bf16[4,512,1536]{2,1,0:T(8,128)(2,1)S(1)}, bf16[4,544,512]{2,1,0:T(8,128)(2,1)S(1)}, f32[8,512]{1,0:T(8,128)S(1)}) custom-call(s32[4,3]{1,0:T(4,128)S(1)} %copy-done.1, bf16[4,512,512]{2,1,0:T(8,128)(2,1)S(1)} %get-tuple-element.61.og_ref, f32[24,512]{1,0:T(8,128)S(1)} %get-tuple-element.55.rx_ref_0_, ...), custom_call_target="tpu_custom_call" | custom-call | flops 3221225472 | bytes 8388608 | tf_op jit(solution)/shard_map/pallas_call | solution.py:698
  39.7 5.2 %shard_map.189 = (bf16[4,544,512]{2,1,0:T(8,128)(2,1)S(1)}, bf16[4,544,512]{2,1,0:T(8,128)(2,1)}, bf16[4,544,512]{2,1,0:T(8,128)(2,1)}, f32[4,8,512]{2,1,0:T(8,128)S(1)}, f32[8,512]{1,0:T(8,128)S(1)}) custom-call(s32[4,3]{1,0:T(4,128)S(1)} %copy-done.1, f32[4,544,512]{2,1,0:T(8,128)S(1)} %get-tuple-element.60.hid_ref, ...), custom_call_target="tpu_custom_call" | custom-call | bytes 8388608 | tf_op jit(solution)/shard_map/pallas_call | solution.py:698
  44.9 2.5 %shard_map.190 = bf16[768,512]{1,0:T(8,128)(2,1)S(1)} custom-call(bf16[4,544,512]{2,1,0:T(8,128)(2,1)S(1)} %get-tuple-element.69.low_ref, bf16[4,512,1536]{2,1,0:T(8,128)(2,1)S(1)} %get-tuple-element.72.gs_ref), custom_call_target="tpu_custom_call" | custom-call | flops 1610612736 | bytes 8388608 | tf_op jit(solution)/shard_map/pallas_call | solution.py:698
  47.6 2.5 %collective-permute-start.8 = (f32[8,512]{1,0:T(8,128)S(1)}, f32[8,512]{1,0:T(8,128)S(1)}, u32[]{:S(2)}, u32[]{:S(2)}) collective-permute-start(f32[8,512]{1,0:T(8,128)S(1)} %get-tuple-element.71.grx_ref_0_), channel_id=1, source_target_pairs={{0,2},{1,3},{2,0},{3,1},{4,6},{5,7},{6,4},{7,5},{8,10},{9,11},{10,... | collective-permute-start | bytes 49160 | tf_op jit(solution)/shard_map/ppermute | solution.py:726
  50.1 1.9 %collective-permute-start.9 = (f32[8,512]{1,0:T(8,128)S(1)}, f32[8,512]{1,0:T(8,128)S(1)}, u32[]{:S(2)}, u32[]{:S(2)}) collective-permute-start(f32[8,512]{1,0:T(8,128)S(1)} %get-tuple-element.71.grx_ref_0_), channel_id=1, source_target_pairs={{0,3},{1,2},{2,1},{3,0},{4,7},{5,6},{6,5},{7,4},{8,11},{9,10},{10,... | collective-permute-start | bytes 49160 | tf_op jit(solution)/shard_map/ppermute | solution.py:726
  52.3 3.3 %collective-permute-done.9.grx_ref_3_ = f32[8,512]{1,0:T(8,128)S(1)} collective-permute-done((f32[8,512]{1,0:T(8,128)S(1)}, f32[8,512]{1,0:T(8,128)S(1)}, u32[]{:S(2)}, u32[]{:S(2)}) %collective-permute-start.9) | collective-permute-done | bytes 16416 | tf_op jit(solution)/shard_map/ppermute | solution.py:726
  55.7 2.5 %shard_map.191 = bf16[768,512]{1,0:T(8,128)(2,1)S(1)} custom-call(bf16[4,544,512]{2,1,0:T(8,128)(2,1)S(1)} %get-tuple-element.69.low_ref, bf16[4,512,1536]{2,1,0:T(8,128)(2,1)S(1)} %get-tuple-element.72.gs_ref), custom_call_target="tpu_custom_call" | custom-call | flops 1610612736 | bytes 8388608 | tf_op jit(solution)/shard_map/pallas_call | solution.py:698
  59.3 3.5 %all-to-all-start = ((bf16[4,192,512]{2,1,0:T(8,128)(2,1)}), bf16[4,192,512]{2,1,0:T(8,128)(2,1)S(1)}, u32[]{:S(2)}, u32[]{:S(2)}) async-start(bf16[4,192,512]{2,1,0:T(8,128)(2,1)} %bitcast.4), calls=%async_computation | async-start | bytes 1572864 | tf_op jit(solution)/shard_map/all_to_all | solution.py:718
  62.8 9.7 %shard_map.192 = (bf16[4,512,1536]{2,1,0:T(8,128)(2,1)}, bf16[768,512]{1,0:T(8,128)(2,1)S(1)}, bf16[768,512]{1,0:T(8,128)(2,1)S(1)}, f32[16,1024]{1,0:T(8,128)S(1)}) custom-call(s32[4,3]{1,0:T(4,128)S(1)} %copy-done.2, bf16[4,512,512]{2,1,0:T(8,128)(2,1)} %get-tuple-element.67.low_hbm, bf16[4,544,512]{2,1,0:T(8,128)(2,1)} %get-tuple-element.73.da_hbm, ...), custom_call_target="tpu_custom_call" | custom-call | flops 3221225472 | bytes 8388608 | tf_op jit(solution)/shard_map/pallas_call | solution.py:698
  73.6 2.3 %collective-permute-done.10 = bf16[768,512]{1,0:T(8,128)(2,1)S(1)} collective-permute-done((bf16[768,512]{1,0:T(8,128)(2,1)S(1)}, bf16[768,512]{1,0:T(8,128)(2,1)S(1)}, u32[]{:S(2)}, u32[]{:S(2)}) %collective-permute-start.10) | collective-permute-done | bytes 786464 | tf_op jit(solution)/shard_map/ppermute | solution.py:726
  76.9 3.9 %all-to-all-start.1 = ((bf16[4,192,512]{2,1,0:T(8,128)(2,1)}), bf16[4,192,512]{2,1,0:T(8,128)(2,1)S(1)}, u32[]{:S(2)}, u32[]{:S(2)}) async-start(bf16[4,192,512]{2,1,0:T(8,128)(2,1)} %bitcast.5), calls=%async_computation.1 | async-start | bytes 1572864 | tf_op jit(solution)/shard_map/all_to_all | solution.py:718
  80.9 10.9 %shard_map.193 = (bf16[4,512,512]{2,1,0:T(8,128)(2,1)}, f32[4,8,512]{2,1,0:T(8,128)S(1)}, f32[8,512]{1,0:T(8,128)S(1)}, bf16[16,2048]{1,0:T(8,128)(2,1)S(1)}) custom-call(s32[4,3]{1,0:T(4,128)S(1)} %copy-done.2, bf16[4,512,1536]{2,1,0:T(8,128)(2,1)} %get-tuple-element.80.gs_hbm, bf16[1536,512]{1,0:T(8,128)(2,1)} %bitcast.21, bf16[4,512,512]{2,1,0:T(8,128)(2,1)} %tok_hbm.6, ...), custom_call_target="tpu_custom_call" | custom-call | flops 3221225472 | bytes 8388608 | tf_op jit(solution)/shard_map/pallas_call | solution.py:698
  92.3 3.3 %collective-permute-start.15 = (bf16[16,2048]{1,0:T(8,128)(2,1)S(1)}, bf16[16,2048]{1,0:T(8,128)(2,1)S(1)}, u32[]{:S(2)}, u32[]{:S(2)}) collective-permute-start(bf16[16,2048]{1,0:T(8,128)(2,1)S(1)} %get-tuple-element.89), channel_id=1, source_target_pairs={{0,1},{1,0},{2,3},{3,2},{4,5},{5,4},{6,7},{7,6},{8,9},{9,8},{10,11... | collective-permute-start | bytes 196616 | tf_op jit(solution)/shard_map/ppermute | solution.py:726
  96.7 3.3 %collective-permute-start.12 = (f32[8,512]{1,0:T(8,128)S(1)}, f32[8,512]{1,0:T(8,128)S(1)}, u32[]{:S(2)}, u32[]{:S(2)}) collective-permute-start(f32[8,512]{1,0:T(8,128)S(1)} %get-tuple-element.87.grx_ref_0_), channel_id=1, source_target_pairs={{0,2},{1,3},{2,0},{3,1},{4,6},{5,7},{6,4},{7,5},{8,10},{9,11},{10,... | collective-permute-start | bytes 49160 | tf_op jit(solution)/shard_map/ppermute | solution.py:726
  102.7 3.6 %all-to-all-start.2 = ((bf16[4,96,512]{2,1,0:T(8,128)(2,1)}), bf16[4,96,512]{2,1,0:T(8,128)(2,1)S(1)}, u32[]{:S(2)}, u32[]{:S(2)}) async-start(bf16[4,96,512]{2,1,0:T(8,128)(2,1)} %pad_maximum_fusion), calls=%async_computation.2 | async-start | bytes 786432 | tf_op jit(solution)/shard_map/all_to_all | solution.py:718
  106.4 1.7 %collective-permute-start.18 = (bf16[32,2176]{1,0:T(8,128)(2,1)S(1)}, bf16[32,2176]{1,0:T(8,128)(2,1)S(1)}, u32[]{:S(2)}, u32[]{:S(2)}) collective-permute-start(bf16[32,2176]{1,0:T(8,128)(2,1)S(1)} %maximum_select_fusion.2), channel_id=1, source_target_pairs={{0,8},{8,0},{16,24},{24,16},{1,9},{9,1},{17,25},{25,17},{2,10},{10... | collective-permute-start | bytes 417800 | tf_op jit(solution)/shard_map/ppermute | solution.py:726
  108.1 8.9 %shard_map.194 = bf16[4,512,512]{2,1,0:T(8,128)(2,1)} custom-call(s32[4,3]{1,0:T(4,128)S(1)} %copy-done.2, bf16[4,544,512]{2,1,0:T(8,128)(2,1)} %get-tuple-element.66.low_hbm, bf16[4,512,512]{2,1,0:T(8,128)(2,1)} %tok_hbm.6, bf16[1536,512]{1,0:T(8,128)(2,1)} %bitcast.29, bf16[1,512]{1,0:T(2,128)(2,1)S(1)} %reshape.66.bias_ref), custom_call_target="tpu_custom_call" | custom-call | flops 3221225472 | bytes 8388608 | tf_op jit(solution)/shard_map/pallas_call | solution.py:698
  117.0 5.2 %shard_map.195 = bf16[4,512,512]{2,1,0:T(8,128)(2,1)} custom-call(s32[4,3]{1,0:T(4,128)S(1)} %copy-done.2, bf16[4,512,512]{2,1,0:T(8,128)(2,1)} %og_hbm.5, bf16[4,512,512]{2,1,0:T(8,128)(2,1)} %get-tuple-element.83.da_hbm, bf16[4,512,512]{2,1,0:T(8,128)(2,1)} %tok_hbm.6, f32[4,8,512]{2,1,0:T(8,128)S(1)} %get-tuple-element.54.st_ref, ...), custom_call_target="tpu_custom_call" | custom-call | bytes 8388608 | tf_op jit(solution)/shard_map/pallas_call | solution.py:698
  123.1 5.2 %all-to-all-start.3 = ((bf16[4,96,512]{2,1,0:T(8,128)(2,1)}), bf16[4,96,512]{2,1,0:T(8,128)(2,1)S(1)}, u32[]{:S(2)}, u32[]{:S(2)}) async-start(bf16[4,96,512]{2,1,0:T(8,128)(2,1)} %broadcast_in_dim.4), calls=%async_computation.3 | async-start | bytes 786432 | tf_op jit(solution)/shard_map/all_to_all | solution.py:722
  130.4 9.7 %all-to-all-done.3 = bf16[4,96,512]{2,1,0:T(8,128)(2,1)S(1)} async-done(((bf16[4,96,512]{2,1,0:T(8,128)(2,1)}), bf16[4,96,512]{2,1,0:T(8,128)(2,1)S(1)}, u32[]{:S(2)}, u32[]{:S(2)}) %all-to-all-start.3) | async-done | bytes 393248 | tf_op jit(solution)/shard_map/all_to_all | solution.py:722
  141.4 3.6 %all-to-all-start.4 = ((bf16[4,4,96,512]{3,2,1,0:T(8,128)(2,1)}), bf16[4,4,96,512]{3,2,1,0:T(8,128)(2,1)S(1)}, u32[]{:S(2)}, u32[]{:S(2)}) async-start(bf16[4,4,96,512]{3,2,1,0:T(8,128)(2,1)} %broadcast_in_dim.5), calls=%async_computation.4 | async-start | bytes 3145728 | tf_op jit(solution)/shard_map/all_to_all | solution.py:722
  149.1 14.5 %all-to-all-done.4 = bf16[4,4,96,512]{3,2,1,0:T(8,128)(2,1)S(1)} async-done(((bf16[4,4,96,512]{3,2,1,0:T(8,128)(2,1)}), bf16[4,4,96,512]{3,2,1,0:T(8,128)(2,1)S(1)}, u32[]{:S(2)}, u32[]{:S(2)}) %all-to-all-start.4) | async-done | bytes 1572896 | tf_op jit(solution)/shard_map/all_to_all | solution.py:722
  165.4 2.3 %fusion.10 = (f32[128,1024]{1,0:T(8,128)}, f32[128,1024]{1,0:T(8,128)}) fusion(f32[128,2048]{1,0:T(8,128)} %fusion), kind=kLoop, calls=%fused_computation.23 | loop fusion | bytes 2097152 | tf_op jit(solution)/shard_map/slice | solution.py:858
  167.7 2.9 %shard_map.196 = (f32[3,512,512]{2,1,0:T(8,128)}, f32[3,512,512]{2,1,0:T(8,128)}) custom-call(bf16[4,4,2,48,512]{4,3,2,1,0:T(8,128)(2,1)S(1)} %bitcast.19, bf16[4,4,2,48,512]{4,3,2,1,0:T(8,128)(2,1)S(1)} %collective-permute-done.20.other_ref), custom_call_target="tpu_custom_call" | custom-call | bytes 8388608 | tf_op jit(solution)/shard_map/pallas_call | solution.py:698
  (85 shorter events, 19.2 us)
Async XLA Ops:
  0.6 10.4 %copy-start = (bf16[128,1024]{1,0:T(8,128)(2,1)S(1)}, bf16[128,1024]{1,0:T(8,128)(2,1)}, u32[]{:S(2)}) copy-start(bf16[128,1024]{1,0:T(8,128)(2,1)} %param.14) | copy-start | bytes 786436
  1.4 9.7 %copy-start.8 = (bf16[1024]{0:T(1024)(128)(2,1)S(1)}, bf16[1024]{0:T(1024)(128)(2,1)}, u32[]{:S(2)}) copy-start(bf16[1024]{0:T(1024)(128)(2,1)} %param.18) | copy-start | bytes 6148
  1.4 9.7 %copy-start.6 = (bf16[4,3,128]{2,0,1:T(4,128)(2,1)S(1)}, bf16[4,3,128]{2,0,1:T(4,128)(2,1)}, u32[]{:S(2)}) copy-start(bf16[4,3,128]{2,0,1:T(4,128)(2,1)} %param.13) | copy-start | bytes 9220
  1.4 9.9 %copy-start.3 = (bf16[128,1024]{1,0:T(8,128)(2,1)S(1)}, bf16[128,1024]{1,0:T(8,128)(2,1)}, u32[]{:S(2)}) copy-start(bf16[128,1024]{1,0:T(8,128)(2,1)} %param.17) | copy-start | bytes 786436
  5.0 6.5 %collective-permute-start = (f32[24,512]{1,0:T(8,128)S(1)}, f32[24,512]{1,0:T(8,128)S(1)}, u32[]{:S(2)}, u32[]{:S(2)}) collective-permute-start(f32[24,512]{1,0:T(8,128)S(1)} %get-tuple-element.56), channel_id=1, source_target_pairs={{0,1},{1,0},{2,3},{3,2},{4,5},{5,4},{6,7},{7,6},{8,9},{9,8},{10,11... | collective-permute-start | bytes 147464 | tf_op jit(solution)/shard_map/ppermute | solution.py:726
  7.9 6.1 %collective-permute-start.1 = (f32[24,512]{1,0:T(8,128)S(1)}, f32[24,512]{1,0:T(8,128)S(1)}, u32[]{:S(2)}, u32[]{:S(2)}) collective-permute-start(f32[24,512]{1,0:T(8,128)S(1)} %get-tuple-element.57), channel_id=1, source_target_pairs={{0,2},{1,3},{2,0},{3,1},{4,6},{5,7},{6,4},{7,5},{8,10},{9,11},{10,... | collective-permute-start | bytes 147464 | tf_op jit(solution)/shard_map/ppermute | solution.py:726
  11.1 5.9 %collective-permute-start.2 = (f32[24,512]{1,0:T(8,128)S(1)}, f32[24,512]{1,0:T(8,128)S(1)}, u32[]{:S(2)}, u32[]{:S(2)}) collective-permute-start(f32[24,512]{1,0:T(8,128)S(1)} %get-tuple-element.58), channel_id=1, source_target_pairs={{0,3},{1,2},{2,1},{3,0},{4,7},{5,6},{6,5},{7,4},{8,11},{9,10},{10,... | collective-permute-start | bytes 147464 | tf_op jit(solution)/shard_map/ppermute | solution.py:726
  27.2 12.5 %collective-permute-start.3 = (f32[8,512]{1,0:T(8,128)S(1)}, f32[8,512]{1,0:T(8,128)S(1)}, u32[]{:S(2)}, u32[]{:S(2)}) collective-permute-start(f32[8,512]{1,0:T(8,128)S(1)} %get-tuple-element.65.rx_ref_0_), channel_id=1, source_target_pairs={{0,1},{1,0},{2,3},{3,2},{4,5},{5,4},{6,7},{7,6},{8,9},{9,8},{10,11... | collective-permute-start | bytes 49160 | tf_op jit(solution)/shard_map/ppermute | solution.py:726
  27.3 12.4 %collective-permute-start.4 = (f32[8,512]{1,0:T(8,128)S(1)}, f32[8,512]{1,0:T(8,128)S(1)}, u32[]{:S(2)}, u32[]{:S(2)}) collective-permute-start(f32[8,512]{1,0:T(8,128)S(1)} %get-tuple-element.65.rx_ref_0_), channel_id=1, source_target_pairs={{0,2},{1,3},{2,0},{3,1},{4,6},{5,7},{6,4},{7,5},{8,10},{9,11},{10,... | collective-permute-start | bytes 49160 | tf_op jit(solution)/shard_map/ppermute | solution.py:726
  29.2 10.6 %collective-permute-start.5 = (f32[8,512]{1,0:T(8,128)S(1)}, f32[8,512]{1,0:T(8,128)S(1)}, u32[]{:S(2)}, u32[]{:S(2)}) collective-permute-start(f32[8,512]{1,0:T(8,128)S(1)} %get-tuple-element.65.rx_ref_0_), channel_id=1, source_target_pairs={{0,3},{1,2},{2,1},{3,0},{4,7},{5,6},{6,5},{7,4},{8,11},{9,10},{10,... | collective-permute-start | bytes 49160 | tf_op jit(solution)/shard_map/ppermute | solution.py:726
  47.5 10.8 %collective-permute-start.6 = (bf16[768,512]{1,0:T(8,128)(2,1)S(1)}, bf16[768,512]{1,0:T(8,128)(2,1)S(1)}, u32[]{:S(2)}, u32[]{:S(2)}) collective-permute-start(bf16[768,512]{1,0:T(8,128)(2,1)S(1)} %shard_map.190), channel_id=1, source_target_pairs={{0,4},{4,0},{1,5},{5,1},{2,6},{6,2},{3,7},{7,3},{8,12},{12,8},{9,1... | collective-permute-start | bytes 2359304 | tf_op jit(solution)/shard_map/ppermute | solution.py:726
  47.5 4.5 %collective-permute-start.7 = (f32[8,512]{1,0:T(8,128)S(1)}, f32[8,512]{1,0:T(8,128)S(1)}, u32[]{:S(2)}, u32[]{:S(2)}) collective-permute-start(f32[8,512]{1,0:T(8,128)S(1)} %get-tuple-element.71.grx_ref_0_), channel_id=1, source_target_pairs={{0,1},{1,0},{2,3},{3,2},{4,5},{5,4},{6,7},{7,6},{8,9},{9,8},{10,11... | collective-permute-start | bytes 49160 | tf_op jit(solution)/shard_map/ppermute | solution.py:726
  47.6 4.7 %collective-permute-start.8 = (f32[8,512]{1,0:T(8,128)S(1)}, f32[8,512]{1,0:T(8,128)S(1)}, u32[]{:S(2)}, u32[]{:S(2)}) collective-permute-start(f32[8,512]{1,0:T(8,128)S(1)} %get-tuple-element.71.grx_ref_0_), channel_id=1, source_target_pairs={{0,2},{1,3},{2,0},{3,1},{4,6},{5,7},{6,4},{7,5},{8,10},{9,11},{10,... | collective-permute-start | bytes 49160 | tf_op jit(solution)/shard_map/ppermute | solution.py:726
  50.1 5.5 %collective-permute-start.9 = (f32[8,512]{1,0:T(8,128)S(1)}, f32[8,512]{1,0:T(8,128)S(1)}, u32[]{:S(2)}, u32[]{:S(2)}) collective-permute-start(f32[8,512]{1,0:T(8,128)S(1)} %get-tuple-element.71.grx_ref_0_), channel_id=1, source_target_pairs={{0,3},{1,2},{2,1},{3,0},{4,7},{5,6},{6,5},{7,4},{8,11},{9,10},{10,... | collective-permute-start | bytes 49160 | tf_op jit(solution)/shard_map/ppermute | solution.py:726
  59.3 13.4 %all-to-all-start = ((bf16[4,192,512]{2,1,0:T(8,128)(2,1)}), bf16[4,192,512]{2,1,0:T(8,128)(2,1)S(1)}, u32[]{:S(2)}, u32[]{:S(2)}) async-start(bf16[4,192,512]{2,1,0:T(8,128)(2,1)} %bitcast.4), calls=%async_computation | async-start | bytes 1572864 | tf_op jit(solution)/shard_map/all_to_all | solution.py:718
  73.6 2.3 %collective-permute-start.10 = (bf16[768,512]{1,0:T(8,128)(2,1)S(1)}, bf16[768,512]{1,0:T(8,128)(2,1)S(1)}, u32[]{:S(2)}, u32[]{:S(2)}) collective-permute-start(bf16[768,512]{1,0:T(8,128)(2,1)S(1)} %get-tuple-element.78), channel_id=1, source_target_pairs={{0,4},{4,0},{1,5},{5,1},{2,6},{6,2},{3,7},{7,3},{8,12},{12,8},{9,1... | collective-permute-start | bytes 2359304 | tf_op jit(solution)/shard_map/ppermute | solution.py:726
  76.9 15.1 %all-to-all-start.1 = ((bf16[4,192,512]{2,1,0:T(8,128)(2,1)}), bf16[4,192,512]{2,1,0:T(8,128)(2,1)S(1)}, u32[]{:S(2)}, u32[]{:S(2)}) async-start(bf16[4,192,512]{2,1,0:T(8,128)(2,1)} %bitcast.5), calls=%async_computation.1 | async-start | bytes 1572864 | tf_op jit(solution)/shard_map/all_to_all | solution.py:718
  80.9 15.7 %copy-start.9 = (bf16[512]{0:T(512)(128)(2,1)S(1)}, bf16[512]{0:T(512)(128)(2,1)}, u32[]{:S(2)}) copy-start(bf16[512]{0:T(512)(128)(2,1)} %param.20) | copy-start | bytes 3076
  91.8 10.0 %copy-start.5 = (bf16[192,512]{1,0:T(8,128)(2,1)S(1)}, bf16[192,512]{1,0:T(8,128)(2,1)}, u32[]{:S(2)}) copy-start(bf16[192,512]{1,0:T(8,128)(2,1)} %reduce_sum.54) | copy-start | bytes 589828
  92.2 7.9 %collective-permute-start.14 = (bf16[16,2048]{1,0:T(8,128)(2,1)S(1)}, bf16[16,2048]{1,0:T(8,128)(2,1)S(1)}, u32[]{:S(2)}, u32[]{:S(2)}) collective-permute-start(bf16[16,2048]{1,0:T(8,128)(2,1)S(1)} %get-tuple-element.89), channel_id=1, source_target_pairs={{0,2},{1,3},{2,0},{3,1},{4,6},{5,7},{6,4},{7,5},{8,10},{9,11},{10,... | collective-permute-start | bytes 196616 | tf_op jit(solution)/shard_map/ppermute | solution.py:726
  92.3 8.9 %collective-permute-start.15 = (bf16[16,2048]{1,0:T(8,128)(2,1)S(1)}, bf16[16,2048]{1,0:T(8,128)(2,1)S(1)}, u32[]{:S(2)}, u32[]{:S(2)}) collective-permute-start(bf16[16,2048]{1,0:T(8,128)(2,1)S(1)} %get-tuple-element.89), channel_id=1, source_target_pairs={{0,1},{1,0},{2,3},{3,2},{4,5},{5,4},{6,7},{7,6},{8,9},{9,8},{10,11... | collective-permute-start | bytes 196616 | tf_op jit(solution)/shard_map/ppermute | solution.py:726
  95.6 6.2 %collective-permute-start.16 = (bf16[16,2048]{1,0:T(8,128)(2,1)S(1)}, bf16[16,2048]{1,0:T(8,128)(2,1)S(1)}, u32[]{:S(2)}, u32[]{:S(2)}) collective-permute-start(bf16[16,2048]{1,0:T(8,128)(2,1)S(1)} %get-tuple-element.89), channel_id=1, source_target_pairs={{0,3},{1,2},{2,1},{3,0},{4,7},{5,6},{6,5},{7,4},{8,11},{9,10},{10,... | collective-permute-start | bytes 196616 | tf_op jit(solution)/shard_map/ppermute | solution.py:726
  96.7 20.3 %collective-permute-start.11 = (f32[8,512]{1,0:T(8,128)S(1)}, f32[8,512]{1,0:T(8,128)S(1)}, u32[]{:S(2)}, u32[]{:S(2)}) collective-permute-start(f32[8,512]{1,0:T(8,128)S(1)} %get-tuple-element.87.grx_ref_0_), channel_id=1, source_target_pairs={{0,1},{1,0},{2,3},{3,2},{4,5},{5,4},{6,7},{7,6},{8,9},{9,8},{10,11... | collective-permute-start | bytes 49160 | tf_op jit(solution)/shard_map/ppermute | solution.py:726
  96.7 20.2 %collective-permute-start.12 = (f32[8,512]{1,0:T(8,128)S(1)}, f32[8,512]{1,0:T(8,128)S(1)}, u32[]{:S(2)}, u32[]{:S(2)}) collective-permute-start(f32[8,512]{1,0:T(8,128)S(1)} %get-tuple-element.87.grx_ref_0_), channel_id=1, source_target_pairs={{0,2},{1,3},{2,0},{3,1},{4,6},{5,7},{6,4},{7,5},{8,10},{9,11},{10,... | collective-permute-start | bytes 49160 | tf_op jit(solution)/shard_map/ppermute | solution.py:726
  100.1 16.9 %collective-permute-start.13 = (f32[8,512]{1,0:T(8,128)S(1)}, f32[8,512]{1,0:T(8,128)S(1)}, u32[]{:S(2)}, u32[]{:S(2)}) collective-permute-start(f32[8,512]{1,0:T(8,128)S(1)} %get-tuple-element.87.grx_ref_0_), channel_id=1, source_target_pairs={{0,3},{1,2},{2,1},{3,0},{4,7},{5,6},{6,5},{7,4},{8,11},{9,10},{10,... | collective-permute-start | bytes 49160 | tf_op jit(solution)/shard_map/ppermute | solution.py:726
  101.8 4.5 %collective-permute-start.17 = (bf16[16,2176]{1,0:T(8,128)(2,1)S(1)}, bf16[16,2176]{1,0:T(8,128)(2,1)S(1)}, u32[]{:S(2)}, u32[]{:S(2)}) collective-permute-start(bf16[16,2176]{1,0:T(8,128)(2,1)S(1)} %pad_maximum_fusion.1), channel_id=1, source_target_pairs={{0,4},{4,0},{1,5},{5,1},{2,6},{6,2},{3,7},{7,3},{8,12},{12,8},{9,1... | collective-permute-start | bytes 208904 | tf_op jit(solution)/shard_map/ppermute | solution.py:726
  102.7 19.6 %all-to-all-start.2 = ((bf16[4,96,512]{2,1,0:T(8,128)(2,1)}), bf16[4,96,512]{2,1,0:T(8,128)(2,1)S(1)}, u32[]{:S(2)}, u32[]{:S(2)}) async-start(bf16[4,96,512]{2,1,0:T(8,128)(2,1)} %pad_maximum_fusion), calls=%async_computation.2 | async-start | bytes 786432 | tf_op jit(solution)/shard_map/all_to_all | solution.py:718
  106.4 22.0 %collective-permute-start.18 = (bf16[32,2176]{1,0:T(8,128)(2,1)S(1)}, bf16[32,2176]{1,0:T(8,128)(2,1)S(1)}, u32[]{:S(2)}, u32[]{:S(2)}) collective-permute-start(bf16[32,2176]{1,0:T(8,128)(2,1)S(1)} %maximum_select_fusion.2), channel_id=1, source_target_pairs={{0,8},{8,0},{16,24},{24,16},{1,9},{9,1},{17,25},{25,17},{2,10},{10... | collective-permute-start | bytes 417800 | tf_op jit(solution)/shard_map/ppermute | solution.py:726
  123.1 16.9 %all-to-all-start.3 = ((bf16[4,96,512]{2,1,0:T(8,128)(2,1)}), bf16[4,96,512]{2,1,0:T(8,128)(2,1)S(1)}, u32[]{:S(2)}, u32[]{:S(2)}) async-start(bf16[4,96,512]{2,1,0:T(8,128)(2,1)} %broadcast_in_dim.4), calls=%async_computation.3 | async-start | bytes 786432 | tf_op jit(solution)/shard_map/all_to_all | solution.py:722
  128.4 16.5 %collective-permute-start.19 = (bf16[64,2176]{1,0:T(8,128)(2,1)S(1)}, bf16[64,2176]{1,0:T(8,128)(2,1)S(1)}, u32[]{:S(2)}, u32[]{:S(2)}) collective-permute-start(bf16[64,2176]{1,0:T(8,128)(2,1)S(1)} %maximum_select_fusion.1), channel_id=1, source_target_pairs={{0,16},{8,24},{16,0},{24,8},{1,17},{9,25},{17,1},{25,9},{2,18},{10... | collective-permute-start | bytes 835592 | tf_op jit(solution)/shard_map/ppermute | solution.py:726
  141.4 22.3 %all-to-all-start.4 = ((bf16[4,4,96,512]{3,2,1,0:T(8,128)(2,1)}), bf16[4,4,96,512]{3,2,1,0:T(8,128)(2,1)S(1)}, u32[]{:S(2)}, u32[]{:S(2)}) async-start(bf16[4,4,96,512]{3,2,1,0:T(8,128)(2,1)} %broadcast_in_dim.5), calls=%async_computation.4 | async-start | bytes 3145728 | tf_op jit(solution)/shard_map/all_to_all | solution.py:722
  163.7 4.1 %collective-permute-start.20 = (bf16[4,4,2,48,512]{4,3,2,1,0:T(8,128)(2,1)S(1)}, bf16[4,4,2,48,512]{4,3,2,1,0:T(8,128)(2,1)S(1)}, u32[]{:S(2)}, u32[]{:S(2)}) collective-permute-start(bf16[4,4,2,48,512]{4,3,2,1,0:T(8,128)(2,1)S(1)} %bitcast.18), channel_id=1, source_target_pairs={{0,4},{4,0},{1,5},{5,1},{2,6},{6,2},{3,7},{7,3},{8,12},{12,8},{9,1... | collective-permute-start | bytes 4718600 | tf_op jit(solution)/shard_map/ppermute | solution.py:726
  (4 other events, 23.0 us)

commit v2 on v1

--- a/solution.py
+++ b/solution.py
@@ -11,7 +11,7 @@
 ROOT_HALF = 0.7071067811865476
 SEGS = 3
 PAD = 16
-CHUNK = 64
+CHUNK = 32
 EDGE = 8 + 16
 F32 = jnp.float32
 BF16 = jnp.bfloat16
@@ -42,23 +42,19 @@
     def segment(self, t):
         return sum((t >= e).astype(jnp.int32) for e in self.ends)
 
-    def chunks(self, uniform_fn, mixed_fn):
-        def body(i, carry):
-            t0 = pl.multiple_of(i * CHUNK, CHUNK)
-            first, last = self.segment(t0), self.segment(t0 + CHUNK - 1)
-            uniform = jnp.logical_and(first == last, first < SEGS)
-
-            @pl.when(uniform)
-            def _():
-                uniform_fn(t0, first)
-
-            @pl.when(jnp.logical_not(uniform))
-            def _():
-                mixed_fn(t0)
-
-            return carry
-
-        lax.fori_loop(0, self.frames // CHUNK, body, 0)
+    def chunks(self, uniform_fn, mixed_fn, sums=None, acc_ref=None, ends=None):
+        for t0 in range(0, self.frames, CHUNK):
+            uniform_fn(t0, self.segment(t0))
+        if sums is not None:
+            sums.put(acc_ref)
+        self.mixed(mixed_fn, ends)
+
+    def mixed(self, fn, ends=None):
+        for end in ends or self.ends:
+
+            @pl.when(jnp.logical_and(jnp.logical_and(end > 0, end < self.frames), end % CHUNK != 0))
+            def _(end=end):
+                fn(pl.multiple_of((end // CHUNK) * CHUNK, CHUNK))
 
 
 def frame_ids(t0, rows, width):
@@ -66,27 +62,36 @@
 
 
 def pick(tab_ref, base, t, row):
-    value = jnp.where(t >= row.ends[0], tab_ref[base + 1 : base + 2, :], tab_ref[base : base + 1, :])
-    return jnp.where(t >= row.ends[1], tab_ref[base + 2 : base + 3, :], value)
-
-
-def row_of(tab_ref, base, s):
-    return tab_ref[pl.ds(base + s, 1), :]
+    value = tab_ref[base, 0:1, :]
+    for s in range(SEGS):
+        value = jnp.where(t >= row.ends[s], tab_ref[base + s + 1, 0:1, :], value)
+    return value
+
+
+def entry(tab_ref, index, rows=CHUNK):
+    value = tab_ref[index]
+    return jnp.broadcast_to(value[None], (rows // 8, *value.shape)).reshape(rows, value.shape[1])
+
+
+def put_entry(tab_ref, index, value):
+    tab_ref[index] = jnp.broadcast_to(value, tab_ref.shape[1:])
+
+
+def put_table(tab_ref, base, values):
+    for s in range(SEGS):
+        put_entry(tab_ref, base + s, values[s])
+    put_entry(tab_ref, base + SEGS, jnp.zeros_like(values[0]))
 
 
 def fold(x):
     return jnp.sum(x.reshape(x.shape[0] // 8, 8, x.shape[1]), axis=0)
-
-
-def add_sums(acc_ref, s, first, second):
-    acc_ref[s] += fold(first)
-    acc_ref[4 + s] += fold(second)
 
 
 def add_masked_sums(acc_ref, t, row, first, second):
     for s in range(SEGS):
         inside = jnp.logical_and(t >= row.begins[s], t < row.ends[s])
-        add_sums(acc_ref, s, jnp.where(inside, first, 0.0), jnp.where(inside, second, 0.0))
+        acc_ref[s] += fold(jnp.where(inside, first, 0.0))
+        acc_ref[4 + s] += fold(jnp.where(inside, second, 0.0))
 
 
 def put_sums(acc_ref, st_ref, msg_refs, row, r):
@@ -124,27 +129,33 @@
         mean, rstd, gain, beta, _ = norm_of(row, r, st_ref, rx_ref, aff_ref, s)
         scales.append(gain * rstd)
         shifts.append(beta - mean * scales[-1])
-        tab_ref[s : s + 1, :] = scales[s]
-        tab_ref[SEGS + s : SEGS + s + 1, :] = shifts[s]
-    tab_ref[6:7, :] = row.of_long(scales)
-    tab_ref[7:8, :] = row.of_long(shifts)
+    put_table(tab_ref, 0, scales)
+    put_table(tab_ref, 4, shifts)
+    put_entry(tab_ref, 12, row.of_long(scales))
+    put_entry(tab_ref, 13, row.of_long(shifts))
 
 
 def put_backward(row, r, st_ref, rx_ref, gst_ref, grx_ref, aff_ref, tab_ref):
     parts = [[], [], []]
     for s in range(SEGS):
         mean, rstd, gain, _, count = norm_of(row, r, st_ref, rx_ref, aff_ref, s)
-        shift, scale = sums_of(row, r, gst_ref, grx_ref, s)
-        scale = rstd * (scale - mean * shift)
+        if isinstance(grx_ref, (list, tuple)):
+            shift, scale = sums_of(row, r, gst_ref, grx_ref, s)
+            scale = rstd * (scale - mean * shift)
+        else:
+            width = mean.shape[1]
+            total = grx_ref[pl.ds(4 * r + s, 1), : 2 * width] + grx_ref[pl.ds(4 * r + SEGS, 1), 2 * width :]
+            shift, local = gst_ref[r, s : s + 1, :], gst_ref[r, SEGS + s : SEGS + s + 1, :]
+            scale = jnp.where(row.long_at == s, total[:, :width], rstd * (local - mean * shift))
+            shift = jnp.where(row.long_at == s, total[:, width:], shift)
         mean_g = gain * shift / count
         slope = rstd * rstd * (gain * scale / count)
         parts[0].append(gain * rstd)
         parts[1].append(-slope)
         parts[2].append(slope * mean - rstd * mean_g)
     for k in range(3):
-        for s in range(SEGS):
-            tab_ref[SEGS * k + s : SEGS * k + s + 1, :] = parts[k][s]
-        tab_ref[9 + k : 10 + k, :] = row.of_long(parts[k])
+        put_table(tab_ref, 4 * k, parts[k])
+        put_entry(tab_ref, 12 + k, row.of_long(parts[k]))
 
 
 def put_affine_grads(row, r, st_ref, rx_ref, gst_ref, aff_ref, out_ref, at):
@@ -222,6 +233,48 @@
                 xs_ref[rows, at : at + width] = jnp.where(keep, value, 0.0).astype(BF16)
 
 
+class Sums:
+    def __init__(self, row, width):
+        self.row = row
+        self.parts = [[jnp.zeros((8, width), F32)] * SEGS for _ in range(2)]
+
+    def add(self, t0, rows, first, second):
+        folded = (fold(first), fold(second))
+        for s in range(SEGS):
+            fills = jnp.logical_and(t0 >= self.row.begins[s], t0 + rows <= self.row.ends[s])
+            weight = jnp.where(fills, 1.0, 0.0)
+            for k in range(2):
+                self.parts[k][s] = self.parts[k][s] + folded[k] * weight
+
+    def put(self, acc_ref):
+        for k in range(2):
+            for s in range(SEGS):
+                acc_ref[4 * k + s] = self.parts[k][s]
+
+
+def rows_moved(ref, at, rows, step):
+    if at - step < 0 or at + rows - step > ref.shape[0]:
+        return pltpu.roll(ref[at : at + rows, :], step % rows, 0)
+    return ref[at - step : at - step + rows, :]
+
+
+def tap_sum(z_ref, row, t0, rows, first=0, last=2):
+    at, t = PAD + t0, frame_ids(t0, rows, z_ref.shape[2])
+    starts = functools.reduce(jnp.logical_or, [t == end for end in row.ends])
+    stops = functools.reduce(jnp.logical_or, [t == end - 1 for end in row.ends])
+    before = jnp.where(starts, 0.0, rows_moved(z_ref.at[first], at, rows, 1))
+    after = jnp.where(stops, 0.0, rows_moved(z_ref.at[last], at, rows, -1))
+    return before + z_ref[1, at : at + rows, :] + after
+
+
+def put_products(x, w_ref, z_ref, transposed=False):
+    width = x.shape[1]
+    dims = (((1,), (1 if transposed else 0,)), ((), ()))
+    for k in range(3):
+        tap = w_ref[k * width : (k + 1) * width, :]
+        z_ref[k] = lax.dot_general(x, tap, dims, preferred_element_type=F32)
+
+
 def times_transposed(xs, w_ref, width):
     out = None
     for k in range(3):
@@ -265,17 +318,17 @@
 
     def body(r, row):
         row_copy(r).wait()
-        acc_ref[...] = jnp.zeros_like(acc_ref)
+        sums = Sums(row, width)
 
         def uniform(t0, s):
             v = tok_ref[r, pl.ds(t0, CHUNK), :].astype(F32)
-            add_sums(acc_ref, s, v, v * v)
+            sums.add(t0, CHUNK, v, v * v)
 
         def mixed(t0):
             v = tok_ref[r, pl.ds(t0, CHUNK), :].astype(F32)
             add_masked_sums(acc_ref, frame_ids(t0, CHUNK, width), row, v, v * v)
 
-        row.chunks(uniform, mixed)
+        row.chunks(uniform, mixed, sums, acc_ref)
         put_sums(acc_ref, st_ref, msg_refs, row, r)
         for j, (head, tail) in enumerate(
             ((tok_ref[r, 0:PAD, :], tok_ref[r, frames - PAD : frames, :]), (head_ref[r], tail_ref[r]))
@@ -291,17 +344,9 @@
     kernel_copy.wait()
 
 
-def first_half_kernel(len_ref, tok_ref, st_ref, rx_ref, aff_ref, w_ref, og_hbm, w2_hbm, low_hbm, hid_hbm,
-                      hid_ref, st2_ref, msg_ref, og_ref, w2_ref, low_ref, buf_ref, xs_ref, tab_ref, acc_ref,
-                      sems, row_sems):
+def first_half_kernel(len_ref, tok_ref, st_ref, rx_ref, aff_ref, w_ref, og_hbm, w2_hbm, low_ref,
+                      hid_ref, st2_ref, msg_ref, og_ref, w2_ref, z_ref, tab_ref, acc_ref, sems):
     rows, frames, width = tok_ref.shape
-
-    def row_copies(r):
-        return (
-            pltpu.make_async_copy(low_ref.at[r], low_hbm.at[r], row_sems.at[r]),
-            pltpu.make_async_copy(hid_ref.at[r], hid_hbm.at[r], row_sems.at[rows + r]),
-        )
-
     copies = (
         pltpu.make_async_copy(og_hbm, og_ref, sems.at[0]),
         pltpu.make_async_copy(w2_hbm, w2_ref, sems.at[1]),
@@ -314,64 +359,71 @@
 
         def uniform(t0, s):
             v = tok_ref[r, pl.ds(t0, CHUNK), :].astype(F32)
-            buf_ref[pl.ds(PAD + t0, CHUNK), :] = silu(v * row_of(tab_ref, 0, s) + row_of(tab_ref, SEGS, s))
+            low = silu(v * entry(tab_ref, s) + entry(tab_ref, 4 + s))
+            low_ref[r, pl.ds(PAD + t0, CHUNK), :] = low.astype(BF16)
 
         def mixed(t0):
             t = frame_ids(t0, CHUNK, width)
             v = tok_ref[r, pl.ds(t0, CHUNK), :].astype(F32)
-            low = silu(v * pick(tab_ref, 0, t, row) + pick(tab_ref, SEGS, t, row))
-            buf_ref[pl.ds(PAD + t0, CHUNK), :] = jnp.where(t < row.ends[2], low, 0.0)
+            low = silu(v * pick(tab_ref, 0, t, row) + pick(tab_ref, 4, t, row))
+            low_ref[r, pl.ds(PAD + t0, CHUNK), :] = jnp.where(t < row.ends[2], low, 0.0).astype(BF16)
 
         row.chunks(uniform, mixed)
         for left in (True, False):
             t, valid = halo_tile(row, frames, width, left)
-            low = silu(edge_tile(rx_ref, row, r, t, 0, left) * tab_ref[6:7, :] + tab_ref[7:8, :])
+            low = silu(edge_tile(rx_ref, row, r, t, 0, left) * tab_ref[12, 0:1, :] + tab_ref[13, 0:1, :])
             at = 0 if left else PAD + frames
-            buf_ref[at : at + PAD, :] = jnp.where(valid, low, 0.0)
-        stack_taps(buf_ref, xs_ref, row, frames, True, True, low_ref, r)
-        hid_ref[r] = jnp.dot(xs_ref[...], w_ref[...], preferred_element_type=F32)
-        for copy in row_copies(r):
-            copy.start()
-
-        acc_ref[...] = jnp.zeros_like(acc_ref)
-
-        def uniform_sums(t0, s):
-            v = hid_ref[r, pl.ds(PAD + t0, CHUNK), :]
-            add_sums(acc_ref, s, v, v * v)
+            low_ref[r, at : at + PAD, :] = jnp.where(valid, low, 0.0).astype(BF16)
+        put_products(low_ref[r], w_ref, z_ref)
+        sums = Sums(row, width)
+        for t0 in range(0, frames, CHUNK):
+            v = tap_sum(z_ref, row, t0, CHUNK)
+            hid_ref[r, PAD + t0 : PAD + t0 + CHUNK, :] = v
+            sums.add(t0, CHUNK, v, v * v)
+        sums.put(acc_ref)
+        for t0 in (-PAD, frames):
+            hid_ref[r, PAD + t0 : 2 * PAD + t0, :] = tap_sum(z_ref, row, t0, PAD)
 
         def mixed_sums(t0):
             v = hid_ref[r, pl.ds(PAD + t0, CHUNK), :]
             add_masked_sums(acc_ref, frame_ids(t0, CHUNK, width), row, v, v * v)
 
-        row.chunks(uniform_sums, mixed_sums)
+        row.mixed(mixed_sums)
         put_sums(acc_ref, st2_ref, [msg_ref], row, r)
 
     for_rows(len_ref, rows, frames, body)
-    for r in range(rows):
-        copies += row_copies(r)
     for copy in copies:
         copy.wait()
 
 
-def branch_grad_kernel(len_ref, og_ref, rx_ref, w_ref, gs_ref, q_ref, bias_ref, buf_ref, xs_ref):
+def branch_grad_kernel(len_ref, og_ref, rx_ref, w_ref, low_ref, hid_ref, gs_ref, q_ref, bias_ref, low_hbm, hid_hbm,
+                       buf_ref, xs_ref, sems):
     rows, frames, width = og_ref.shape
+    stores = (
+        pltpu.make_async_copy(low_ref, low_hbm, sems.at[0]),
+        pltpu.make_async_copy(hid_ref, hid_hbm, sems.at[1]),
+    )
+    for copy in stores:
+        copy.start()
     bias_ref[...] = jnp.zeros_like(bias_ref)
 
     def body(r, row):
-        def put(t0, g):
+        def put(t0, g, weight):
             g = g.astype(BF16).astype(F32)
             buf_ref[pl.ds(PAD + t0, CHUNK), :] = g
-            bias_ref[...] += fold(g)
+            bias_ref[...] += fold(g) * weight
 
         def uniform(t0, s):
-            put(t0, og_ref[r, pl.ds(t0, CHUNK), :].astype(F32) * ROOT_HALF)
+            scale = jnp.where(s < SEGS, ROOT_HALF, 0.0)
+            g = og_ref[r, pl.ds(t0, CHUNK), :].astype(F32) * scale
+            put(t0, g, jnp.where(t0 + CHUNK <= row.ends[2], 1.0, 0.0))
 
         def mixed(t0):
             t = frame_ids(t0, CHUNK, width)
             g = og_ref[r, pl.ds(t0, CHUNK), :].astype(F32) * ROOT_HALF
-            put(t0, jnp.where(t < row.ends[2], g, 0.0))
-
-        row.chunks(uniform, mixed)
+            put(t0, jnp.where(t < row.ends[2], g, 0.0), 1.0)
+
+        row.chunks(uniform, mixed, ends=row.ends[2:])
         for left in (True, False):
             t, valid = halo_tile(row, frames, width, left)
             at = 0 if left else PAD + frames
@@ -382,60 +434,51 @@
         q_ref[r] = times_transposed(xs_ref[...], w_ref, width).astype(BF16)
 
     for_rows(len_ref, rows, frames, body)
-
-
-def second_norm_kernel(len_ref, hid_ref, q_ref, st_ref, rx_ref, aff_ref, low_ref, low_hbm, da_hbm, gst_ref, msg_ref,
-                       da_ref, tab_ref, acc_ref, row_sems):
+    for copy in stores:
+        copy.wait()
+
+
+def second_norm_kernel(len_ref, hid_ref, q_ref, st_ref, rx_ref, aff_ref, low_ref, da_ref, gst_ref, msg_ref,
+                       tab_ref, acc_ref):
     rows, padded, width = hid_ref.shape
     frames = padded - 2 * PAD
 
-    def row_copies(r):
-        return (
-            pltpu.make_async_copy(low_ref.at[r], low_hbm.at[r], row_sems.at[r]),
-            pltpu.make_async_copy(da_ref.at[r], da_hbm.at[r], row_sems.at[rows + r]),
-        )
-
     def body(r, row):
         put_forward(row, r, st_ref, rx_ref, aff_ref, tab_ref)
-        acc_ref[...] = jnp.zeros_like(acc_ref)
+        sums = Sums(row, width)
 
         def uniform(t0, s):
             at = pl.ds(PAD + t0, CHUNK)
             v = hid_ref[r, at, :]
-            low, slope = silu_and_slope(v * row_of(tab_ref, 0, s) + row_of(tab_ref, SEGS, s))
+            low, slope = silu_and_slope(v * entry(tab_ref, s) + entry(tab_ref, 4 + s))
             da = slope * q_ref[r, at, :].astype(F32)
             low_ref[r, at, :] = low.astype(BF16)
             da_ref[r, at, :] = da.astype(BF16)
-            add_sums(acc_ref, s, da, da * v)
+            sums.add(t0, CHUNK, da, da * v)
 
         def mixed(t0):
             at = pl.ds(PAD + t0, CHUNK)
             t = frame_ids(t0, CHUNK, width)
             live = t < row.ends[2]
             v = hid_ref[r, at, :]
-            low, slope = silu_and_slope(v * pick(tab_ref, 0, t, row) + pick(tab_ref, SEGS, t, row))
+            low, slope = silu_and_slope(v * pick(tab_ref, 0, t, row) + pick(tab_ref, 4, t, row))
             da = slope * q_ref[r, at, :].astype(F32)
             low_ref[r, at, :] = jnp.where(live, low, 0.0).astype(BF16)
             da_ref[r, at, :] = jnp.where(live, da, 0.0).astype(BF16)
             add_masked_sums(acc_ref, t, row, da, da * v)
 
-        row.chunks(uniform, mixed)
+        row.chunks(uniform, mixed, sums, acc_ref)
         for left in (True, False):
             t, valid = halo_tile(row, frames, width, left)
             at = 0 if left else PAD + frames
             v = hid_ref[r, at : at + PAD, :]
-            low, slope = silu_and_slope(v * tab_ref[6:7, :] + tab_ref[7:8, :])
+            low, slope = silu_and_slope(v * tab_ref[12, 0:1, :] + tab_ref[13, 0:1, :])
             da = slope * q_ref[r, at : at + PAD, :].astype(F32)
             low_ref[r, at : at + PAD, :] = jnp.where(valid, low, 0.0).astype(BF16)
             da_ref[r, at : at + PAD, :] = jnp.where(valid, da, 0.0).astype(BF16)
-        for copy in row_copies(r):
-            copy.start()
         put_sums(acc_ref, gst_ref, [msg_ref], row, r)
 
     for_rows(len_ref, rows, frames, body)
-    for r in range(rows):
-        for copy in row_copies(r):
-            copy.wait()
 
 
 class Loads:
@@ -445,12 +488,11 @@
         self.row = lambda r: [
             pltpu.make_async_copy(a.at[r], b.at[r], sems.at[count + i * rows + r]) for i, (a, b) in enumerate(by_row)
         ]
-        for r in range(rows):
+        for copy in (*self.row(0), *self.whole):
+            copy.start()
+        for r in range(1, rows):
             for copy in self.row(r):
                 copy.start()
-            if r == 0:
-                for copy in self.whole:
-                    copy.start()
 
     def wait(self, r):
         for copy in self.row(r):
@@ -462,8 +504,8 @@
                 copy.wait()
 
 
-def block_out_kernel(len_ref, low_hbm, tok_hbm, w_hbm, bias_ref, out_hbm, low_ref, tok_ref, w_ref, buf_ref, xs_ref,
-                     out_ref, sems, row_sems):
+def block_out_kernel(len_ref, low_hbm, tok_hbm, w_hbm, bias_ref, out_hbm, low_ref, tok_ref, w_ref, z_ref, out_ref,
+                     sems, row_sems):
     rows, frames, width = tok_ref.shape
     loads = Loads(rows, sems, [(w_hbm, w_ref)], [(low_hbm, low_ref), (tok_hbm, tok_ref)])
 
@@ -472,12 +514,13 @@
 
     def body(r, row):
         loads.wait(r)
-        buf_ref[...] = low_ref[r].astype(F32)
-        stack_taps(buf_ref, xs_ref, row, frames, True, False)
-        branch = jnp.dot(xs_ref[...], w_ref[...], preferred_element_type=F32) + bias_ref[...].astype(F32)
-        live = frame_ids(0, frames, width) < row.ends[2]
-        out = (tok_ref[r].astype(F32) + jnp.where(live, branch, 0.0)) * ROOT_HALF
-        out_ref[r] = out.astype(BF16)
+        bias = bias_ref[...].astype(F32)
+        put_products(low_ref[r], w_ref, z_ref)
+        for t0 in range(0, frames, CHUNK):
+            live = frame_ids(t0, CHUNK, width) < row.ends[2]
+            branch = tap_sum(z_ref, row, t0, CHUNK) + jnp.where(live, bias, 0.0)
+            out = (tok_ref[r, t0 : t0 + CHUNK, :].astype(F32) + branch) * ROOT_HALF
+            out_ref[r, t0 : t0 + CHUNK, :] = out.astype(BF16)
         row_copy(r).start()
 
     for_rows(len_ref, rows, frames, body)
@@ -497,7 +540,9 @@
         out_ref[k * half : (k + 1) * half, :] = acc_ref[:, k * width : (k + 1) * width].astype(BF16)
 
 
-def kernel_grad_kernel(own, first_frame, low_ref, gs_ref, out_ref, acc_ref):
+def kernel_grad_kernel(own, first_frame, low_ref, gs_ref, kept_ref, out_ref, kept_hbm, acc_ref, sems):
+    store = pltpu.make_async_copy(kept_ref, kept_hbm, sems.at[0])
+    store.start()
     core = lax.axis_index("core")
     half = core if own else 1 - core
     acc_ref[...] = half_of_grad(low_ref, gs_ref, 0, half, first_frame)
@@ -508,18 +553,19 @@
 
     lax.fori_loop(1, low_ref.shape[0], step, 0)
     put_half(acc_ref, out_ref)
+    store.wait()
 
 
 def hidden_grad_kernel(len_ref, low_hbm, da_hbm, hid_hbm, st_ref, rx_ref, gst_ref, grx_ref, aff_ref,
-                       gs_hbm, send_ref, keep_ref, part_ref, low_ref, da_ref, hid_ref, gs_ref, buf_ref, tab_ref, acc_ref,
+                       g_hbm, send_ref, keep_ref, part_ref, low_ref, da_ref, hid_ref, g_ref, gs_ref, buf_ref, tab_ref, acc_ref,
                        sems, row_sems):
-    rows, frames, width = low_ref.shape
+    rows, frames, width = low_ref.shape[0], gs_ref.shape[0], low_ref.shape[2]
     loads = Loads(rows, sems, [], [(da_hbm, da_ref), (hid_hbm, hid_ref), (low_hbm, low_ref)])
     part_ref[...] = jnp.zeros_like(part_ref)
     acc_ref[...] = jnp.zeros_like(acc_ref)
 
     def row_copy(r):
-        return pltpu.make_async_copy(gs_ref.at[r], gs_hbm.at[r], row_sems.at[r])
+        return pltpu.make_async_copy(g_ref.at[r], g_hbm.at[r], row_sems.at[r])
 
     def body(r, row):
         put_affine_grads(row, r, st_ref, rx_ref, gst_ref, aff_ref, part_ref, 0)
@@ -529,9 +575,9 @@
         def uniform(t0, s):
             at = pl.ds(PAD + t0, CHUNK)
             buf_ref[at, :] = (
-                da_ref[r, at, :].astype(F32) * row_of(tab_ref, 0, s)
-                + hid_ref[r, at, :] * row_of(tab_ref, SEGS, s)
-                + row_of(tab_ref, 2 * SEGS, s)
+                da_ref[r, at, :].astype(F32) * entry(tab_ref, s)
+                + hid_ref[r, at, :] * entry(tab_ref, 4 + s)
+                + entry(tab_ref, 8 + s)
             )
 
         def mixed(t0):
@@ -539,8 +585,8 @@
             t = frame_ids(t0, CHUNK, width)
             grad = (
                 da_ref[r, at, :].astype(F32) * pick(tab_ref, 0, t, row)
-                + hid_ref[r, at, :] * pick(tab_ref, SEGS, t, row)
-                + pick(tab_ref, 2 * SEGS, t, row)
+                + hid_ref[r, at, :] * pick(tab_ref, 4, t, row)
+                + pick(tab_ref, 8, t, row)
             )
             buf_ref[at, :] = jnp.where(t < row.ends[2], grad, 0.0)
 
@@ -549,15 +595,16 @@
             t, valid = halo_tile(row, frames, width, left)
             at = 0 if left else PAD + frames
             grad = (
-                da_ref[r, at : at + PAD, :].astype(F32) * tab_ref[9:10, :]
-                + hid_ref[r, at : at + PAD, :] * tab_ref[10:11, :]
-                + tab_ref[11:12, :]
+                da_ref[r, at : at + PAD, :].astype(F32) * tab_ref[12, 0:1, :]
+                + hid_ref[r, at : at + PAD, :] * tab_ref[13, 0:1, :]
+                + tab_ref[14, 0:1, :]
             )
             buf_ref[at : at + PAD, :] = jnp.where(valid, grad, 0.0)
-        stack_taps(buf_ref, gs_ref.at[r], row, frames, False, False)
+        g_ref[r] = buf_ref[...].astype(BF16)
+        stack_taps(buf_ref, gs_ref, row, frames, False, False)
         row_copy(r).start()
         acc_ref[...] += lax.dot_general(
-            low_ref[r], gs_ref[r], (((0,), (0,)), ((), ())), preferred_element_type=F32
+            low_ref[r, PAD : PAD + frames, :], gs_ref[...], (((0,), (0,)), ((), ())), preferred_element_type=F32
         )
 
     for_rows(len_ref, rows, frames, body)
@@ -568,11 +615,11 @@
         row_copy(r).wait()
 
 
-def first_norm_grad_kernel(len_ref, gs_hbm, w_hbm, tok_hbm, st_ref, rx_ref, aff_ref, part2_ref, bias_ref,
-                           da_hbm, gst_ref, msg_ref, out_ref, gs_ref, w_ref, tok_ref, da_ref, q_ref, tab_ref, acc_ref,
+def first_norm_grad_kernel(len_ref, g_hbm, w_hbm, tok_hbm, st_ref, rx_ref, aff_ref, part2_ref, bias_ref,
+                           da_hbm, gst_ref, out_ref, g_ref, w_ref, tok_ref, da_ref, q_ref, z_ref, tab_ref, acc_ref,
                            part_ref, sems, row_sems):
     rows, frames, width = tok_ref.shape
-    loads = Loads(rows, sems, [(w_hbm, w_ref)], [(gs_hbm, gs_ref), (tok_hbm, tok_ref)])
+    loads = Loads(rows, sems, [(w_hbm, w_ref)], [(g_hbm, g_ref), (tok_hbm, tok_ref)])
     part_ref[:, : 2 * width] = jnp.zeros((part_ref.shape[0], 2 * width), F32)
     part_ref[:, 2 * width :] = part2_ref[...]
     part_ref[SEGS : SEGS + 1, :width] = jnp.sum(bias_ref[...], axis=0, keepdims=True)
@@ -583,30 +630,34 @@
     def body(r, row):
         put_forward(row, r, st_ref, rx_ref, aff_ref, tab_ref)
         loads.wait(r)
-        q_ref[...] = times_transposed(gs_ref[r], w_ref, width)
-        acc_ref[...] = jnp.zeros_like(acc_ref)
+        put_products(g_ref[r], w_ref, z_ref, True)
+        for t0 in range(0, frames, CHUNK):
+            q_ref[t0 : t0 + CHUNK, :] = tap_sum(z_ref, row, t0, CHUNK, 2, 0)
+        sums = Sums(row, width)
 
         def uniform(t0, s):
             at = pl.ds(t0, CHUNK)
             v = tok_ref[r, at, :].astype(F32)
-            _, slope = silu_and_slope(v * row_of(tab_ref, 0, s) + row_of(tab_ref, SEGS, s))
+            _, slope = silu_and_slope(v * entry(tab_ref, s) + entry(tab_ref, 4 + s))
             da = slope * q_ref[at, :]
             da_ref[r, at, :] = da.astype(BF16)
-            add_sums(acc_ref, s, da, da * v)
+            sums.add(t0, CHUNK, da, da * v)
 
         def mixed(t0):
             at = pl.ds(t0, CHUNK)
             t = frame_ids(t0, CHUNK, width)
             v = tok_ref[r, at, :].astype(F32)
-            _, slope = silu_and_slope(v * pick(tab_ref, 0, t, row) + pick(tab_ref, SEGS, t, row))
+            _, slope = silu_and_slope(v * pick(tab_ref, 0, t, row) + pick(tab_ref, 4, t, row))
             da = slope * q_ref[at, :]
             da_ref[r, at, :] = jnp.where(t < row.ends[2], da, 0.0).astype(BF16)
             add_masked_sums(acc_ref, t, row, da, da * v)
 
-        row.chunks(uniform, mixed)
+        row.chunks(uniform, mixed, sums, acc_ref)
         row_copy(r).start()
-        put_sums(acc_ref, gst_ref, [msg_ref], row, r)
+        put_sums(acc_ref, gst_ref, [], row, r)
         put_affine_grads(row, r, st_ref, rx_ref, gst_ref, aff_ref, part_ref, 0)
+        value = part_ref[pl.ds(4 * r + row.long_at, 1), : 2 * width]
+        part_ref[pl.ds(4 * r + SEGS, 1), 2 * width :] = value - value.astype(BF16).astype(F32)
 
     for_rows(len_ref, rows, frames, body)
     out_ref[...] = part_ref[...].astype(BF16)
@@ -630,9 +681,9 @@
             at = pl.ds(t0, CHUNK)
             out = (
                 og_ref[r, at, :].astype(F32) * ROOT_HALF
-                + da_ref[r, at, :].astype(F32) * row_of(tab_ref, 0, s)
-                + tok_ref[r, at, :].astype(F32) * row_of(tab_ref, SEGS, s)
-                + row_of(tab_ref, 2 * SEGS, s)
+                + da_ref[r, at, :].astype(F32) * entry(tab_ref, s)
+                + tok_ref[r, at, :].astype(F32) * entry(tab_ref, 4 + s)
+                + entry(tab_ref, 8 + s)
             )
             out_ref[r, at, :] = out.astype(BF16)
 
@@ -641,8 +692,8 @@
             t = frame_ids(t0, CHUNK, width)
             grad = (
                 da_ref[r, at, :].astype(F32) * pick(tab_ref, 0, t, row)
-                + tok_ref[r, at, :].astype(F32) * pick(tab_ref, SEGS, t, row)
-                + pick(tab_ref, 2 * SEGS, t, row)
+                + tok_ref[r, at, :].astype(F32) * pick(tab_ref, 4, t, row)
+                + pick(tab_ref, 8, t, row)
             )
             out = og_ref[r, at, :].astype(F32) * ROOT_HALF + jnp.where(t < row.ends[2], grad, 0.0)
             out_ref[r, at, :] = out.astype(BF16)
@@ -655,21 +706,46 @@
         row_copy(r).wait()
 
 
-def assemble_kernel(mine_ref, other_ref, out2_hbm, out1_hbm, buf_ref, sems):
-    chips, count, _, rows, width = mine_ref.shape
+def projection_grad_kernel(all_ref, fc1_hbm, fc2_hbm, bias1_ref, bias2_ref, conv_bias_ref, rows_ref, grad_ref, sems):
+    device = lax.axis_index("chip") * 2 + lax.axis_index("core")
+    width = conv_bias_ref.shape[1]
+    for i in range(all_ref.shape[0] // PAD):
+        block = pl.ds(pl.multiple_of((device ^ i) * PAD, PAD), PAD)
+        rows_ref[i * PAD : (i + 1) * PAD, :] = all_ref[block, :]
+    grads, styles = rows_ref[:, : 4 * width], rows_ref[:, 4 * width :]
+    grad_ref[...] = lax.dot_general(styles, grads, (((0,), (0,)), ((), ())), preferred_element_type=F32)
+    copies = [
+        pltpu.make_async_copy(grad_ref.at[:, pl.ds(i * 2 * width, 2 * width)], out, sems.at[i])
+        for i, out in enumerate((fc1_hbm, fc2_hbm))
+    ]
+    for copy in copies:
+        copy.start()
+    values = grads.astype(F32)
+    of_segment = frame_ids(0, values.shape[0], values.shape[1]) % 4 < SEGS
+    bias = jnp.sum(jnp.where(of_segment, values, 0.0), axis=0, keepdims=True)
+    bias1_ref[...] = bias[:, : 2 * width]
+    bias2_ref[...] = bias[:, 2 * width :]
+    rest = jnp.where(of_segment[:, :width], 0.0, values[:, :width])
+    conv_bias_ref[...] = jnp.sum(rest, axis=0, keepdims=True)
+    for copy in copies:
+        copy.wait()
+
+
+def assemble_kernel(own, half_ref, *refs):
+    out2_hbm, out1_hbm, buf_ref, sems = refs[-4:]
+    chips, count, _, rows, width = half_ref.shape
     half = chips * count * rows // 3
-    first = lax.axis_index("core") == 0
+    core = lax.axis_index("core")
+    place = pl.ds(pl.multiple_of((core if own else 1 - core) * half, half), half)
     copies = []
     for which, out_hbm in enumerate((out2_hbm, out1_hbm)):
         for b in range(chips * count):
             for j in range(rows // PAD):
                 at = b * rows + j * PAD
                 tap, channel = at // half, at % half
-                block = (b // count, b % count, which, slice(j * PAD, (j + 1) * PAD))
-                mine, other = mine_ref[block].astype(F32), other_ref[block].astype(F32)
-                buf_ref[which, tap, channel : channel + PAD, :] = jnp.where(first, mine, other)
-                buf_ref[which, tap, half + channel : half + channel + PAD, :] = jnp.where(first, other, mine)
-        copies.append(pltpu.make_async_copy(buf_ref.at[which], out_hbm, sems.at[which]))
+                block = half_ref[b // count, b % count, which, j * PAD : (j + 1) * PAD]
+                buf_ref[which, tap, channel : channel + PAD, :] = block.astype(F32)
+        copies.append(pltpu.make_async_copy(buf_ref.at[which], out_hbm.at[:, place, :], sems.at[which]))
         copies[-1].start()
     for copy in copies:
         copy.wait()
@@ -678,7 +754,7 @@
 SPACES = {"s": pltpu.SMEM, "v": pltpu.VMEM, "h": pltpu.HBM}
 
 
-def call(kernel, spaces, arrays, outs, scratch, vmem_mib, flops=0, nbytes=8 << 20):
+def call(kernel, spaces, arrays, outs, scratch, vmem_mib, flops=0, nbytes=8 << 20, aliases=()):
     arrays = [
         pltpu.with_memory_space_constraint(a, pltpu.HBM) if c == "h" else a for c, a in zip(spaces, arrays)
     ]
@@ -700,6 +776,7 @@
         out_shape=shapes,
         in_specs=specs,
         out_specs=out_specs,
+        input_output_aliases=dict(aliases),
         scratch_shapes=[pltpu.SemaphoreType.DMA(s) if len(s) == 1 else pltpu.VMEM(*s) for s in scratch],
         compiler_params=pltpu.CompilerParams(vmem_limit_bytes=vmem_mib << 20),
         cost_estimate=pl.CostEstimate(flops=flops, bytes_accessed=nbytes, transcendentals=0),
@@ -738,9 +815,7 @@
 def gather_rows(x):
     steps = [("core", 1)] + [("chip", 1 << b) for b in range((lax.axis_size("chip") - 1).bit_length())]
     for axis, bit in steps:
-        other = swap(x, axis, bit)
-        upper = (lax.axis_index(axis) & bit) != 0
-        x = jnp.where(upper, jnp.concatenate([other, x]), jnp.concatenate([x, other]))
+        x = jnp.concatenate([x, swap(x, axis, bit)])
     return x
 
 
@@ -756,8 +831,9 @@
     own, wide = ((rows, frames, width), BF16), ((rows, padded, width), BF16)
     hid, taps, kernel = ((rows, padded, width), F32), ((rows, frames, 3 * width), BF16), ((3 * width, width), BF16)
     sums, msg, half = ((rows, 8, width), F32), ((2 * rows, width), F32), ((3 * width // 2, width), BF16)
-    acc, tab = ((8, 8, width), F32), ((16, width), F32)
+    acc, tab = ((8, 8, width), F32), ((16, 8, width), F32)
     buf, xs = ((padded, width), F32), ((padded, 3 * width), BF16)
+    products = ((3, padded, width), F32)
     flops = 2 * rows * frames * 3 * width * width
 
     tok, w1, st1, msg1 = call(
@@ -766,82 +842,99 @@
         [((rows, PAD, width), BF16), ((rows, PAD, width), BF16), acc, (3,), (rows,)], SMALL,
     )
     rx1 = exchange(msg1)
-    low1, hidden_hbm, hidden, st2, msg2, og, w2 = call(
-        first_half_kernel, "svvvvvhh" + "hhvvvvv", (lengths, tok, st1, rx1, affine1, w1, out_grad, kernel2),
-        [own, hid, hid, sums, msg, own, kernel], [own, buf, xs, tab, acc, (2,), (2 * rows,)], SMALL, flops,
+    low1, hidden, st2, msg2, og, w2 = call(
+        first_half_kernel, "svvvvvhh" + "vvvvvv", (lengths, tok, st1, rx1, affine1, w1, out_grad, kernel2),
+        [wide, hid, sums, msg, own, kernel], [products, tab, acc, (2,)], SMALL, flops,
     )
     rx2 = exchange([msg2] * count)
-    gs2, grad_low2, bias_part = call(
-        branch_grad_kernel, "svvv" + "vvv", (lengths, og, rx1, w2), [taps, wide, ((8, width), F32)], [buf, xs],
-        SMALL, flops,
-    )
-    low2, low2_hbm, da2, gst2, msg3 = call(
-        second_norm_kernel, "svvvvv" + "vhhvv", (lengths, hidden, grad_low2, st2, rx2, affine2),
-        [wide, wide, wide, sums, msg], [wide, tab, acc, (2 * rows,)], SMALL,
+    gs2, grad_low2, bias_part, low1_hbm, hidden_hbm = call(
+        branch_grad_kernel, "svvvvv" + "vvvhh", (lengths, og, rx1, w2, low1, hidden),
+        [taps, wide, ((8, width), F32), wide, hid], [buf, xs, (2,)], SMALL, flops,
+    )
+    low2, da2, gst2, msg3 = call(
+        second_norm_kernel, "svvvvv" + "vvvv", (lengths, hidden, grad_low2, st2, rx2, affine2),
+        [wide, wide, sums, msg], [tab, acc], SMALL,
     )
     rx3 = exchange([msg3] * count)
 
-    def kernel_grad(own_half, first_frame, low, gs):
+    def kernel_grad(own_half, first_frame, low, gs, kept):
         return call(
-            functools.partial(kernel_grad_kernel, own_half, first_frame), "vvv", (low, gs), [half],
-            [((width // 2, 3 * width), F32)], SMALL, flops // 2,
-        )[0]
-
-    send2 = kernel_grad(False, PAD, low2, gs2)
+            functools.partial(kernel_grad_kernel, own_half, first_frame), "vvv" + "vh", (low, gs, kept), [half, wide],
+            [((width // 2, 3 * width), F32), (1,)], SMALL, flops // 2,
+        )
+
+    send2, low2_hbm = kernel_grad(False, PAD, low2, gs2, low2)
     got2 = swap(send2, "core", 1)
-    keep2 = kernel_grad(True, PAD, low2, after(gs2, send2, *rx3))
-    half2 = (got2.astype(F32) + keep2.astype(F32)).astype(BF16)
-    part2 = scatter_sum(half2.reshape(chips, -1, width), "chip")
-
-    gs1, send1, keep1, affine_part2 = call(
+    keep2, da2_hbm = kernel_grad(True, PAD, low2, after(gs2, send2), da2)
+    half2 = (got2.astype(F32) + after(keep2, *rx3).astype(F32)).astype(BF16)
+    blocks2 = lax.all_to_all(half2.reshape(chips, -1, width), "chip", 0, 0)
+
+    grad_hidden, send1, keep1, affine_part2 = call(
         hidden_grad_kernel, "shhhvvvvv" + "hvvv",
-        (lengths, low1, after(da2, half2), hidden_hbm, st2, rx2, gst2, rx3, affine2),
-        [taps, half, half, ((4 * rows, 2 * width), F32)],
-        [own, wide, hid, taps, buf, tab, ((width, 3 * width), F32), (3 * rows,), (rows,)], LARGE, flops,
-    )
-    got1 = swap(after(send1, part2), "core", 1)
+        (lengths, low1_hbm, after(da2_hbm, half2), hidden_hbm, st2, rx2, gst2, rx3, affine2),
+        [wide, half, half, ((4 * rows, 2 * width), F32)],
+        [wide, wide, hid, wide, ((frames, 3 * width), BF16), buf, tab, ((width, 3 * width), F32), (3 * rows,), (rows,)], LARGE, flops,
+    )
+    got1 = swap(after(send1, blocks2), "core", 1)
+    part2 = jnp.sum(blocks2.astype(F32), axis=0).astype(BF16)
     half1 = (got1.astype(F32) + keep1.astype(F32)).astype(BF16)
     part1 = scatter_sum(half1.reshape(chips, -1, width), "chip")
 
-    da1, gst1, msg4, affine_part = call(
-        first_norm_grad_kernel, "shhhvvvvv" + "hvvv",
-        (lengths, after(gs1, half1), kernel1, tokens, st1, rx1, affine1, affine_part2, bias_part),
-        [own, sums, msg, ((4 * rows, 4 * width), BF16)],
-        [taps, kernel, own, own, ((frames, width), F32), tab, acc, ((4 * rows, 4 * width), F32), (1 + 2 * rows,), (rows,)],
+    da1, gst1, last_part = call(
+        first_norm_grad_kernel, "shhhvvvvv" + "hvv",
+        (lengths, after(grad_hidden, half1), kernel1, tokens, st1, rx1, affine1, affine_part2, bias_part),
+        [own, sums, ((4 * rows, 4 * width), BF16)],
+        [wide, kernel, own, own, ((frames, width), F32), products, tab, acc, ((4 * rows, 4 * width), F32),
+         (1 + 2 * rows,), (rows,)],
         LARGE, flops,
     )
     both = jnp.concatenate([part2.reshape(count, -1, width), part1.reshape(count, -1, width)], axis=1)
-    both = scatter_sum(after(both, da1), "tm")
-    rx4 = exchange([after(msg4, part1)] * count)
-    affine_grads = sum_over_tm(after(affine_part, part1)).astype(BF16)
+    both = after(both, da1)
+    last_part = after(last_part, both)
+    both = scatter_sum(both, "tm")
     (block_out,) = call(
-        block_out_kernel, "shhhv" + "h", (lengths, low2_hbm, after(tokens, da1), kernel2, conv2_bias.reshape(1, width)), [own],
-        [wide, own, kernel, buf, ((frames, 3 * width), BF16), own, (1 + 2 * rows,), (rows,)], LARGE, flops,
-    )
-    both = spread(after(both, block_out), "tm")
+        block_out_kernel, "shhhv" + "h", (lengths, low2_hbm, after(tokens, both), kernel2, conv2_bias.reshape(1, width)), [own],
+        [wide, own, kernel, products, own, (1 + 2 * rows,), (rows,)], LARGE, flops,
+    )
+    last = sum_over_tm(last_part)
+    affine_grads = after(last, both).astype(BF16)
+    both = spread(both, "tm")
     (input_grad,) = call(
-        input_grad_kernel, "shhhvvvvv" + "h", (lengths, out_grad, da1, tokens, st1, rx1, gst1, rx4, affine1), [own],
+        input_grad_kernel, "shhhvvvvv" + "h", (lengths, out_grad, after(da1, both), tokens, st1, rx1, gst1, last, affine1), [own],
         [own, own, own, tab, own, (3 * rows,), (rows,)], LARGE,
     )
-    both = spread(after(both, input_grad), "chip")
-
     mine = affine_grads.reshape(rows, 4, 4 * width)[:, :SEGS].reshape(rows * SEGS, 4 * width)
     style_grad = lax.dot_general(
         mine[:, : 2 * width], fc1_weight, (((1,), (1,)), ((), ())), preferred_element_type=F32
     ) + lax.dot_general(mine[:, 2 * width :], fc2_weight, (((1,), (1,)), ((), ())), preferred_element_type=F32)
+    style_grad = style_grad.reshape(style.shape)
     style_pad = jnp.pad(style, ((0, 0), (0, 1), (0, 0))).reshape(rows * 4, -1)
     gathered = gather_rows(jnp.concatenate([affine_grads, style_pad], axis=1))
-    grads, styles = gathered[:, : 4 * width], gathered[:, 4 * width :]
-    fc_grads = lax.dot_general(styles, grads, (((0,), (0,)), ((), ())), preferred_element_type=F32)
-    by_segment = jnp.sum(grads.reshape(-1, 4, 4 * width).astype(F32), axis=0)
-    fc_bias_grads = jnp.sum(by_segment[:SEGS], axis=0)
+    both = spread(after(both, block_out, gathered), "chip")
+    fc_shape, bias_shape = ((style.shape[2], 2 * width), F32), ((1, 2 * width), F32)
+    fc1_grad, fc2_grad, fc1_bias_grad, fc2_bias_grad, conv2_bias_grad = call(
+        projection_grad_kernel, "v" + "hhvvv", (gathered,), [fc_shape, fc_shape, bias_shape, bias_shape, ((1, width), F32)],
+        [(gathered.shape, BF16), ((style.shape[2], 4 * width), F32), (2,)], SMALL,
+    )
+    fc1_bias_grad, fc2_bias_grad, conv2_bias_grad = (
+        b.reshape(b.shape[1]) for b in (fc1_bias_grad, fc2_bias_grad, conv2_bias_grad)
+    )
 
     both = both.reshape(chips, count, 2, -1, width)
-    other = swap(after(both, fc_grads, fc_bias_grads, style_grad), "core", 1)
+    both, input_grad, *small = lax.optimization_barrier(
+        (both, input_grad, style_grad, fc1_grad, fc2_grad, fc1_bias_grad, fc2_bias_grad, conv2_bias_grad)
+    )
+    style_grad, fc1_grad, fc2_grad, fc1_bias_grad, fc2_bias_grad, conv2_bias_grad = small
+    other = swap(both, "core", 1)
     if both.shape[3] % PAD == 0:
         conv_shape = ((3, width, width), F32)
+        buffers = [((2, 3, width // 2, width), F32), (2,)]
+        sums_own = call(
+            functools.partial(assemble_kernel, True), "v" + "hh", (both,), [conv_shape, conv_shape], buffers, SMALL,
+        )
         conv2_sum, conv1_sum = call(
-            assemble_kernel, "vv" + "hh", (both, other), [conv_shape, conv_shape], [((2, 3, width, width), F32), (2,)], SMALL,
+            functools.partial(assemble_kernel, False), "vhh" + "hh", (other, *sums_own), [conv_shape, conv_shape], buffers,
+            SMALL, aliases=((1, 0), (2, 1)),
         )
     else:
         first = lax.axis_index("core") == 0
@@ -849,16 +942,8 @@
         halves = [jnp.moveaxis(h, 2, 0).reshape(2, 3, width // 2, width) for h in halves]
         conv2_sum, conv1_sum = jnp.concatenate(halves, axis=2).astype(F32)
     return (
-        block_out,
-        input_grad,
-        style_grad.reshape(style.shape),
-        fc_grads[:, : 2 * width],
-        fc_bias_grads[: 2 * width],
-        conv1_sum,
-        fc_grads[:, 2 * width :],
-        fc_bias_grads[2 * width :],
-        conv2_sum,
-        by_segment[SEGS, :width],
+        block_out, input_grad, style_grad, fc1_grad, fc1_bias_grad, conv1_sum, fc2_grad, fc2_bias_grad, conv2_sum,
+        conv2_bias_grad,
     )
 
 

time: 171 us -> 155 us (0.906)
  starting transfers between devices: 47.3 us -> 41.1 us
  local copies, waits for them, and re-layouts: 8.52 us -> 3.54 us
  Pallas kernels: 69.7 us -> 66.8 us
  other arithmetic: 5.47 us -> 3.51 us
    ppermute x21 -> x18, waiting for transfers between devices: 12 us -> 23.4 us  [swap(): lax.ppermute(x, axis, [(i, i ^ bit) for i in range(lax.axis_size(axis))])]
    all_to_all x2, waiting for transfers between devices: 24.2 us -> 13 us  [spread(): lax.all_to_all(jnp.broadcast_to(block[None], (lax.axis_size(axis), *block...]
    ppermute x21 -> x18, starting transfers between devices: 27.4 us -> 22.6 us  [swap(): lax.ppermute(x, axis, [(i, i ^ bit) for i in range(lax.axis_size(axis))])]
    all_to_all x0 -> x1, starting transfers between devices: none -> 3.67 us  [per_device(): blocks2 = lax.all_to_all(half2.reshape(chips, -1, width), 'chip', 0, 0)]
    slice x3 -> x0, local copies, waits for them, and re-layouts: 3.46 us -> none  [the longest x1 2.28 us: per_device(): fc_grads[:, 2 * width:]]
    all_to_all x3 -> x2, starting transfers between devices: 11.1 us -> 7.65 us  [scatter_sum(): lax.all_to_all(blocks, axis, 0, 0).astype(F32)]
    pallas_call x11 -> x13, Pallas kernels: 69.7 us -> 66.8 us  [call(): pl.pallas_call(kernel, out_shape=shapes, in_specs=specs, out_specs=out_sp...]
  transfers between devices with their start and end apart: 26 -> 23, of which waited for: 10 -> 10; matrix products, arithmetic and copies ran while one was open for 7% -> 2% of each run, Pallas kernels for 26% -> 31%
where the time goes in v2:
time: 155 us; the launch traced here: 154 us
  Pallas kernels  66.8 us (43%)
  starting transfers between devices  41.1 us (27%)
  waiting for transfers between devices  37.4 us (24%)
  local copies, waits for them, and re-layouts  3.54 us (2%)
  other arithmetic  3.51 us (2%)
    pallas_call x13, Pallas kernels, call(): pl.pallas_call(kernel, out_shape=shapes, in_specs=specs, out_specs=out_sp...  66.8 us
    ppermute x18, waiting for transfers between devices, swap(): lax.ppermute(x, axis, [(i, i ^ bit) for i in range(lax.axis_size(axis))])  23.4 us
    ppermute x18, starting transfers between devices, swap(): lax.ppermute(x, axis, [(i, i ^ bit) for i in range(lax.axis_size(axis))])  22.6 us
    all_to_all x2, waiting for transfers between devices, spread(): lax.all_to_all(jnp.broadcast_to(block[None], (lax.axis_size(axis), *block...  13 us
    all_to_all x2, starting transfers between devices, scatter_sum(): lax.all_to_all(blocks, axis, 0, 0).astype(F32)  7.65 us
    all_to_all x2, starting transfers between devices, spread(): lax.all_to_all(jnp.broadcast_to(block[None], (lax.axis_size(axis), *block...  7.15 us
    all_to_all x1, starting transfers between devices, per_device(): blocks2 = lax.all_to_all(half2.reshape(chips, -1, width), 'chip', 0, 0)  3.67 us
  transfers between devices with their start and end apart: 23, of which 10 were waited for; matrix products, arithmetic and copies ran while one was open for 2% of the time, Pallas kernels for 31%

profile of v2, /device:TPU:0, one launch (start us, length us, event | category | flops | bytes accessed | tf_op | source)
XLA Modules:
  0.0 154.2 jit_solution(7721942578294362177)
XLA Ops:
  1.4 3.2 %shard_map.186 = (bf16[4,512,512]{2,1,0:T(8,128)(2,1)S(1)}, bf16[1536,512]{1,0:T(8,128)(2,1)S(1)}, f32[4,8,512]{2,1,0:T(8,128)S(1)}, f32[24,512]{1,0:T(8,128)S(1...) custom-call(s32[4,3]{1,0:T(4,128)S(1)} %copy-done.1, bf16[4,512,512]{2,1,0:T(8,128)(2,1)} %tok_hbm.6, ...), custom_call_target="tpu_custom_call" | custom-call | bytes 8388608 | tf_op jit(solution)/shard_map/pallas_call | solution.py:774
  4.6 3.0 %collective-permute-start = (f32[24,512]{1,0:T(8,128)S(1)}, f32[24,512]{1,0:T(8,128)S(1)}, u32[]{:S(2)}, u32[]{:S(2)}) collective-permute-start(f32[24,512]{1,0:T(8,128)S(1)} %get-tuple-element.74), channel_id=1, source_target_pairs={{0,1},{1,0},{2,3},{3,2},{4,5},{5,4},{6,7},{7,6},{8,9},{9,8},{10,11... | collective-permute-start | bytes 147464 | tf_op jit(solution)/shard_map/ppermute | solution.py:803
  7.6 2.9 %collective-permute-start.1 = (f32[24,512]{1,0:T(8,128)S(1)}, f32[24,512]{1,0:T(8,128)S(1)}, u32[]{:S(2)}, u32[]{:S(2)}) collective-permute-start(f32[24,512]{1,0:T(8,128)S(1)} %get-tuple-element.75), channel_id=1, source_target_pairs={{0,2},{1,3},{2,0},{3,1},{4,6},{5,7},{6,4},{7,5},{8,10},{9,11},{10,... | collective-permute-start | bytes 147464 | tf_op jit(solution)/shard_map/ppermute | solution.py:803
  10.9 2.7 %collective-permute-done.1.rx_ref_2_ = f32[24,512]{1,0:T(8,128)S(1)} collective-permute-done((f32[24,512]{1,0:T(8,128)S(1)}, f32[24,512]{1,0:T(8,128)S(1)}, u32[]{:S(2)}, u32[]{:S(2)}) %collective-permute-start.1) | collective-permute-done | bytes 49184 | tf_op jit(solution)/shard_map/ppermute | solution.py:803
  13.6 2.8 %collective-permute-done.2.rx_ref_3_ = f32[24,512]{1,0:T(8,128)S(1)} collective-permute-done((f32[24,512]{1,0:T(8,128)S(1)}, f32[24,512]{1,0:T(8,128)S(1)}, u32[]{:S(2)}, u32[]{:S(2)}) %collective-permute-start.2) | collective-permute-done | bytes 49184 | tf_op jit(solution)/shard_map/ppermute | solution.py:803
  16.4 7.7 %shard_map.187 = (bf16[4,544,512]{2,1,0:T(8,128)(2,1)S(1)}, f32[4,544,512]{2,1,0:T(8,128)S(1)}, f32[4,8,512]{2,1,0:T(8,128)S(1)}, f32[8,512]{1,0:T(8,128)S(1)}, ...) custom-call(s32[4,3]{1,0:T(4,128)S(1)} %copy-done.1, bf16[4,512,512]{2,1,0:T(8,128)(2,1)S(1)} %get-tuple-element.71.tok_ref, ...), custom_call_target="tpu_custom_call" | custom-call | flops 3221225472 | bytes 8388608 | tf_op jit(solution)/shard_map/pallas_call | solution.py:774
  24.2 1.7 %collective-permute-start.4 = (f32[8,512]{1,0:T(8,128)S(1)}, f32[8,512]{1,0:T(8,128)S(1)}, u32[]{:S(2)}, u32[]{:S(2)}) collective-permute-start(f32[8,512]{1,0:T(8,128)S(1)} %get-tuple-element.84.rx_ref_0_), channel_id=1, source_target_pairs={{0,2},{1,3},{2,0},{3,1},{4,6},{5,7},{6,4},{7,5},{8,10},{9,11},{10,... | collective-permute-start | bytes 49160 | tf_op jit(solution)/shard_map/ppermute | solution.py:803
  25.9 2.7 %collective-permute-start.5 = (f32[8,512]{1,0:T(8,128)S(1)}, f32[8,512]{1,0:T(8,128)S(1)}, u32[]{:S(2)}, u32[]{:S(2)}) collective-permute-start(f32[8,512]{1,0:T(8,128)S(1)} %get-tuple-element.84.rx_ref_0_), channel_id=1, source_target_pairs={{0,3},{1,2},{2,1},{3,0},{4,7},{5,6},{6,5},{7,4},{8,11},{9,10},{10,... | collective-permute-start | bytes 49160 | tf_op jit(solution)/shard_map/ppermute | solution.py:803
  28.5 7.4 %shard_map.188 = (bf16[4,512,1536]{2,1,0:T(8,128)(2,1)S(1)}, bf16[4,544,512]{2,1,0:T(8,128)(2,1)S(1)}, f32[8,512]{1,0:T(8,128)S(1)}, bf16[4,544,512]{2,1,0:T(8,128)(2,1)}, f32[4,544,512]{2,1,0:T(8,128)}) custom-call(s32[4,3]{1,0:T(4,128)S(1)} %copy-done.1, bf16[4,512,512]{2,1,0:T(8,128)(2,1)S(1)} %get-tuple-element.79.og_ref, ...), custom_call_target="tpu_custom_call" | custom-call | flops 3221225472 | bytes 8388608 | tf_op jit(solution)/shard_map/pallas_call | solution.py:774
  36.0 4.2 %shard_map.189 = (bf16[4,544,512]{2,1,0:T(8,128)(2,1)S(1)}, bf16[4,544,512]{2,1,0:T(8,128)(2,1)S(1)}, f32[4,8,512]{2,1,0:T(8,128)S(1)}, f32[8,512]{1,0:T(8,128)S(1)}) custom-call(s32[4,3]{1,0:T(4,128)S(1)} %copy-done.1, f32[4,544,512]{2,1,0:T(8,128)S(1)} %get-tuple-element.78.hid_ref, bf16[4,544,512]{2,1,0:T(8,128)(2,1)S(1)} %get-tuple-element.82.q_ref, ...), custom_call_target="tpu_custom_call" | custom-call | bytes 8388608 | tf_op jit(solution)/shard_map/pallas_call | solution.py:774
  40.2 2.6 %shard_map.190 = (bf16[768,512]{1,0:T(8,128)(2,1)S(1)}, bf16[4,544,512]{2,1,0:T(8,128)(2,1)}) custom-call(bf16[4,544,512]{2,1,0:T(8,128)(2,1)S(1)} %get-tuple-element.85.low_ref.kept_ref, bf16[4,512,1536]{2,1,0:T(8,128)(2,1)S(1)} %get-tuple-element.89.gs_ref, bf16[4,544,512]{2,1,0:T(8,128)(2,1)S(1)} %get-tuple-element.85.low_ref.kept_ref), custom_call_target="tpu_custom_call" | custom-call | flops 1610612736 | bytes 8388608 | tf_op jit(solution)/shard_map/pallas_call | solution.py:774
  42.9 2.3 %collective-permute-start.8 = (f32[8,512]{1,0:T(8,128)S(1)}, f32[8,512]{1,0:T(8,128)S(1)}, u32[]{:S(2)}, u32[]{:S(2)}) collective-permute-start(f32[8,512]{1,0:T(8,128)S(1)} %get-tuple-element.92.grx_ref_0_), channel_id=1, source_target_pairs={{0,2},{1,3},{2,0},{3,1},{4,6},{5,7},{6,4},{7,5},{8,10},{9,11},{10,... | collective-permute-start | bytes 49160 | tf_op jit(solution)/shard_map/ppermute | solution.py:803
  45.2 2.1 %collective-permute-start.9 = (f32[8,512]{1,0:T(8,128)S(1)}, f32[8,512]{1,0:T(8,128)S(1)}, u32[]{:S(2)}, u32[]{:S(2)}) collective-permute-start(f32[8,512]{1,0:T(8,128)S(1)} %get-tuple-element.92.grx_ref_0_), channel_id=1, source_target_pairs={{0,3},{1,2},{2,1},{3,0},{4,7},{5,6},{6,5},{7,4},{8,11},{9,10},{10,... | collective-permute-start | bytes 49160 | tf_op jit(solution)/shard_map/ppermute | solution.py:803
  47.3 2.5 %shard_map.191 = (bf16[768,512]{1,0:T(8,128)(2,1)S(1)}, bf16[4,544,512]{2,1,0:T(8,128)(2,1)}) custom-call(bf16[4,544,512]{2,1,0:T(8,128)(2,1)S(1)} %get-tuple-element.85.low_ref.kept_ref, bf16[4,512,1536]{2,1,0:T(8,128)(2,1)S(1)} %get-tuple-element.89.gs_ref, bf16[4,544,512]{2,1,0:T(8,128)(2,1)S(1)} %get-tuple-element.90.kept_ref), custom_call_target="tpu_custom_call" | custom-call | flops 1610612736 | bytes 8388608 | tf_op jit(solution)/shard_map/pallas_call | solution.py:774
  51.9 3.7 %all-to-all-start = ((bf16[4,192,512]{2,1,0:T(8,128)(2,1)}), bf16[4,192,512]{2,1,0:T(8,128)(2,1)S(1)}, u32[]{:S(2)}, u32[]{:S(2)}) async-start(bf16[4,192,512]{2,1,0:T(8,128)(2,1)} %bitcast.4), calls=%async_computation | async-start | bytes 1572864 | tf_op jit(solution)/shard_map/all_to_all | solution.py:870
  55.6 9.1 %shard_map.192 = (bf16[4,544,512]{2,1,0:T(8,128)(2,1)}, bf16[768,512]{1,0:T(8,128)(2,1)S(1)}, bf16[768,512]{1,0:T(8,128)(2,1)S(1)}, f32[16,1024]{1,0:T(8,128)S(1)}) custom-call(s32[4,3]{1,0:T(4,128)S(1)} %copy-done.2, bf16[4,544,512]{2,1,0:T(8,128)(2,1)} %get-tuple-element.94.low_hbm, bf16[4,544,512]{2,1,0:T(8,128)(2,1)} %get-tuple-element.96.da_hbm, ...), custom_call_target="tpu_custom_call" | custom-call | flops 3221225472 | bytes 8388608 | tf_op jit(solution)/shard_map/pallas_call | solution.py:774
  65.7 2.3 %collective-permute-done.10 = bf16[768,512]{1,0:T(8,128)(2,1)S(1)} collective-permute-done((bf16[768,512]{1,0:T(8,128)(2,1)S(1)}, bf16[768,512]{1,0:T(8,128)(2,1)S(1)}, u32[]{:S(2)}, u32[]{:S(2)}) %collective-permute-start.10) | collective-permute-done | bytes 786464 | tf_op jit(solution)/shard_map/ppermute | solution.py:803
  69.1 3.7 %all-to-all-start.1 = ((bf16[4,192,512]{2,1,0:T(8,128)(2,1)}), bf16[4,192,512]{2,1,0:T(8,128)(2,1)S(1)}, u32[]{:S(2)}, u32[]{:S(2)}) async-start(bf16[4,192,512]{2,1,0:T(8,128)(2,1)} %bitcast.6), calls=%async_computation.1 | async-start | bytes 1572864 | tf_op jit(solution)/shard_map/all_to_all | solution.py:795
  72.9 11.2 %shard_map.193 = (bf16[4,512,512]{2,1,0:T(8,128)(2,1)}, f32[4,8,512]{2,1,0:T(8,128)S(1)}, bf16[16,2048]{1,0:T(8,128)(2,1)S(1)}) custom-call(s32[4,3]{1,0:T(4,128)S(1)} %copy-done.2, bf16[4,544,512]{2,1,0:T(8,128)(2,1)} %get-tuple-element.103.g_hbm, bf16[1536,512]{1,0:T(8,128)(2,1)} %bitcast.23, bf16[4,512,512]{2,1,0:T(8,128)(2,1)} %tok_hbm.6, ...), custom_call_target="tpu_custom_call" | custom-call | flops 3221225472 | bytes 8388608 | tf_op jit(solution)/shard_map/pallas_call | solution.py:774
  85.0 4.0 %all-to-all-start.2 = ((bf16[4,96,512]{2,1,0:T(8,128)(2,1)}), bf16[4,96,512]{2,1,0:T(8,128)(2,1)S(1)}, u32[]{:S(2)}, u32[]{:S(2)}) async-start(bf16[4,96,512]{2,1,0:T(8,128)(2,1)} %pad_maximum_fusion.1), calls=%async_computation.2 | async-start | bytes 786432 | tf_op jit(solution)/shard_map/all_to_all | solution.py:795
  89.0 2.9 %collective-permute-start.11 = (bf16[16,2048]{1,0:T(8,128)(2,1)S(1)}, bf16[16,2048]{1,0:T(8,128)(2,1)S(1)}, u32[]{:S(2)}, u32[]{:S(2)}) collective-permute-start(bf16[16,2048]{1,0:T(8,128)(2,1)S(1)} %get-tuple-element.110), channel_id=1, source_target_pairs={{0,2},{1,3},{2,0},{3,1},{4,6},{5,7},{6,4},{7,5},{8,10},{9,11},{10,... | collective-permute-start | bytes 196616 | tf_op jit(solution)/shard_map/ppermute | solution.py:803
  93.4 12.4 %collective-permute-done.11 = bf16[16,2048]{1,0:T(8,128)(2,1)S(1)} collective-permute-done((bf16[16,2048]{1,0:T(8,128)(2,1)S(1)}, bf16[16,2048]{1,0:T(8,128)(2,1)S(1)}, u32[]{:S(2)}, u32[]{:S(2)}) %collective-permute-start.11) | collective-permute-done | bytes 65568 | tf_op jit(solution)/shard_map/ppermute | solution.py:803
  107.3 1.5 %collective-permute-start.15 = (bf16[32,2176]{1,0:T(8,128)(2,1)S(1)}, bf16[32,2176]{1,0:T(8,128)(2,1)S(1)}, u32[]{:S(2)}, u32[]{:S(2)}) collective-permute-start(bf16[32,2176]{1,0:T(8,128)(2,1)S(1)} %pad_maximum_fusion.3), channel_id=1, source_target_pairs={{0,8},{8,0},{16,24},{24,16},{1,9},{9,1},{17,25},{25,17},{2,10},{10... | collective-permute-start | bytes 417800 | tf_op jit(solution)/shard_map/ppermute | solution.py:803
  109.6 3.5 %all-to-all-start.3 = ((bf16[4,96,512]{2,1,0:T(8,128)(2,1)}), bf16[4,96,512]{2,1,0:T(8,128)(2,1)S(1)}, u32[]{:S(2)}, u32[]{:S(2)}) async-start(bf16[4,96,512]{2,1,0:T(8,128)(2,1)} %broadcast_in_dim.4), calls=%async_computation.3 | async-start | bytes 786432 | tf_op jit(solution)/shard_map/all_to_all | solution.py:799
  113.1 1.7 %collective-permute-start.16 = (bf16[64,2176]{1,0:T(8,128)(2,1)S(1)}, bf16[64,2176]{1,0:T(8,128)(2,1)S(1)}, u32[]{:S(2)}, u32[]{:S(2)}) collective-permute-start(bf16[64,2176]{1,0:T(8,128)(2,1)S(1)} %pad_maximum_fusion.2), channel_id=1, source_target_pairs={{0,16},{8,24},{16,0},{24,8},{1,17},{9,25},{17,1},{25,9},{2,18},{10... | collective-permute-start | bytes 835592 | tf_op jit(solution)/shard_map/ppermute | solution.py:803
  114.9 8.6 %shard_map.194 = bf16[4,512,512]{2,1,0:T(8,128)(2,1)} custom-call(s32[4,3]{1,0:T(4,128)S(1)} %copy-done.2, bf16[4,544,512]{2,1,0:T(8,128)(2,1)} %get-tuple-element.87.low_hbm, bf16[4,512,512]{2,1,0:T(8,128)(2,1)} %tok_hbm.6, bf16[1536,512]{1,0:T(8,128)(2,1)} %bitcast.32, bf16[1,512]{1,0:T(2,128)(2,1)S(1)} %reshape.75.bias_ref), custom_call_target="tpu_custom_call" | custom-call | flops 3221225472 | bytes 8388608 | tf_op jit(solution)/shard_map/pallas_call | solution.py:774
  126.4 3.7 %all-to-all-start.4 = ((bf16[4,4,96,512]{3,2,1,0:T(8,128)(2,1)}), bf16[4,4,96,512]{3,2,1,0:T(8,128)(2,1)S(1)}, u32[]{:S(2)}, u32[]{:S(2)}) async-start(bf16[4,4,96,512]{3,2,1,0:T(8,128)(2,1)} %broadcast_in_dim.5), calls=%async_computation.4 | async-start | bytes 3145728 | tf_op jit(solution)/shard_map/all_to_all | solution.py:799
  130.5 2.0 %shard_map.196 = (f32[128,1024]{1,0:T(8,128)}, f32[128,1024]{1,0:T(8,128)}, f32[1,1024]{1,0:T(1,128)}, f32[1,1024]{1,0:T(1,128)}, f32[1,512]{1,0:T(1,128)}) custom-call(bf16[128,2176]{1,0:T(8,128)(2,1)S(1)} %pad_maximum_fusion.all_ref), custom_call_target="tpu_custom_call" | custom-call | bytes 8388608 | tf_op jit(solution)/shard_map/pallas_call | solution.py:774
  132.5 4.9 %shard_map.195 = bf16[4,512,512]{2,1,0:T(8,128)(2,1)} custom-call(s32[4,3]{1,0:T(4,128)S(1)} %copy-done.2, bf16[4,512,512]{2,1,0:T(8,128)(2,1)} %og_hbm.5, bf16[4,512,512]{2,1,0:T(8,128)(2,1)} %get-tuple-element.113.da_hbm, bf16[4,512,512]{2,1,0:T(8,128)(2,1)} %tok_hbm.6, f32[4,8,512]{2,1,0:T(8,128)S(1)} %get-tuple-element.72.st_ref, ...), custom_call_target="tpu_custom_call" | custom-call | bytes 8388608 | tf_op jit(solution)/shard_map/pallas_call | solution.py:774
  137.4 11.4 %all-to-all-done.4 = bf16[4,4,96,512]{3,2,1,0:T(8,128)(2,1)S(1)} async-done(((bf16[4,4,96,512]{3,2,1,0:T(8,128)(2,1)}), bf16[4,4,96,512]{3,2,1,0:T(8,128)(2,1)S(1)}, u32[]{:S(2)}, u32[]{:S(2)}) %all-to-all-start.4) | async-done | bytes 1572896 | tf_op jit(solution)/shard_map/all_to_all | solution.py:799
  148.8 1.8 %shard_map.197 = (f32[3,512,512]{2,1,0:T(8,128)}, f32[3,512,512]{2,1,0:T(8,128)}) custom-call(bf16[4,4,2,48,512]{4,3,2,1,0:T(8,128)(2,1)S(1)} %bitcast.21), custom_call_target="tpu_custom_call" | custom-call | bytes 8388608 | tf_op jit(solution)/shard_map/pallas_call | solution.py:774
  152.2 1.8 %shard_map.198 = (f32[3,512,512]{2,1,0:T(8,128)}, f32[3,512,512]{2,1,0:T(8,128)}) custom-call(bf16[4,4,2,48,512]{4,3,2,1,0:T(8,128)(2,1)S(1)} %collective-permute-done.17.half_ref, f32[3,512,512]{2,1,0:T(8,128)} %get-tuple-element.125.refs_0_, f32[3,512,512]{2,1,0:T(8,128)} %get-tuple-element.126.refs_1_), custom_call_target="tpu_custom_call", output_to_operand_aliasing={{0}: (1, {}), {1}: (2, {})} | custom-call | bytes 8388608 | tf_op jit(solution)/shard_map/pallas_call | solution.py:774
  (72 shorter events, 15.3 us)
Async XLA Ops:
  0.6 9.9 %copy-start = (bf16[128,1024]{1,0:T(8,128)(2,1)S(1)}, bf16[128,1024]{1,0:T(8,128)(2,1)}, u32[]{:S(2)}) copy-start(bf16[128,1024]{1,0:T(8,128)(2,1)} %param.14) | copy-start | bytes 786436
  0.7 0.7 copy-start.1
  1.4 9.2 %copy-start.6 = (bf16[1024]{0:T(1024)(128)(2,1)S(1)}, bf16[1024]{0:T(1024)(128)(2,1)}, u32[]{:S(2)}) copy-start(bf16[1024]{0:T(1024)(128)(2,1)} %param.15) | copy-start | bytes 6148
  1.4 9.2 %copy-start.7 = (bf16[1024]{0:T(1024)(128)(2,1)S(1)}, bf16[1024]{0:T(1024)(128)(2,1)}, u32[]{:S(2)}) copy-start(bf16[1024]{0:T(1024)(128)(2,1)} %param.18) | copy-start | bytes 6148
  1.4 9.2 %copy-start.5 = (bf16[4,3,128]{2,0,1:T(4,128)(2,1)S(1)}, bf16[4,3,128]{2,0,1:T(4,128)(2,1)}, u32[]{:S(2)}) copy-start(bf16[4,3,128]{2,0,1:T(4,128)(2,1)} %param.13) | copy-start | bytes 9220
  1.4 9.4 %copy-start.3 = (bf16[128,1024]{1,0:T(8,128)(2,1)S(1)}, bf16[128,1024]{1,0:T(8,128)(2,1)}, u32[]{:S(2)}) copy-start(bf16[128,1024]{1,0:T(8,128)(2,1)} %param.17) | copy-start | bytes 786436
  4.6 6.3 %collective-permute-start = (f32[24,512]{1,0:T(8,128)S(1)}, f32[24,512]{1,0:T(8,128)S(1)}, u32[]{:S(2)}, u32[]{:S(2)}) collective-permute-start(f32[24,512]{1,0:T(8,128)S(1)} %get-tuple-element.74), channel_id=1, source_target_pairs={{0,1},{1,0},{2,3},{3,2},{4,5},{5,4},{6,7},{7,6},{8,9},{9,8},{10,11... | collective-permute-start | bytes 147464 | tf_op jit(solution)/shard_map/ppermute | solution.py:803
  7.6 6.0 %collective-permute-start.1 = (f32[24,512]{1,0:T(8,128)S(1)}, f32[24,512]{1,0:T(8,128)S(1)}, u32[]{:S(2)}, u32[]{:S(2)}) collective-permute-start(f32[24,512]{1,0:T(8,128)S(1)} %get-tuple-element.75), channel_id=1, source_target_pairs={{0,2},{1,3},{2,0},{3,1},{4,6},{5,7},{6,4},{7,5},{8,10},{9,11},{10,... | collective-permute-start | bytes 147464 | tf_op jit(solution)/shard_map/ppermute | solution.py:803
  10.5 5.9 %collective-permute-start.2 = (f32[24,512]{1,0:T(8,128)S(1)}, f32[24,512]{1,0:T(8,128)S(1)}, u32[]{:S(2)}, u32[]{:S(2)}) collective-permute-start(f32[24,512]{1,0:T(8,128)S(1)} %get-tuple-element.76), channel_id=1, source_target_pairs={{0,3},{1,2},{2,1},{3,0},{4,7},{5,6},{6,5},{7,4},{8,11},{9,10},{10,... | collective-permute-start | bytes 147464 | tf_op jit(solution)/shard_map/ppermute | solution.py:803
  24.1 11.9 %collective-permute-start.3 = (f32[8,512]{1,0:T(8,128)S(1)}, f32[8,512]{1,0:T(8,128)S(1)}, u32[]{:S(2)}, u32[]{:S(2)}) collective-permute-start(f32[8,512]{1,0:T(8,128)S(1)} %get-tuple-element.84.rx_ref_0_), channel_id=1, source_target_pairs={{0,1},{1,0},{2,3},{3,2},{4,5},{5,4},{6,7},{7,6},{8,9},{9,8},{10,11... | collective-permute-start | bytes 49160 | tf_op jit(solution)/shard_map/ppermute | solution.py:803
  24.2 11.8 %collective-permute-start.4 = (f32[8,512]{1,0:T(8,128)S(1)}, f32[8,512]{1,0:T(8,128)S(1)}, u32[]{:S(2)}, u32[]{:S(2)}) collective-permute-start(f32[8,512]{1,0:T(8,128)S(1)} %get-tuple-element.84.rx_ref_0_), channel_id=1, source_target_pairs={{0,2},{1,3},{2,0},{3,1},{4,6},{5,7},{6,4},{7,5},{8,10},{9,11},{10,... | collective-permute-start | bytes 49160 | tf_op jit(solution)/shard_map/ppermute | solution.py:803
  25.9 10.1 %collective-permute-start.5 = (f32[8,512]{1,0:T(8,128)S(1)}, f32[8,512]{1,0:T(8,128)S(1)}, u32[]{:S(2)}, u32[]{:S(2)}) collective-permute-start(f32[8,512]{1,0:T(8,128)S(1)} %get-tuple-element.84.rx_ref_0_), channel_id=1, source_target_pairs={{0,3},{1,2},{2,1},{3,0},{4,7},{5,6},{6,5},{7,4},{8,11},{9,10},{10,... | collective-permute-start | bytes 49160 | tf_op jit(solution)/shard_map/ppermute | solution.py:803
  42.8 8.0 %collective-permute-start.6 = (bf16[768,512]{1,0:T(8,128)(2,1)S(1)}, bf16[768,512]{1,0:T(8,128)(2,1)S(1)}, u32[]{:S(2)}, u32[]{:S(2)}) collective-permute-start(bf16[768,512]{1,0:T(8,128)(2,1)S(1)} %get-tuple-element.88), channel_id=1, source_target_pairs={{0,4},{4,0},{1,5},{5,1},{2,6},{6,2},{3,7},{7,3},{8,12},{12,8},{9,1... | collective-permute-start | bytes 2359304 | tf_op jit(solution)/shard_map/ppermute | solution.py:803
  42.9 7.0 %collective-permute-start.7 = (f32[8,512]{1,0:T(8,128)S(1)}, f32[8,512]{1,0:T(8,128)S(1)}, u32[]{:S(2)}, u32[]{:S(2)}) collective-permute-start(f32[8,512]{1,0:T(8,128)S(1)} %get-tuple-element.92.grx_ref_0_), channel_id=1, source_target_pairs={{0,1},{1,0},{2,3},{3,2},{4,5},{5,4},{6,7},{7,6},{8,9},{9,8},{10,11... | collective-permute-start | bytes 49160 | tf_op jit(solution)/shard_map/ppermute | solution.py:803
  42.9 6.9 %collective-permute-start.8 = (f32[8,512]{1,0:T(8,128)S(1)}, f32[8,512]{1,0:T(8,128)S(1)}, u32[]{:S(2)}, u32[]{:S(2)}) collective-permute-start(f32[8,512]{1,0:T(8,128)S(1)} %get-tuple-element.92.grx_ref_0_), channel_id=1, source_target_pairs={{0,2},{1,3},{2,0},{3,1},{4,6},{5,7},{6,4},{7,5},{8,10},{9,11},{10,... | collective-permute-start | bytes 49160 | tf_op jit(solution)/shard_map/ppermute | solution.py:803
  45.2 5.5 %collective-permute-start.9 = (f32[8,512]{1,0:T(8,128)S(1)}, f32[8,512]{1,0:T(8,128)S(1)}, u32[]{:S(2)}, u32[]{:S(2)}) collective-permute-start(f32[8,512]{1,0:T(8,128)S(1)} %get-tuple-element.92.grx_ref_0_), channel_id=1, source_target_pairs={{0,3},{1,2},{2,1},{3,0},{4,7},{5,6},{6,5},{7,4},{8,11},{9,10},{10,... | collective-permute-start | bytes 49160 | tf_op jit(solution)/shard_map/ppermute | solution.py:803
  49.8 5.7 %copy-start.2 = (s32[4,3]{1,0:T(4,128)S(1)}, s32[4,3]{1,0:T(4,128)}, u32[]{:S(2)}) copy-start(s32[4,3]{1,0:T(4,128)} %len_ref.15) | copy-start | bytes 148
  51.9 13.8 %all-to-all-start = ((bf16[4,192,512]{2,1,0:T(8,128)(2,1)}), bf16[4,192,512]{2,1,0:T(8,128)(2,1)S(1)}, u32[]{:S(2)}, u32[]{:S(2)}) async-start(bf16[4,192,512]{2,1,0:T(8,128)(2,1)} %bitcast.4), calls=%async_computation | async-start | bytes 1572864 | tf_op jit(solution)/shard_map/all_to_all | solution.py:870
  65.7 2.3 %collective-permute-start.10 = (bf16[768,512]{1,0:T(8,128)(2,1)S(1)}, bf16[768,512]{1,0:T(8,128)(2,1)S(1)}, u32[]{:S(2)}, u32[]{:S(2)}) collective-permute-start(bf16[768,512]{1,0:T(8,128)(2,1)S(1)} %get-tuple-element.100), channel_id=1, source_target_pairs={{0,4},{4,0},{1,5},{5,1},{2,6},{6,2},{3,7},{7,3},{8,12},{12,8},{9,1... | collective-permute-start | bytes 2359304 | tf_op jit(solution)/shard_map/ppermute | solution.py:803
  69.1 15.0 %all-to-all-start.1 = ((bf16[4,192,512]{2,1,0:T(8,128)(2,1)}), bf16[4,192,512]{2,1,0:T(8,128)(2,1)S(1)}, u32[]{:S(2)}, u32[]{:S(2)}) async-start(bf16[4,192,512]{2,1,0:T(8,128)(2,1)} %bitcast.6), calls=%async_computation.1 | async-start | bytes 1572864 | tf_op jit(solution)/shard_map/all_to_all | solution.py:795
  84.1 24.8 %copy-start.8 = (bf16[512]{0:T(512)(128)(2,1)S(1)}, bf16[512]{0:T(512)(128)(2,1)}, u32[]{:S(2)}) copy-start(bf16[512]{0:T(512)(128)(2,1)} %param.20) | copy-start | bytes 3076
  85.0 20.8 %all-to-all-start.2 = ((bf16[4,96,512]{2,1,0:T(8,128)(2,1)}), bf16[4,96,512]{2,1,0:T(8,128)(2,1)S(1)}, u32[]{:S(2)}, u32[]{:S(2)}) async-start(bf16[4,96,512]{2,1,0:T(8,128)(2,1)} %pad_maximum_fusion.1), calls=%async_computation.2 | async-start | bytes 786432 | tf_op jit(solution)/shard_map/all_to_all | solution.py:795
  89.0 16.8 %collective-permute-start.11 = (bf16[16,2048]{1,0:T(8,128)(2,1)S(1)}, bf16[16,2048]{1,0:T(8,128)(2,1)S(1)}, u32[]{:S(2)}, u32[]{:S(2)}) collective-permute-start(bf16[16,2048]{1,0:T(8,128)(2,1)S(1)} %get-tuple-element.110), channel_id=1, source_target_pairs={{0,2},{1,3},{2,0},{3,1},{4,6},{5,7},{6,4},{7,5},{8,10},{9,11},{10,... | collective-permute-start | bytes 196616 | tf_op jit(solution)/shard_map/ppermute | solution.py:803
  91.9 13.9 %collective-permute-start.12 = (bf16[16,2048]{1,0:T(8,128)(2,1)S(1)}, bf16[16,2048]{1,0:T(8,128)(2,1)S(1)}, u32[]{:S(2)}, u32[]{:S(2)}) collective-permute-start(bf16[16,2048]{1,0:T(8,128)(2,1)S(1)} %get-tuple-element.110), channel_id=1, source_target_pairs={{0,1},{1,0},{2,3},{3,2},{4,5},{5,4},{6,7},{7,6},{8,9},{9,8},{10,11... | collective-permute-start | bytes 196616 | tf_op jit(solution)/shard_map/ppermute | solution.py:803
  93.4 12.4 %collective-permute-start.13 = (bf16[16,2048]{1,0:T(8,128)(2,1)S(1)}, bf16[16,2048]{1,0:T(8,128)(2,1)S(1)}, u32[]{:S(2)}, u32[]{:S(2)}) collective-permute-start(bf16[16,2048]{1,0:T(8,128)(2,1)S(1)} %get-tuple-element.110), channel_id=1, source_target_pairs={{0,3},{1,2},{2,1},{3,0},{4,7},{5,6},{6,5},{7,4},{8,11},{9,10},{10,... | collective-permute-start | bytes 196616 | tf_op jit(solution)/shard_map/ppermute | solution.py:803
  106.0 1.3 collective-permute-start.14
  107.3 5.8 %collective-permute-start.15 = (bf16[32,2176]{1,0:T(8,128)(2,1)S(1)}, bf16[32,2176]{1,0:T(8,128)(2,1)S(1)}, u32[]{:S(2)}, u32[]{:S(2)}) collective-permute-start(bf16[32,2176]{1,0:T(8,128)(2,1)S(1)} %pad_maximum_fusion.3), channel_id=1, source_target_pairs={{0,8},{8,0},{16,24},{24,16},{1,9},{9,1},{17,25},{25,17},{2,10},{10... | collective-permute-start | bytes 417800 | tf_op jit(solution)/shard_map/ppermute | solution.py:803
  109.6 15.4 %all-to-all-start.3 = ((bf16[4,96,512]{2,1,0:T(8,128)(2,1)}), bf16[4,96,512]{2,1,0:T(8,128)(2,1)S(1)}, u32[]{:S(2)}, u32[]{:S(2)}) async-start(bf16[4,96,512]{2,1,0:T(8,128)(2,1)} %broadcast_in_dim.4), calls=%async_computation.3 | async-start | bytes 786432 | tf_op jit(solution)/shard_map/all_to_all | solution.py:799
  113.1 10.3 %collective-permute-start.16 = (bf16[64,2176]{1,0:T(8,128)(2,1)S(1)}, bf16[64,2176]{1,0:T(8,128)(2,1)S(1)}, u32[]{:S(2)}, u32[]{:S(2)}) collective-permute-start(bf16[64,2176]{1,0:T(8,128)(2,1)S(1)} %pad_maximum_fusion.2), channel_id=1, source_target_pairs={{0,16},{8,24},{16,0},{24,8},{1,17},{9,25},{17,1},{25,9},{2,18},{10... | collective-permute-start | bytes 835592 | tf_op jit(solution)/shard_map/ppermute | solution.py:803
  126.4 4.0 %copy-start.4 = (bf16[128,1024]{1,0:T(8,128)(2,1)S(1)}, bf16[128,1024]{1,0:T(8,128)(2,1)}, u32[]{:S(2)}) copy-start(bf16[128,1024]{1,0:T(8,128)(2,1)} %param.17) | copy-start | bytes 786436
  126.4 22.5 %all-to-all-start.4 = ((bf16[4,4,96,512]{3,2,1,0:T(8,128)(2,1)}), bf16[4,4,96,512]{3,2,1,0:T(8,128)(2,1)S(1)}, u32[]{:S(2)}, u32[]{:S(2)}) async-start(bf16[4,4,96,512]{3,2,1,0:T(8,128)(2,1)} %broadcast_in_dim.5), calls=%async_computation.4 | async-start | bytes 3145728 | tf_op jit(solution)/shard_map/all_to_all | solution.py:799
  148.8 3.4 %collective-permute-start.17 = (bf16[4,4,2,48,512]{4,3,2,1,0:T(8,128)(2,1)S(1)}, bf16[4,4,2,48,512]{4,3,2,1,0:T(8,128)(2,1)S(1)}, u32[]{:S(2)}, u32[]{:S(2)}) collective-permute-start(bf16[4,4,2,48,512]{4,3,2,1,0:T(8,128)(2,1)S(1)} %bitcast.20), channel_id=1, source_target_pairs={{0,4},{4,0},{1,5},{5,1},{2,6},{6,2},{3,7},{7,3},{8,12},{12,8},{9,1... | collective-permute-start | bytes 4718600 | tf_op jit(solution)/shard_map/ppermute | solution.py:803

commit v3 on v2

--- a/solution.py
+++ b/solution.py
@@ -396,15 +396,8 @@
         copy.wait()
 
 
-def branch_grad_kernel(len_ref, og_ref, rx_ref, w_ref, low_ref, hid_ref, gs_ref, q_ref, bias_ref, low_hbm, hid_hbm,
-                       buf_ref, xs_ref, sems):
+def branch_grad_kernel(len_ref, og_ref, rx_ref, w_ref, gs_ref, q_ref, bias_ref, buf_ref, xs_ref):
     rows, frames, width = og_ref.shape
-    stores = (
-        pltpu.make_async_copy(low_ref, low_hbm, sems.at[0]),
-        pltpu.make_async_copy(hid_ref, hid_hbm, sems.at[1]),
-    )
-    for copy in stores:
-        copy.start()
     bias_ref[...] = jnp.zeros_like(bias_ref)
 
     def body(r, row):
@@ -434,8 +427,6 @@
         q_ref[r] = times_transposed(xs_ref[...], w_ref, width).astype(BF16)
 
     for_rows(len_ref, rows, frames, body)
-    for copy in stores:
-        copy.wait()
 
 
 def second_norm_kernel(len_ref, hid_ref, q_ref, st_ref, rx_ref, aff_ref, low_ref, da_ref, gst_ref, msg_ref,
@@ -540,9 +531,11 @@
         out_ref[k * half : (k + 1) * half, :] = acc_ref[:, k * width : (k + 1) * width].astype(BF16)
 
 
-def kernel_grad_kernel(own, first_frame, low_ref, gs_ref, kept_ref, out_ref, kept_hbm, acc_ref, sems):
-    store = pltpu.make_async_copy(kept_ref, kept_hbm, sems.at[0])
-    store.start()
+def kernel_grad_kernel(own, first_frame, low_ref, gs_ref, out_ref, *refs):
+    acc_ref = refs[-1] if own else refs[1]
+    if not own:
+        store = pltpu.make_async_copy(low_ref, refs[0], refs[2].at[0])
+        store.start()
     core = lax.axis_index("core")
     half = core if own else 1 - core
     acc_ref[...] = half_of_grad(low_ref, gs_ref, 0, half, first_frame)
@@ -553,14 +546,13 @@
 
     lax.fori_loop(1, low_ref.shape[0], step, 0)
     put_half(acc_ref, out_ref)
-    store.wait()
-
-
-def hidden_grad_kernel(len_ref, low_hbm, da_hbm, hid_hbm, st_ref, rx_ref, gst_ref, grx_ref, aff_ref,
-                       g_hbm, send_ref, keep_ref, part_ref, low_ref, da_ref, hid_ref, g_ref, gs_ref, buf_ref, tab_ref, acc_ref,
-                       sems, row_sems):
-    rows, frames, width = low_ref.shape[0], gs_ref.shape[0], low_ref.shape[2]
-    loads = Loads(rows, sems, [], [(da_hbm, da_ref), (hid_hbm, hid_ref), (low_hbm, low_ref)])
+    if not own:
+        store.wait()
+
+
+def hidden_grad_kernel(len_ref, low_ref, da_ref, hid_ref, st_ref, rx_ref, gst_ref, grx_ref, aff_ref,
+                       g_hbm, gs_ref, send_ref, part_ref, g_ref, buf_ref, tab_ref, acc_ref, row_sems):
+    rows, frames, width = low_ref.shape[0], gs_ref.shape[1], low_ref.shape[2]
     part_ref[...] = jnp.zeros_like(part_ref)
     acc_ref[...] = jnp.zeros_like(acc_ref)
 
@@ -570,7 +562,6 @@
     def body(r, row):
         put_affine_grads(row, r, st_ref, rx_ref, gst_ref, aff_ref, part_ref, 0)
         put_backward(row, r, st_ref, rx_ref, gst_ref, grx_ref, aff_ref, tab_ref)
-        loads.wait(r)
 
         def uniform(t0, s):
             at = pl.ds(PAD + t0, CHUNK)
@@ -601,16 +592,12 @@
             )
             buf_ref[at : at + PAD, :] = jnp.where(valid, grad, 0.0)
         g_ref[r] = buf_ref[...].astype(BF16)
-        stack_taps(buf_ref, gs_ref, row, frames, False, False)
+        stack_taps(buf_ref, gs_ref.at[r], row, frames, False, False)
         row_copy(r).start()
-        acc_ref[...] += lax.dot_general(
-            low_ref[r, PAD : PAD + frames, :], gs_ref[...], (((0,), (0,)), ((), ())), preferred_element_type=F32
-        )
+        acc_ref[...] += half_of_grad(low_ref, gs_ref, r, 1 - lax.axis_index("core"), PAD)
 
     for_rows(len_ref, rows, frames, body)
-    core, half = lax.axis_index("core"), width // 2
-    for ref, which in ((send_ref, 1 - core), (keep_ref, core)):
-        put_half(acc_ref.at[pl.ds(pl.multiple_of(which * half, half), half), :], ref)
+    put_half(acc_ref, send_ref)
     for r in range(rows):
         row_copy(r).wait()
 
@@ -812,10 +799,11 @@
     return parts[0]
 
 
-def gather_rows(x):
-    steps = [("core", 1)] + [("chip", 1 << b) for b in range((lax.axis_size("chip") - 1).bit_length())]
-    for axis, bit in steps:
-        x = jnp.concatenate([x, swap(x, axis, bit)])
+def gather_rows(x, first, rest):
+    x = jnp.concatenate([x, swap(x, "core", 1)])
+    for b in range((lax.axis_size("chip") - 1).bit_length()):
+        x = after(x, first if b == 0 else rest)
+        x = jnp.concatenate([x, swap(x, "chip", 1 << b)])
     return x
 
 
@@ -847,9 +835,8 @@
         [wide, hid, sums, msg, own, kernel], [products, tab, acc, (2,)], SMALL, flops,
     )
     rx2 = exchange([msg2] * count)
-    gs2, grad_low2, bias_part, low1_hbm, hidden_hbm = call(
-        branch_grad_kernel, "svvvvv" + "vvvhh", (lengths, og, rx1, w2, low1, hidden),
-        [taps, wide, ((8, width), F32), wide, hid], [buf, xs, (2,)], SMALL, flops,
+    gs2, grad_low2, bias_part = call(
+        branch_grad_kernel, "svvv" + "vvv", (lengths, og, rx1, w2), [taps, wide, ((8, width), F32)], [buf, xs], SMALL, flops,
     )
     low2, da2, gst2, msg3 = call(
         second_norm_kernel, "svvvvv" + "vvvv", (lengths, hidden, grad_low2, st2, rx2, affine2),
@@ -857,47 +844,47 @@
     )
     rx3 = exchange([msg3] * count)
 
-    def kernel_grad(own_half, first_frame, low, gs, kept):
-        return call(
-            functools.partial(kernel_grad_kernel, own_half, first_frame), "vvv" + "vh", (low, gs, kept), [half, wide],
-            [((width // 2, 3 * width), F32), (1,)], SMALL, flops // 2,
-        )
-
-    send2, low2_hbm = kernel_grad(False, PAD, low2, gs2, low2)
+    half_acc = ((width // 2, 3 * width), F32)
+    send2, low2_hbm = call(
+        functools.partial(kernel_grad_kernel, False, PAD), "vv" + "vh", (low2, gs2), [half, wide], [half_acc, (1,)], SMALL,
+    )
     got2 = swap(send2, "core", 1)
-    keep2, da2_hbm = kernel_grad(True, PAD, low2, after(gs2, send2), da2)
+    (keep2,) = call(
+        functools.partial(kernel_grad_kernel, True, PAD), "vv" + "v", (low2, after(gs2, send2)), [half], [half_acc], SMALL,
+    )
     half2 = (got2.astype(F32) + after(keep2, *rx3).astype(F32)).astype(BF16)
-    blocks2 = lax.all_to_all(half2.reshape(chips, -1, width), "chip", 0, 0)
-
-    grad_hidden, send1, keep1, affine_part2 = call(
-        hidden_grad_kernel, "shhhvvvvv" + "hvvv",
-        (lengths, low1_hbm, after(da2_hbm, half2), hidden_hbm, st2, rx2, gst2, rx3, affine2),
-        [wide, half, half, ((4 * rows, 2 * width), F32)],
-        [wide, wide, hid, wide, ((frames, 3 * width), BF16), buf, tab, ((width, 3 * width), F32), (3 * rows,), (rows,)], LARGE, flops,
-    )
-    got1 = swap(after(send1, blocks2), "core", 1)
-    part2 = jnp.sum(blocks2.astype(F32), axis=0).astype(BF16)
+    grad_hidden, gs1, send1, affine_part2 = call(
+        hidden_grad_kernel, "svvvvvvvv" + "hvvv",
+        (lengths, low1, after(da2, half2), hidden, st2, rx2, gst2, rx3, affine2),
+        [wide, taps, half, ((4 * rows, 2 * width), F32)], [wide, buf, tab, half_acc, (rows,)], SMALL, flops,
+    )
+    got1 = swap(send1, "core", 1)
+    (keep1,) = call(
+        functools.partial(kernel_grad_kernel, True, PAD), "vv" + "v", (low1, after(gs1, send1)), [half], [half_acc], SMALL,
+    )
     half1 = (got1.astype(F32) + keep1.astype(F32)).astype(BF16)
-    part1 = scatter_sum(half1.reshape(chips, -1, width), "chip")
+    both = jnp.concatenate([h.reshape(chips, count, 1, -1, width) for h in (half2, half1)], axis=2)
+    both = both.reshape(chips, -1, width)
+    grad_hidden = after(grad_hidden, both)
+    both = scatter_sum(both, "chip").reshape(count, -1, width)
 
     da1, gst1, last_part = call(
         first_norm_grad_kernel, "shhhvvvvv" + "hvv",
-        (lengths, after(grad_hidden, half1), kernel1, tokens, st1, rx1, affine1, affine_part2, bias_part),
+        (lengths, grad_hidden, kernel1, tokens, st1, rx1, affine1, affine_part2, bias_part),
         [own, sums, ((4 * rows, 4 * width), BF16)],
         [wide, kernel, own, own, ((frames, width), F32), products, tab, acc, ((4 * rows, 4 * width), F32),
          (1 + 2 * rows,), (rows,)],
         LARGE, flops,
     )
-    both = jnp.concatenate([part2.reshape(count, -1, width), part1.reshape(count, -1, width)], axis=1)
-    both = after(both, da1)
-    last_part = after(last_part, both)
+    last = sum_over_tm(last_part)
+    both = after(both, da1, last)
+    affine_grads, unscattered = last.astype(BF16), both
     both = scatter_sum(both, "tm")
+    scattered = both
     (block_out,) = call(
         block_out_kernel, "shhhv" + "h", (lengths, low2_hbm, after(tokens, both), kernel2, conv2_bias.reshape(1, width)), [own],
         [wide, own, kernel, products, own, (1 + 2 * rows,), (rows,)], LARGE, flops,
     )
-    last = sum_over_tm(last_part)
-    affine_grads = after(last, both).astype(BF16)
     both = spread(both, "tm")
     (input_grad,) = call(
         input_grad_kernel, "shhhvvvvv" + "h", (lengths, out_grad, after(da1, both), tokens, st1, rx1, gst1, last, affine1), [own],
@@ -909,7 +896,7 @@
     ) + lax.dot_general(mine[:, 2 * width :], fc2_weight, (((1,), (1,)), ((), ())), preferred_element_type=F32)
     style_grad = style_grad.reshape(style.shape)
     style_pad = jnp.pad(style, ((0, 0), (0, 1), (0, 0))).reshape(rows * 4, -1)
-    gathered = gather_rows(jnp.concatenate([affine_grads, style_pad], axis=1))
+    gathered = gather_rows(jnp.concatenate([affine_grads, style_pad], axis=1), unscattered, scattered)
     both = spread(after(both, block_out, gathered), "chip")
     fc_shape, bias_shape = ((style.shape[2], 2 * width), F32), ((1, 2 * width), F32)
     fc1_grad, fc2_grad, fc1_bias_grad, fc2_bias_grad, conv2_bias_grad = call(

time: 155 us -> 148 us (0.955)
  starting transfers between devices: 41.1 us -> 37.7 us
  waiting for transfers between devices: 37.4 us -> 35.5 us
    ppermute x18, waiting for transfers between devices: 23.4 us -> 16.3 us  [swap(): lax.ppermute(x, axis, [(i, i ^ bit) for i in range(lax.axis_size(axis))])]
    all_to_all x2, waiting for transfers between devices: 0.01 us -> 6.39 us  [scatter_sum(): lax.all_to_all(blocks, axis, 0, 0).astype(F32)]
    all_to_all x1 -> x0, starting transfers between devices: 3.67 us -> none  [per_device(): blocks2 = lax.all_to_all(half2.reshape(chips, -1, width), 'chip', 0, 0)]
    pallas_call x13 -> x14, Pallas kernels: 66.8 us -> 66.4 us  [call(): pl.pallas_call(kernel, out_shape=shapes, in_specs=specs, out_specs=out_sp...]
  transfers between devices with their start and end apart: 23 -> 22, of which waited for: 10 -> 11; matrix products, arithmetic and copies ran while one was open for 2% -> 2% of each run, Pallas kernels for 31% -> 27%
where the time goes in v3:
time: 148 us
  Pallas kernels  66.4 us (45%)
  starting transfers between devices  37.7 us (25%)
  waiting for transfers between devices  35.5 us (24%)
  local copies, waits for them, and re-layouts  3.58 us (2%)
  other arithmetic  2.99 us (2%)
    pallas_call x14, Pallas kernels, call(): pl.pallas_call(kernel, out_shape=shapes, in_specs=specs, out_specs=out_sp...  66.4 us
    ppermute x18, starting transfers between devices, swap(): lax.ppermute(x, axis, [(i, i ^ bit) for i in range(lax.axis_size(axis))])  23 us
    ppermute x18, waiting for transfers between devices, swap(): lax.ppermute(x, axis, [(i, i ^ bit) for i in range(lax.axis_size(axis))])  16.3 us
    all_to_all x2, waiting for transfers between devices, spread(): lax.all_to_all(jnp.broadcast_to(block[None], (lax.axis_size(axis), *block...  12.8 us
    all_to_all x2, starting transfers between devices, scatter_sum(): lax.all_to_all(blocks, axis, 0, 0).astype(F32)  7.71 us
    all_to_all x2, starting transfers between devices, spread(): lax.all_to_all(jnp.broadcast_to(block[None], (lax.axis_size(axis), *block...  7.02 us
    all_to_all x2, waiting for transfers between devices, scatter_sum(): lax.all_to_all(blocks, axis, 0, 0).astype(F32)  6.39 us
  transfers between devices with their start and end apart: 22, of which 11 were waited for; matrix products, arithmetic and copies ran while one was open for 2% of the time, Pallas kernels for 27%

profile of v3, /device:TPU:0, one launch (start us, length us, event | category | flops | bytes accessed | tf_op | source)
XLA Modules:
  0.0 148.1 jit_solution(17962019761032404194)
XLA Ops:
  1.4 3.2 %shard_map.186 = (bf16[4,512,512]{2,1,0:T(8,128)(2,1)S(1)}, bf16[1536,512]{1,0:T(8,128)(2,1)S(1)}, f32[4,8,512]{2,1,0:T(8,128)S(1)}, f32[24,512]{1,0:T(8,128)S(1...) custom-call(s32[4,3]{1,0:T(4,128)S(1)} %copy-done.1, bf16[4,512,512]{2,1,0:T(8,128)(2,1)} %tok_hbm.6, ...), custom_call_target="tpu_custom_call" | custom-call | bytes 8388608 | tf_op jit(solution)/shard_map/pallas_call | solution.py:761
  4.6 3.0 %collective-permute-start = (f32[24,512]{1,0:T(8,128)S(1)}, f32[24,512]{1,0:T(8,128)S(1)}, u32[]{:S(2)}, u32[]{:S(2)}) collective-permute-start(f32[24,512]{1,0:T(8,128)S(1)} %get-tuple-element.70), channel_id=1, source_target_pairs={{0,1},{1,0},{2,3},{3,2},{4,5},{5,4},{6,7},{7,6},{8,9},{9,8},{10,11... | collective-permute-start | bytes 147464 | tf_op jit(solution)/shard_map/ppermute | solution.py:790
  7.6 2.8 %collective-permute-start.1 = (f32[24,512]{1,0:T(8,128)S(1)}, f32[24,512]{1,0:T(8,128)S(1)}, u32[]{:S(2)}, u32[]{:S(2)}) collective-permute-start(f32[24,512]{1,0:T(8,128)S(1)} %get-tuple-element.71), channel_id=1, source_target_pairs={{0,2},{1,3},{2,0},{3,1},{4,6},{5,7},{6,4},{7,5},{8,10},{9,11},{10,... | collective-permute-start | bytes 147464 | tf_op jit(solution)/shard_map/ppermute | solution.py:790
  10.8 2.8 %collective-permute-done.1.rx_ref_2_ = f32[24,512]{1,0:T(8,128)S(1)} collective-permute-done((f32[24,512]{1,0:T(8,128)S(1)}, f32[24,512]{1,0:T(8,128)S(1)}, u32[]{:S(2)}, u32[]{:S(2)}) %collective-permute-start.1) | collective-permute-done | bytes 49184 | tf_op jit(solution)/shard_map/ppermute | solution.py:790
  13.6 2.8 %collective-permute-done.2.rx_ref_3_ = f32[24,512]{1,0:T(8,128)S(1)} collective-permute-done((f32[24,512]{1,0:T(8,128)S(1)}, f32[24,512]{1,0:T(8,128)S(1)}, u32[]{:S(2)}, u32[]{:S(2)}) %collective-permute-start.2) | collective-permute-done | bytes 49184 | tf_op jit(solution)/shard_map/ppermute | solution.py:790
  16.3 7.6 %shard_map.187 = (bf16[4,544,512]{2,1,0:T(8,128)(2,1)S(1)}, f32[4,544,512]{2,1,0:T(8,128)S(1)}, f32[4,8,512]{2,1,0:T(8,128)S(1)}, f32[8,512]{1,0:T(8,128)S(1)}, ...) custom-call(s32[4,3]{1,0:T(4,128)S(1)} %copy-done.1, bf16[4,512,512]{2,1,0:T(8,128)(2,1)S(1)} %get-tuple-element.67.tok_ref, ...), custom_call_target="tpu_custom_call" | custom-call | flops 3221225472 | bytes 8388608 | tf_op jit(solution)/shard_map/pallas_call | solution.py:761
  25.7 2.7 %collective-permute-start.5 = (f32[8,512]{1,0:T(8,128)S(1)}, f32[8,512]{1,0:T(8,128)S(1)}, u32[]{:S(2)}, u32[]{:S(2)}) collective-permute-start(f32[8,512]{1,0:T(8,128)S(1)} %get-tuple-element.79.rx_ref_0_), channel_id=1, source_target_pairs={{0,3},{1,2},{2,1},{3,0},{4,7},{5,6},{6,5},{7,4},{8,11},{9,10},{10,... | collective-permute-start | bytes 49160 | tf_op jit(solution)/shard_map/ppermute | solution.py:790
  28.4 7.4 %shard_map.188 = (bf16[4,512,1536]{2,1,0:T(8,128)(2,1)S(1)}, bf16[4,544,512]{2,1,0:T(8,128)(2,1)S(1)}, f32[8,512]{1,0:T(8,128)S(1)}) custom-call(s32[4,3]{1,0:T(4,128)S(1)} %copy-done.1, bf16[4,512,512]{2,1,0:T(8,128)(2,1)S(1)} %get-tuple-element.75.og_ref, f32[24,512]{1,0:T(8,128)S(1)} %get-tuple-element.69.rx_ref_0_, ...), custom_call_target="tpu_custom_call" | custom-call | flops 3221225472 | bytes 8388608 | tf_op jit(solution)/shard_map/pallas_call | solution.py:761
  35.9 4.2 %shard_map.189 = (bf16[4,544,512]{2,1,0:T(8,128)(2,1)S(1)}, bf16[4,544,512]{2,1,0:T(8,128)(2,1)S(1)}, f32[4,8,512]{2,1,0:T(8,128)S(1)}, f32[8,512]{1,0:T(8,128)S(1)}) custom-call(s32[4,3]{1,0:T(4,128)S(1)} %copy-done.1, f32[4,544,512]{2,1,0:T(8,128)S(1)} %get-tuple-element.74.hid_ref, bf16[4,544,512]{2,1,0:T(8,128)(2,1)S(1)} %get-tuple-element.77.q_ref, ...), custom_call_target="tpu_custom_call" | custom-call | bytes 8388608 | tf_op jit(solution)/shard_map/pallas_call | solution.py:761
  40.1 2.6 %shard_map.190 = (bf16[768,512]{1,0:T(8,128)(2,1)S(1)}, bf16[4,544,512]{2,1,0:T(8,128)(2,1)}) custom-call(bf16[4,544,512]{2,1,0:T(8,128)(2,1)S(1)} %get-tuple-element.80.low_ref, bf16[4,512,1536]{2,1,0:T(8,128)(2,1)S(1)} %get-tuple-element.84.gs_ref), custom_call_target="tpu_custom_call" | custom-call | bytes 8388608 | tf_op jit(solution)/shard_map/pallas_call | solution.py:761
  42.8 1.9 %collective-permute-start.8 = (f32[8,512]{1,0:T(8,128)S(1)}, f32[8,512]{1,0:T(8,128)S(1)}, u32[]{:S(2)}, u32[]{:S(2)}) collective-permute-start(f32[8,512]{1,0:T(8,128)S(1)} %get-tuple-element.85.grx_ref_0_), channel_id=1, source_target_pairs={{0,2},{1,3},{2,0},{3,1},{4,6},{5,7},{6,4},{7,5},{8,10},{9,11},{10,... | collective-permute-start | bytes 49160 | tf_op jit(solution)/shard_map/ppermute | solution.py:790
  44.7 2.5 %collective-permute-start.9 = (f32[8,512]{1,0:T(8,128)S(1)}, f32[8,512]{1,0:T(8,128)S(1)}, u32[]{:S(2)}, u32[]{:S(2)}) collective-permute-start(f32[8,512]{1,0:T(8,128)S(1)} %get-tuple-element.85.grx_ref_0_), channel_id=1, source_target_pairs={{0,3},{1,2},{2,1},{3,0},{4,7},{5,6},{6,5},{7,4},{8,11},{9,10},{10,... | collective-permute-start | bytes 49160 | tf_op jit(solution)/shard_map/ppermute | solution.py:790
  47.2 2.5 %shard_map.191 = bf16[768,512]{1,0:T(8,128)(2,1)S(1)} custom-call(bf16[4,544,512]{2,1,0:T(8,128)(2,1)S(1)} %get-tuple-element.80.low_ref, bf16[4,512,1536]{2,1,0:T(8,128)(2,1)S(1)} %get-tuple-element.84.gs_ref), custom_call_target="tpu_custom_call" | custom-call | bytes 8388608 | tf_op jit(solution)/shard_map/pallas_call | solution.py:761
  50.5 6.5 %shard_map.192 = (bf16[4,544,512]{2,1,0:T(8,128)(2,1)}, bf16[4,512,1536]{2,1,0:T(8,128)(2,1)S(1)}, bf16[768,512]{1,0:T(8,128)(2,1)S(1)}, f32[16,1024]{1,0:T(8,128)S(1)}) custom-call(s32[4,3]{1,0:T(4,128)S(1)} %copy-done.1, bf16[4,544,512]{2,1,0:T(8,128)(2,1)S(1)} %get-tuple-element.87.low_ref, bf16[4,544,512]{2,1,0:T(8,128)(2,1)S(1)} %get-tuple-element.89.da_ref, ...), custom_call_target="tpu_custom_call" | custom-call | flops 3221225472 | bytes 8388608 | tf_op jit(solution)/shard_map/pallas_call | solution.py:761
  57.1 2.5 %shard_map.193 = bf16[768,512]{1,0:T(8,128)(2,1)S(1)} custom-call(bf16[4,544,512]{2,1,0:T(8,128)(2,1)S(1)} %get-tuple-element.87.low_ref, bf16[4,512,1536]{2,1,0:T(8,128)(2,1)S(1)} %get-tuple-element.93.gs_ref), custom_call_target="tpu_custom_call" | custom-call | bytes 8388608 | tf_op jit(solution)/shard_map/pallas_call | solution.py:761
  61.1 4.3 %all-to-all-start = ((bf16[4,384,512]{2,1,0:T(8,128)(2,1)}), bf16[4,384,512]{2,1,0:T(8,128)(2,1)S(1)}, u32[]{:S(2)}, u32[]{:S(2)}) async-start(bf16[4,384,512]{2,1,0:T(8,128)(2,1)} %bitcast.26), calls=%async_computation | async-start | bytes 3145728 | tf_op jit(solution)/shard_map/all_to_all | solution.py:782
  65.4 11.0 %shard_map.194 = (bf16[4,512,512]{2,1,0:T(8,128)(2,1)}, f32[4,8,512]{2,1,0:T(8,128)S(1)}, bf16[16,2048]{1,0:T(8,128)(2,1)S(1)}) custom-call(s32[4,3]{1,0:T(4,128)S(1)} %copy-done.2, bf16[4,544,512]{2,1,0:T(8,128)(2,1)} %get-tuple-element.95.g_hbm, bf16[1536,512]{1,0:T(8,128)(2,1)} %bitcast.30, bf16[4,512,512]{2,1,0:T(8,128)(2,1)} %tok_hbm.6, ...), custom_call_target="tpu_custom_call" | custom-call | flops 3221225472 | bytes 8388608 | tf_op jit(solution)/shard_map/pallas_call | solution.py:761
  76.4 2.8 %collective-permute-start.13 = (bf16[16,2048]{1,0:T(8,128)(2,1)S(1)}, bf16[16,2048]{1,0:T(8,128)(2,1)S(1)}, u32[]{:S(2)}, u32[]{:S(2)}) collective-permute-start(bf16[16,2048]{1,0:T(8,128)(2,1)S(1)} %get-tuple-element.99), channel_id=1, source_target_pairs={{0,3},{1,2},{2,1},{3,0},{4,7},{5,6},{6,5},{7,4},{8,11},{9,10},{10,... | collective-permute-start | bytes 196616 | tf_op jit(solution)/shard_map/ppermute | solution.py:790
  80.9 2.4 %collective-permute-done.13 = bf16[16,2048]{1,0:T(8,128)(2,1)S(1)} collective-permute-done((bf16[16,2048]{1,0:T(8,128)(2,1)S(1)}, bf16[16,2048]{1,0:T(8,128)(2,1)S(1)}, u32[]{:S(2)}, u32[]{:S(2)}) %collective-permute-start.13) | collective-permute-done | bytes 65568 | tf_op jit(solution)/shard_map/ppermute | solution.py:790
  83.3 2.1 %collective-permute-done.12 = bf16[16,2048]{1,0:T(8,128)(2,1)S(1)} collective-permute-done((bf16[16,2048]{1,0:T(8,128)(2,1)S(1)}, bf16[16,2048]{1,0:T(8,128)(2,1)S(1)}, u32[]{:S(2)}, u32[]{:S(2)}) %collective-permute-start.12) | collective-permute-done | bytes 65568 | tf_op jit(solution)/shard_map/ppermute | solution.py:790
  87.2 3.5 %all-to-all-start.1 = ((bf16[4,96,512]{2,1,0:T(8,128)(2,1)}), bf16[4,96,512]{2,1,0:T(8,128)(2,1)S(1)}, u32[]{:S(2)}, u32[]{:S(2)}) async-start(bf16[4,96,512]{2,1,0:T(8,128)(2,1)} %bitcast.9), calls=%async_computation.1 | async-start | bytes 786432 | tf_op jit(solution)/shard_map/all_to_all | solution.py:782
  90.7 1.9 %collective-permute-start.15 = (bf16[32,2176]{1,0:T(8,128)(2,1)S(1)}, bf16[32,2176]{1,0:T(8,128)(2,1)S(1)}, u32[]{:S(2)}, u32[]{:S(2)}) collective-permute-start(bf16[32,2176]{1,0:T(8,128)(2,1)S(1)} %pad_maximum_fusion.2), channel_id=1, source_target_pairs={{0,8},{8,0},{16,24},{24,16},{1,9},{9,1},{17,25},{25,17},{2,10},{10... | collective-permute-start | bytes 417800 | tf_op jit(solution)/shard_map/ppermute | solution.py:790
  92.6 4.2 %collective-permute-done.15 = bf16[32,2176]{1,0:T(8,128)(2,1)S(1)} collective-permute-done((bf16[32,2176]{1,0:T(8,128)(2,1)S(1)}, bf16[32,2176]{1,0:T(8,128)(2,1)S(1)}, u32[]{:S(2)}, u32[]{:S(2)}) %collective-permute-start.15) | collective-permute-done | bytes 139296 | tf_op jit(solution)/shard_map/ppermute | solution.py:790
  96.8 6.4 %all-to-all-done.1 = bf16[4,96,512]{2,1,0:T(8,128)(2,1)S(1)} async-done(((bf16[4,96,512]{2,1,0:T(8,128)(2,1)}), bf16[4,96,512]{2,1,0:T(8,128)(2,1)S(1)}, u32[]{:S(2)}, u32[]{:S(2)}) %all-to-all-start.1) | async-done | bytes 393248 | tf_op jit(solution)/shard_map/all_to_all | solution.py:782
  105.8 3.5 %all-to-all-start.2 = ((bf16[4,96,512]{2,1,0:T(8,128)(2,1)}), bf16[4,96,512]{2,1,0:T(8,128)(2,1)S(1)}, u32[]{:S(2)}, u32[]{:S(2)}) async-start(bf16[4,96,512]{2,1,0:T(8,128)(2,1)} %broadcast_in_dim.4), calls=%async_computation.2 | async-start | bytes 786432 | tf_op jit(solution)/shard_map/all_to_all | solution.py:786
  109.3 8.5 %shard_map.195 = bf16[4,512,512]{2,1,0:T(8,128)(2,1)} custom-call(s32[4,3]{1,0:T(4,128)S(1)} %copy-done.2, bf16[4,544,512]{2,1,0:T(8,128)(2,1)} %get-tuple-element.82.low_hbm, bf16[4,512,512]{2,1,0:T(8,128)(2,1)} %tok_hbm.6, bf16[1536,512]{1,0:T(8,128)(2,1)} %bitcast.35, bf16[1,512]{1,0:T(2,128)(2,1)S(1)} %reshape.75.bias_ref), custom_call_target="tpu_custom_call" | custom-call | flops 3221225472 | bytes 8388608 | tf_op jit(solution)/shard_map/pallas_call | solution.py:761
  117.8 2.7 %all-to-all-done.2 = bf16[4,96,512]{2,1,0:T(8,128)(2,1)S(1)} async-done(((bf16[4,96,512]{2,1,0:T(8,128)(2,1)}), bf16[4,96,512]{2,1,0:T(8,128)(2,1)S(1)}, u32[]{:S(2)}, u32[]{:S(2)}) %all-to-all-start.2) | async-done | bytes 393248 | tf_op jit(solution)/shard_map/all_to_all | solution.py:786
  121.8 3.6 %all-to-all-start.3 = ((bf16[4,4,96,512]{3,2,1,0:T(8,128)(2,1)}), bf16[4,4,96,512]{3,2,1,0:T(8,128)(2,1)S(1)}, u32[]{:S(2)}, u32[]{:S(2)}) async-start(bf16[4,4,96,512]{3,2,1,0:T(8,128)(2,1)} %broadcast_in_dim.5), calls=%async_computation.3 | async-start | bytes 3145728 | tf_op jit(solution)/shard_map/all_to_all | solution.py:786
  125.8 2.0 %shard_map.197 = (f32[128,1024]{1,0:T(8,128)}, f32[128,1024]{1,0:T(8,128)}, f32[1,1024]{1,0:T(1,128)}, f32[1,1024]{1,0:T(1,128)}, f32[1,512]{1,0:T(1,128)}) custom-call(bf16[128,2176]{1,0:T(8,128)(2,1)S(1)} %constant_dynamic-update-slice_fusion.all_ref), custom_call_target="tpu_custom_call" | custom-call | bytes 8388608 | tf_op jit(solution)/shard_map/pallas_call | solution.py:761
  127.8 4.8 %shard_map.196 = bf16[4,512,512]{2,1,0:T(8,128)(2,1)} custom-call(s32[4,3]{1,0:T(4,128)S(1)} %copy-done.2, bf16[4,512,512]{2,1,0:T(8,128)(2,1)} %og_hbm.5, bf16[4,512,512]{2,1,0:T(8,128)(2,1)} %get-tuple-element.105.da_hbm, bf16[4,512,512]{2,1,0:T(8,128)(2,1)} %tok_hbm.6, f32[4,8,512]{2,1,0:T(8,128)S(1)} %get-tuple-element.68.st_ref, ...), custom_call_target="tpu_custom_call" | custom-call | bytes 8388608 | tf_op jit(solution)/shard_map/pallas_call | solution.py:761
  132.6 10.1 %all-to-all-done.3 = bf16[4,4,96,512]{3,2,1,0:T(8,128)(2,1)S(1)} async-done(((bf16[4,4,96,512]{3,2,1,0:T(8,128)(2,1)}), bf16[4,4,96,512]{3,2,1,0:T(8,128)(2,1)S(1)}, u32[]{:S(2)}, u32[]{:S(2)}) %all-to-all-start.3) | async-done | bytes 1572896 | tf_op jit(solution)/shard_map/all_to_all | solution.py:786
  142.8 1.8 %shard_map.198 = (f32[3,512,512]{2,1,0:T(8,128)}, f32[3,512,512]{2,1,0:T(8,128)}) custom-call(bf16[4,4,2,48,512]{4,3,2,1,0:T(8,128)(2,1)S(1)} %bitcast.25), custom_call_target="tpu_custom_call" | custom-call | bytes 8388608 | tf_op jit(solution)/shard_map/pallas_call | solution.py:761
  (68 shorter events, 16.5 us)
Async XLA Ops:
  0.6 9.8 %copy-start = (bf16[128,1024]{1,0:T(8,128)(2,1)S(1)}, bf16[128,1024]{1,0:T(8,128)(2,1)}, u32[]{:S(2)}) copy-start(bf16[128,1024]{1,0:T(8,128)(2,1)} %param.14) | copy-start | bytes 786436
  0.7 0.7 copy-start.1
  1.4 9.0 %copy-start.5 = (bf16[1024]{0:T(1024)(128)(2,1)S(1)}, bf16[1024]{0:T(1024)(128)(2,1)}, u32[]{:S(2)}) copy-start(bf16[1024]{0:T(1024)(128)(2,1)} %param.15) | copy-start | bytes 6148
  1.4 9.0 %copy-start.6 = (bf16[1024]{0:T(1024)(128)(2,1)S(1)}, bf16[1024]{0:T(1024)(128)(2,1)}, u32[]{:S(2)}) copy-start(bf16[1024]{0:T(1024)(128)(2,1)} %param.18) | copy-start | bytes 6148
  1.4 9.1 %copy-start.4 = (bf16[4,3,128]{2,0,1:T(4,128)(2,1)S(1)}, bf16[4,3,128]{2,0,1:T(4,128)(2,1)}, u32[]{:S(2)}) copy-start(bf16[4,3,128]{2,0,1:T(4,128)(2,1)} %param.13) | copy-start | bytes 9220
  1.4 9.2 %copy-start.3 = (bf16[128,1024]{1,0:T(8,128)(2,1)S(1)}, bf16[128,1024]{1,0:T(8,128)(2,1)}, u32[]{:S(2)}) copy-start(bf16[128,1024]{1,0:T(8,128)(2,1)} %param.17) | copy-start | bytes 786436
  4.6 6.2 %collective-permute-start = (f32[24,512]{1,0:T(8,128)S(1)}, f32[24,512]{1,0:T(8,128)S(1)}, u32[]{:S(2)}, u32[]{:S(2)}) collective-permute-start(f32[24,512]{1,0:T(8,128)S(1)} %get-tuple-element.70), channel_id=1, source_target_pairs={{0,1},{1,0},{2,3},{3,2},{4,5},{5,4},{6,7},{7,6},{8,9},{9,8},{10,11... | collective-permute-start | bytes 147464 | tf_op jit(solution)/shard_map/ppermute | solution.py:790
  7.6 5.9 %collective-permute-start.1 = (f32[24,512]{1,0:T(8,128)S(1)}, f32[24,512]{1,0:T(8,128)S(1)}, u32[]{:S(2)}, u32[]{:S(2)}) collective-permute-start(f32[24,512]{1,0:T(8,128)S(1)} %get-tuple-element.71), channel_id=1, source_target_pairs={{0,2},{1,3},{2,0},{3,1},{4,6},{5,7},{6,4},{7,5},{8,10},{9,11},{10,... | collective-permute-start | bytes 147464 | tf_op jit(solution)/shard_map/ppermute | solution.py:790
  10.4 5.9 %collective-permute-start.2 = (f32[24,512]{1,0:T(8,128)S(1)}, f32[24,512]{1,0:T(8,128)S(1)}, u32[]{:S(2)}, u32[]{:S(2)}) collective-permute-start(f32[24,512]{1,0:T(8,128)S(1)} %get-tuple-element.72), channel_id=1, source_target_pairs={{0,3},{1,2},{2,1},{3,0},{4,7},{5,6},{6,5},{7,4},{8,11},{9,10},{10,... | collective-permute-start | bytes 147464 | tf_op jit(solution)/shard_map/ppermute | solution.py:790
  24.0 11.9 %collective-permute-start.3 = (f32[8,512]{1,0:T(8,128)S(1)}, f32[8,512]{1,0:T(8,128)S(1)}, u32[]{:S(2)}, u32[]{:S(2)}) collective-permute-start(f32[8,512]{1,0:T(8,128)S(1)} %get-tuple-element.79.rx_ref_0_), channel_id=1, source_target_pairs={{0,1},{1,0},{2,3},{3,2},{4,5},{5,4},{6,7},{7,6},{8,9},{9,8},{10,11... | collective-permute-start | bytes 49160 | tf_op jit(solution)/shard_map/ppermute | solution.py:790
  24.0 11.8 %collective-permute-start.4 = (f32[8,512]{1,0:T(8,128)S(1)}, f32[8,512]{1,0:T(8,128)S(1)}, u32[]{:S(2)}, u32[]{:S(2)}) collective-permute-start(f32[8,512]{1,0:T(8,128)S(1)} %get-tuple-element.79.rx_ref_0_), channel_id=1, source_target_pairs={{0,2},{1,3},{2,0},{3,1},{4,6},{5,7},{6,4},{7,5},{8,10},{9,11},{10,... | collective-permute-start | bytes 49160 | tf_op jit(solution)/shard_map/ppermute | solution.py:790
  25.7 10.2 %collective-permute-start.5 = (f32[8,512]{1,0:T(8,128)S(1)}, f32[8,512]{1,0:T(8,128)S(1)}, u32[]{:S(2)}, u32[]{:S(2)}) collective-permute-start(f32[8,512]{1,0:T(8,128)S(1)} %get-tuple-element.79.rx_ref_0_), channel_id=1, source_target_pairs={{0,3},{1,2},{2,1},{3,0},{4,7},{5,6},{6,5},{7,4},{8,11},{9,10},{10,... | collective-permute-start | bytes 49160 | tf_op jit(solution)/shard_map/ppermute | solution.py:790
  42.7 7.6 %collective-permute-start.6 = (bf16[768,512]{1,0:T(8,128)(2,1)S(1)}, bf16[768,512]{1,0:T(8,128)(2,1)S(1)}, u32[]{:S(2)}, u32[]{:S(2)}) collective-permute-start(bf16[768,512]{1,0:T(8,128)(2,1)S(1)} %get-tuple-element.83), channel_id=1, source_target_pairs={{0,4},{4,0},{1,5},{5,1},{2,6},{6,2},{3,7},{7,3},{8,12},{12,8},{9,1... | collective-permute-start | bytes 2359304 | tf_op jit(solution)/shard_map/ppermute | solution.py:790
  42.8 7.0 %collective-permute-start.7 = (f32[8,512]{1,0:T(8,128)S(1)}, f32[8,512]{1,0:T(8,128)S(1)}, u32[]{:S(2)}, u32[]{:S(2)}) collective-permute-start(f32[8,512]{1,0:T(8,128)S(1)} %get-tuple-element.85.grx_ref_0_), channel_id=1, source_target_pairs={{0,1},{1,0},{2,3},{3,2},{4,5},{5,4},{6,7},{7,6},{8,9},{9,8},{10,11... | collective-permute-start | bytes 49160 | tf_op jit(solution)/shard_map/ppermute | solution.py:790
  42.8 6.9 %collective-permute-start.8 = (f32[8,512]{1,0:T(8,128)S(1)}, f32[8,512]{1,0:T(8,128)S(1)}, u32[]{:S(2)}, u32[]{:S(2)}) collective-permute-start(f32[8,512]{1,0:T(8,128)S(1)} %get-tuple-element.85.grx_ref_0_), channel_id=1, source_target_pairs={{0,2},{1,3},{2,0},{3,1},{4,6},{5,7},{6,4},{7,5},{8,10},{9,11},{10,... | collective-permute-start | bytes 49160 | tf_op jit(solution)/shard_map/ppermute | solution.py:790
  44.7 5.5 %collective-permute-start.9 = (f32[8,512]{1,0:T(8,128)S(1)}, f32[8,512]{1,0:T(8,128)S(1)}, u32[]{:S(2)}, u32[]{:S(2)}) collective-permute-start(f32[8,512]{1,0:T(8,128)S(1)} %get-tuple-element.85.grx_ref_0_), channel_id=1, source_target_pairs={{0,3},{1,2},{2,1},{3,0},{4,7},{5,6},{6,5},{7,4},{8,11},{9,10},{10,... | collective-permute-start | bytes 49160 | tf_op jit(solution)/shard_map/ppermute | solution.py:790
  57.0 2.6 %collective-permute-start.10 = (bf16[768,512]{1,0:T(8,128)(2,1)S(1)}, bf16[768,512]{1,0:T(8,128)(2,1)S(1)}, u32[]{:S(2)}, u32[]{:S(2)}) collective-permute-start(bf16[768,512]{1,0:T(8,128)(2,1)S(1)} %get-tuple-element.91), channel_id=1, source_target_pairs={{0,4},{4,0},{1,5},{5,1},{2,6},{6,2},{3,7},{7,3},{8,12},{12,8},{9,1... | collective-permute-start | bytes 2359304 | tf_op jit(solution)/shard_map/ppermute | solution.py:790
  61.1 4.3 %copy-start.2 = (s32[4,3]{1,0:T(4,128)S(1)}, s32[4,3]{1,0:T(4,128)}, u32[]{:S(2)}) copy-start(s32[4,3]{1,0:T(4,128)} %len_ref.15) | copy-start | bytes 148
  61.1 25.0 %all-to-all-start = ((bf16[4,384,512]{2,1,0:T(8,128)(2,1)}), bf16[4,384,512]{2,1,0:T(8,128)(2,1)S(1)}, u32[]{:S(2)}, u32[]{:S(2)}) async-start(bf16[4,384,512]{2,1,0:T(8,128)(2,1)} %bitcast.26), calls=%async_computation | async-start | bytes 3145728 | tf_op jit(solution)/shard_map/all_to_all | solution.py:782
  76.4 16.2 %copy-start.7 = (bf16[512]{0:T(512)(128)(2,1)S(1)}, bf16[512]{0:T(512)(128)(2,1)}, u32[]{:S(2)}) copy-start(bf16[512]{0:T(512)(128)(2,1)} %param.20) | copy-start | bytes 3076
  76.4 6.9 %collective-permute-start.13 = (bf16[16,2048]{1,0:T(8,128)(2,1)S(1)}, bf16[16,2048]{1,0:T(8,128)(2,1)S(1)}, u32[]{:S(2)}, u32[]{:S(2)}) collective-permute-start(bf16[16,2048]{1,0:T(8,128)(2,1)S(1)} %get-tuple-element.99), channel_id=1, source_target_pairs={{0,3},{1,2},{2,1},{3,0},{4,7},{5,6},{6,5},{7,4},{8,11},{9,10},{10,... | collective-permute-start | bytes 196616 | tf_op jit(solution)/shard_map/ppermute | solution.py:790
  79.2 6.1 %collective-permute-start.12 = (bf16[16,2048]{1,0:T(8,128)(2,1)S(1)}, bf16[16,2048]{1,0:T(8,128)(2,1)S(1)}, u32[]{:S(2)}, u32[]{:S(2)}) collective-permute-start(bf16[16,2048]{1,0:T(8,128)(2,1)S(1)} %get-tuple-element.99), channel_id=1, source_target_pairs={{0,1},{1,0},{2,3},{3,2},{4,5},{5,4},{6,7},{7,6},{8,9},{9,8},{10,11... | collective-permute-start | bytes 196616 | tf_op jit(solution)/shard_map/ppermute | solution.py:790
  79.2 6.7 %collective-permute-start.11 = (bf16[16,2048]{1,0:T(8,128)(2,1)S(1)}, bf16[16,2048]{1,0:T(8,128)(2,1)S(1)}, u32[]{:S(2)}, u32[]{:S(2)}) collective-permute-start(bf16[16,2048]{1,0:T(8,128)(2,1)S(1)} %get-tuple-element.99), channel_id=1, source_target_pairs={{0,2},{1,3},{2,0},{3,1},{4,6},{5,7},{6,4},{7,5},{8,10},{9,11},{10,... | collective-permute-start | bytes 196616 | tf_op jit(solution)/shard_map/ppermute | solution.py:790
  86.0 4.6 %collective-permute-start.14 = (bf16[16,2176]{1,0:T(8,128)(2,1)S(1)}, bf16[16,2176]{1,0:T(8,128)(2,1)S(1)}, u32[]{:S(2)}, u32[]{:S(2)}) collective-permute-start(bf16[16,2176]{1,0:T(8,128)(2,1)S(1)} %pad_maximum_fusion.3), channel_id=1, source_target_pairs={{0,4},{4,0},{1,5},{5,1},{2,6},{6,2},{3,7},{7,3},{8,12},{12,8},{9,1... | collective-permute-start | bytes 208904 | tf_op jit(solution)/shard_map/ppermute | solution.py:790
  87.2 16.0 %all-to-all-start.1 = ((bf16[4,96,512]{2,1,0:T(8,128)(2,1)}), bf16[4,96,512]{2,1,0:T(8,128)(2,1)S(1)}, u32[]{:S(2)}, u32[]{:S(2)}) async-start(bf16[4,96,512]{2,1,0:T(8,128)(2,1)} %bitcast.9), calls=%async_computation.1 | async-start | bytes 786432 | tf_op jit(solution)/shard_map/all_to_all | solution.py:782
  90.7 6.1 %collective-permute-start.15 = (bf16[32,2176]{1,0:T(8,128)(2,1)S(1)}, bf16[32,2176]{1,0:T(8,128)(2,1)S(1)}, u32[]{:S(2)}, u32[]{:S(2)}) collective-permute-start(bf16[32,2176]{1,0:T(8,128)(2,1)S(1)} %pad_maximum_fusion.2), channel_id=1, source_target_pairs={{0,8},{8,0},{16,24},{24,16},{1,9},{9,1},{17,25},{25,17},{2,10},{10... | collective-permute-start | bytes 417800 | tf_op jit(solution)/shard_map/ppermute | solution.py:790
  103.3 14.5 %collective-permute-start.16 = (bf16[64,2176]{1,0:T(8,128)(2,1)S(1)}, bf16[64,2176]{1,0:T(8,128)(2,1)S(1)}, u32[]{:S(2)}, u32[]{:S(2)}) collective-permute-start(bf16[64,2176]{1,0:T(8,128)(2,1)S(1)} %pad_maximum_fusion.1), channel_id=1, source_target_pairs={{0,16},{8,24},{16,0},{24,8},{1,17},{9,25},{17,1},{25,9},{2,18},{10... | collective-permute-start | bytes 835592 | tf_op jit(solution)/shard_map/ppermute | solution.py:790
  105.8 14.7 %all-to-all-start.2 = ((bf16[4,96,512]{2,1,0:T(8,128)(2,1)}), bf16[4,96,512]{2,1,0:T(8,128)(2,1)S(1)}, u32[]{:S(2)}, u32[]{:S(2)}) async-start(bf16[4,96,512]{2,1,0:T(8,128)(2,1)} %broadcast_in_dim.4), calls=%async_computation.2 | async-start | bytes 786432 | tf_op jit(solution)/shard_map/all_to_all | solution.py:786
  121.8 20.9 %all-to-all-start.3 = ((bf16[4,4,96,512]{3,2,1,0:T(8,128)(2,1)}), bf16[4,4,96,512]{3,2,1,0:T(8,128)(2,1)S(1)}, u32[]{:S(2)}, u32[]{:S(2)}) async-start(bf16[4,4,96,512]{3,2,1,0:T(8,128)(2,1)} %broadcast_in_dim.5), calls=%async_computation.3 | async-start | bytes 3145728 | tf_op jit(solution)/shard_map/all_to_all | solution.py:786
  142.8 3.4 %collective-permute-start.17 = (bf16[4,4,2,48,512]{4,3,2,1,0:T(8,128)(2,1)S(1)}, bf16[4,4,2,48,512]{4,3,2,1,0:T(8,128)(2,1)S(1)}, u32[]{:S(2)}, u32[]{:S(2)}) collective-permute-start(bf16[4,4,2,48,512]{4,3,2,1,0:T(8,128)(2,1)S(1)} %bitcast.24), channel_id=1, source_target_pairs={{0,4},{4,0},{1,5},{5,1},{2,6},{6,2},{3,7},{7,3},{8,12},{12,8},{9,1... | collective-permute-start | bytes 4718600 | tf_op jit(solution)/shard_map/ppermute | solution.py:790

commit v4 on v3

--- a/solution.py
+++ b/solution.py
@@ -825,7 +825,7 @@
     flops = 2 * rows * frames * 3 * width * width
 
     tok, w1, st1, msg1 = call(
-        token_sums_kernel, "shhh" + "vvvv", (lengths, tokens, out_grad, kernel1),
+        token_sums_kernel, "shhh" + "vvvv", (pltpu.with_memory_space_constraint(lengths, pltpu.HBM), tokens, out_grad, kernel1),
         [own, kernel, sums, [((EDGE, width), F32)] * count],
         [((rows, PAD, width), BF16), ((rows, PAD, width), BF16), acc, (3,), (rows,)], SMALL,
     )

time: 148 us -> 148 us (level)
  transfers between devices with their start and end apart: 22 -> 22, of which waited for: 11 -> 10; matrix products, arithmetic and copies ran while one was open for 2% -> 2% of each run, Pallas kernels for 27% -> 27%
where the time goes in v4:
time: 148 us
  Pallas kernels  66.4 us (45%)
  starting transfers between devices  37.6 us (25%)
  waiting for transfers between devices  36 us (24%)
  other arithmetic  2.99 us (2%)
  local copies, waits for them, and re-layouts  2.86 us (2%)
    pallas_call x14, Pallas kernels, call(): pl.pallas_call(kernel, out_shape=shapes, in_specs=specs, out_specs=out_sp...  66.4 us
    ppermute x18, starting transfers between devices, swap(): lax.ppermute(x, axis, [(i, i ^ bit) for i in range(lax.axis_size(axis))])  22.8 us
    ppermute x18, waiting for transfers between devices, swap(): lax.ppermute(x, axis, [(i, i ^ bit) for i in range(lax.axis_size(axis))])  16.9 us
    all_to_all x2, waiting for transfers between devices, spread(): lax.all_to_all(jnp.broadcast_to(block[None], (lax.axis_size(axis), *block...  12.7 us
    all_to_all x2, starting transfers between devices, scatter_sum(): lax.all_to_all(blocks, axis, 0, 0).astype(F32)  7.77 us
    all_to_all x2, starting transfers between devices, spread(): lax.all_to_all(jnp.broadcast_to(block[None], (lax.axis_size(axis), *block...  7.02 us
    all_to_all x2, waiting for transfers between devices, scatter_sum(): lax.all_to_all(blocks, axis, 0, 0).astype(F32)  6.44 us
  transfers between devices with their start and end apart: 22, of which 10 were waited for; matrix products, arithmetic and copies ran while one was open for 2% of the time, Pallas kernels for 27%

profile of v4, /device:TPU:0, one launch (start us, length us, event | category | flops | bytes accessed | tf_op | source)
XLA Modules:
  0.0 147.8 jit_solution(16302678928289614491)
XLA Ops:
  0.7 3.4 %shard_map.186 = (bf16[4,512,512]{2,1,0:T(8,128)(2,1)S(1)}, bf16[1536,512]{1,0:T(8,128)(2,1)S(1)}, f32[4,8,512]{2,1,0:T(8,128)S(1)}, f32[24,512]{1,0:T(8,128)S(1...) custom-call(s32[4,3]{1,0:T(4,128)} %len_ref.15, bf16[4,512,512]{2,1,0:T(8,128)(2,1)} %tok_hbm.6, ...), custom_call_target="tpu_custom_call" | custom-call | bytes 8388608 | tf_op jit(solution)/shard_map/pallas_call | solution.py:761
  4.2 3.1 %collective-permute-start = (f32[24,512]{1,0:T(8,128)S(1)}, f32[24,512]{1,0:T(8,128)S(1)}, u32[]{:S(2)}, u32[]{:S(2)}) collective-permute-start(f32[24,512]{1,0:T(8,128)S(1)} %get-tuple-element.70), channel_id=1, source_target_pairs={{0,1},{1,0},{2,3},{3,2},{4,5},{5,4},{6,7},{7,6},{8,9},{9,8},{10,11... | collective-permute-start | bytes 147464 | tf_op jit(solution)/shard_map/ppermute | solution.py:790
  7.2 2.9 %collective-permute-start.1 = (f32[24,512]{1,0:T(8,128)S(1)}, f32[24,512]{1,0:T(8,128)S(1)}, u32[]{:S(2)}, u32[]{:S(2)}) collective-permute-start(f32[24,512]{1,0:T(8,128)S(1)} %get-tuple-element.71), channel_id=1, source_target_pairs={{0,2},{1,3},{2,0},{3,1},{4,6},{5,7},{6,4},{7,5},{8,10},{9,11},{10,... | collective-permute-start | bytes 147464 | tf_op jit(solution)/shard_map/ppermute | solution.py:790
  10.5 2.6 %collective-permute-done.1.rx_ref_2_ = f32[24,512]{1,0:T(8,128)S(1)} collective-permute-done((f32[24,512]{1,0:T(8,128)S(1)}, f32[24,512]{1,0:T(8,128)S(1)}, u32[]{:S(2)}, u32[]{:S(2)}) %collective-permute-start.1) | collective-permute-done | bytes 49184 | tf_op jit(solution)/shard_map/ppermute | solution.py:790
  13.1 2.9 %collective-permute-done.2.rx_ref_3_ = f32[24,512]{1,0:T(8,128)S(1)} collective-permute-done((f32[24,512]{1,0:T(8,128)S(1)}, f32[24,512]{1,0:T(8,128)S(1)}, u32[]{:S(2)}, u32[]{:S(2)}) %collective-permute-start.2) | collective-permute-done | bytes 49184 | tf_op jit(solution)/shard_map/ppermute | solution.py:790
  16.0 7.6 %shard_map.187 = (bf16[4,544,512]{2,1,0:T(8,128)(2,1)S(1)}, f32[4,544,512]{2,1,0:T(8,128)S(1)}, f32[4,8,512]{2,1,0:T(8,128)S(1)}, f32[8,512]{1,0:T(8,128)S(1)}, ...) custom-call(s32[4,3]{1,0:T(4,128)S(1)} %copy-done.1, bf16[4,512,512]{2,1,0:T(8,128)(2,1)S(1)} %get-tuple-element.67.tok_ref, ...), custom_call_target="tpu_custom_call" | custom-call | flops 3221225472 | bytes 8388608 | tf_op jit(solution)/shard_map/pallas_call | solution.py:761
  23.7 2.0 %collective-permute-start.4 = (f32[8,512]{1,0:T(8,128)S(1)}, f32[8,512]{1,0:T(8,128)S(1)}, u32[]{:S(2)}, u32[]{:S(2)}) collective-permute-start(f32[8,512]{1,0:T(8,128)S(1)} %get-tuple-element.79.rx_ref_0_), channel_id=1, source_target_pairs={{0,2},{1,3},{2,0},{3,1},{4,6},{5,7},{6,4},{7,5},{8,10},{9,11},{10,... | collective-permute-start | bytes 49160 | tf_op jit(solution)/shard_map/ppermute | solution.py:790
  25.6 2.4 %collective-permute-start.5 = (f32[8,512]{1,0:T(8,128)S(1)}, f32[8,512]{1,0:T(8,128)S(1)}, u32[]{:S(2)}, u32[]{:S(2)}) collective-permute-start(f32[8,512]{1,0:T(8,128)S(1)} %get-tuple-element.79.rx_ref_0_), channel_id=1, source_target_pairs={{0,3},{1,2},{2,1},{3,0},{4,7},{5,6},{6,5},{7,4},{8,11},{9,10},{10,... | collective-permute-start | bytes 49160 | tf_op jit(solution)/shard_map/ppermute | solution.py:790
  28.1 7.3 %shard_map.188 = (bf16[4,512,1536]{2,1,0:T(8,128)(2,1)S(1)}, bf16[4,544,512]{2,1,0:T(8,128)(2,1)S(1)}, f32[8,512]{1,0:T(8,128)S(1)}) custom-call(s32[4,3]{1,0:T(4,128)S(1)} %copy-done.1, bf16[4,512,512]{2,1,0:T(8,128)(2,1)S(1)} %get-tuple-element.75.og_ref, f32[24,512]{1,0:T(8,128)S(1)} %get-tuple-element.69.rx_ref_0_, ...), custom_call_target="tpu_custom_call" | custom-call | flops 3221225472 | bytes 8388608 | tf_op jit(solution)/shard_map/pallas_call | solution.py:761
  35.4 4.2 %shard_map.189 = (bf16[4,544,512]{2,1,0:T(8,128)(2,1)S(1)}, bf16[4,544,512]{2,1,0:T(8,128)(2,1)S(1)}, f32[4,8,512]{2,1,0:T(8,128)S(1)}, f32[8,512]{1,0:T(8,128)S(1)}) custom-call(s32[4,3]{1,0:T(4,128)S(1)} %copy-done.1, f32[4,544,512]{2,1,0:T(8,128)S(1)} %get-tuple-element.74.hid_ref, bf16[4,544,512]{2,1,0:T(8,128)(2,1)S(1)} %get-tuple-element.77.q_ref, ...), custom_call_target="tpu_custom_call" | custom-call | bytes 8388608 | tf_op jit(solution)/shard_map/pallas_call | solution.py:761
  39.6 2.6 %shard_map.190 = (bf16[768,512]{1,0:T(8,128)(2,1)S(1)}, bf16[4,544,512]{2,1,0:T(8,128)(2,1)}) custom-call(bf16[4,544,512]{2,1,0:T(8,128)(2,1)S(1)} %get-tuple-element.80.low_ref, bf16[4,512,1536]{2,1,0:T(8,128)(2,1)S(1)} %get-tuple-element.84.gs_ref), custom_call_target="tpu_custom_call" | custom-call | bytes 8388608 | tf_op jit(solution)/shard_map/pallas_call | solution.py:761
  42.3 2.7 %collective-permute-start.8 = (f32[8,512]{1,0:T(8,128)S(1)}, f32[8,512]{1,0:T(8,128)S(1)}, u32[]{:S(2)}, u32[]{:S(2)}) collective-permute-start(f32[8,512]{1,0:T(8,128)S(1)} %get-tuple-element.85.grx_ref_0_), channel_id=1, source_target_pairs={{0,2},{1,3},{2,0},{3,1},{4,6},{5,7},{6,4},{7,5},{8,10},{9,11},{10,... | collective-permute-start | bytes 49160 | tf_op jit(solution)/shard_map/ppermute | solution.py:790
  46.7 2.5 %shard_map.191 = bf16[768,512]{1,0:T(8,128)(2,1)S(1)} custom-call(bf16[4,544,512]{2,1,0:T(8,128)(2,1)S(1)} %get-tuple-element.80.low_ref, bf16[4,512,1536]{2,1,0:T(8,128)(2,1)S(1)} %get-tuple-element.84.gs_ref), custom_call_target="tpu_custom_call" | custom-call | bytes 8388608 | tf_op jit(solution)/shard_map/pallas_call | solution.py:761
  50.8 6.4 %shard_map.192 = (bf16[4,544,512]{2,1,0:T(8,128)(2,1)}, bf16[4,512,1536]{2,1,0:T(8,128)(2,1)S(1)}, bf16[768,512]{1,0:T(8,128)(2,1)S(1)}, f32[16,1024]{1,0:T(8,128)S(1)}) custom-call(s32[4,3]{1,0:T(4,128)S(1)} %copy-done.1, bf16[4,544,512]{2,1,0:T(8,128)(2,1)S(1)} %get-tuple-element.87.low_ref, bf16[4,544,512]{2,1,0:T(8,128)(2,1)S(1)} %get-tuple-element.89.da_ref, ...), custom_call_target="tpu_custom_call" | custom-call | flops 3221225472 | bytes 8388608 | tf_op jit(solution)/shard_map/pallas_call | solution.py:761
  57.3 2.5 %shard_map.193 = bf16[768,512]{1,0:T(8,128)(2,1)S(1)} custom-call(bf16[4,544,512]{2,1,0:T(8,128)(2,1)S(1)} %get-tuple-element.87.low_ref, bf16[4,512,1536]{2,1,0:T(8,128)(2,1)S(1)} %get-tuple-element.93.gs_ref), custom_call_target="tpu_custom_call" | custom-call | bytes 8388608 | tf_op jit(solution)/shard_map/pallas_call | solution.py:761
  61.4 3.7 %all-to-all-start = ((bf16[4,384,512]{2,1,0:T(8,128)(2,1)}), bf16[4,384,512]{2,1,0:T(8,128)(2,1)S(1)}, u32[]{:S(2)}, u32[]{:S(2)}) async-start(bf16[4,384,512]{2,1,0:T(8,128)(2,1)} %bitcast.26), calls=%async_computation | async-start | bytes 3145728 | tf_op jit(solution)/shard_map/all_to_all | solution.py:782
  65.1 11.1 %shard_map.194 = (bf16[4,512,512]{2,1,0:T(8,128)(2,1)}, f32[4,8,512]{2,1,0:T(8,128)S(1)}, bf16[16,2048]{1,0:T(8,128)(2,1)S(1)}) custom-call(s32[4,3]{1,0:T(4,128)S(1)} %copy-done.1, bf16[4,544,512]{2,1,0:T(8,128)(2,1)} %get-tuple-element.95.g_hbm, bf16[1536,512]{1,0:T(8,128)(2,1)} %bitcast.30, bf16[4,512,512]{2,1,0:T(8,128)(2,1)} %tok_hbm.6, ...), custom_call_target="tpu_custom_call" | custom-call | flops 3221225472 | bytes 8388608 | tf_op jit(solution)/shard_map/pallas_call | solution.py:761
  76.2 3.1 %collective-permute-start.13 = (bf16[16,2048]{1,0:T(8,128)(2,1)S(1)}, bf16[16,2048]{1,0:T(8,128)(2,1)S(1)}, u32[]{:S(2)}, u32[]{:S(2)}) collective-permute-start(bf16[16,2048]{1,0:T(8,128)(2,1)S(1)} %get-tuple-element.99), channel_id=1, source_target_pairs={{0,3},{1,2},{2,1},{3,0},{4,7},{5,6},{6,5},{7,4},{8,11},{9,10},{10,... | collective-permute-start | bytes 196616 | tf_op jit(solution)/shard_map/ppermute | solution.py:790
  80.7 2.3 %collective-permute-done.13 = bf16[16,2048]{1,0:T(8,128)(2,1)S(1)} collective-permute-done((bf16[16,2048]{1,0:T(8,128)(2,1)S(1)}, bf16[16,2048]{1,0:T(8,128)(2,1)S(1)}, u32[]{:S(2)}, u32[]{:S(2)}) %collective-permute-start.13) | collective-permute-done | bytes 65568 | tf_op jit(solution)/shard_map/ppermute | solution.py:790
  83.0 2.5 %collective-permute-done.12 = bf16[16,2048]{1,0:T(8,128)(2,1)S(1)} collective-permute-done((bf16[16,2048]{1,0:T(8,128)(2,1)S(1)}, bf16[16,2048]{1,0:T(8,128)(2,1)S(1)}, u32[]{:S(2)}, u32[]{:S(2)}) %collective-permute-start.12) | collective-permute-done | bytes 65568 | tf_op jit(solution)/shard_map/ppermute | solution.py:790
  86.7 4.0 %all-to-all-start.1 = ((bf16[4,96,512]{2,1,0:T(8,128)(2,1)}), bf16[4,96,512]{2,1,0:T(8,128)(2,1)S(1)}, u32[]{:S(2)}, u32[]{:S(2)}) async-start(bf16[4,96,512]{2,1,0:T(8,128)(2,1)} %bitcast.9), calls=%async_computation.1 | async-start | bytes 786432 | tf_op jit(solution)/shard_map/all_to_all | solution.py:782
  92.5 4.1 %collective-permute-done.15 = bf16[32,2176]{1,0:T(8,128)(2,1)S(1)} collective-permute-done((bf16[32,2176]{1,0:T(8,128)(2,1)S(1)}, bf16[32,2176]{1,0:T(8,128)(2,1)S(1)}, u32[]{:S(2)}, u32[]{:S(2)}) %collective-permute-start.15) | collective-permute-done | bytes 139296 | tf_op jit(solution)/shard_map/ppermute | solution.py:790
  96.7 6.4 %all-to-all-done.1 = bf16[4,96,512]{2,1,0:T(8,128)(2,1)S(1)} async-done(((bf16[4,96,512]{2,1,0:T(8,128)(2,1)}), bf16[4,96,512]{2,1,0:T(8,128)(2,1)S(1)}, u32[]{:S(2)}, u32[]{:S(2)}) %all-to-all-start.1) | async-done | bytes 393248 | tf_op jit(solution)/shard_map/all_to_all | solution.py:782
  105.5 3.5 %all-to-all-start.2 = ((bf16[4,96,512]{2,1,0:T(8,128)(2,1)}), bf16[4,96,512]{2,1,0:T(8,128)(2,1)S(1)}, u32[]{:S(2)}, u32[]{:S(2)}) async-start(bf16[4,96,512]{2,1,0:T(8,128)(2,1)} %broadcast_in_dim.4), calls=%async_computation.2 | async-start | bytes 786432 | tf_op jit(solution)/shard_map/all_to_all | solution.py:786
  109.0 8.6 %shard_map.195 = bf16[4,512,512]{2,1,0:T(8,128)(2,1)} custom-call(s32[4,3]{1,0:T(4,128)S(1)} %copy-done.1, bf16[4,544,512]{2,1,0:T(8,128)(2,1)} %get-tuple-element.82.low_hbm, bf16[4,512,512]{2,1,0:T(8,128)(2,1)} %tok_hbm.6, bf16[1536,512]{1,0:T(8,128)(2,1)} %bitcast.35, bf16[1,512]{1,0:T(2,128)(2,1)S(1)} %reshape.75.bias_ref), custom_call_target="tpu_custom_call" | custom-call | flops 3221225472 | bytes 8388608 | tf_op jit(solution)/shard_map/pallas_call | solution.py:761
  117.6 2.6 %all-to-all-done.2 = bf16[4,96,512]{2,1,0:T(8,128)(2,1)S(1)} async-done(((bf16[4,96,512]{2,1,0:T(8,128)(2,1)}), bf16[4,96,512]{2,1,0:T(8,128)(2,1)S(1)}, u32[]{:S(2)}, u32[]{:S(2)}) %all-to-all-start.2) | async-done | bytes 393248 | tf_op jit(solution)/shard_map/all_to_all | solution.py:786
  121.5 3.6 %all-to-all-start.3 = ((bf16[4,4,96,512]{3,2,1,0:T(8,128)(2,1)}), bf16[4,4,96,512]{3,2,1,0:T(8,128)(2,1)S(1)}, u32[]{:S(2)}, u32[]{:S(2)}) async-start(bf16[4,4,96,512]{3,2,1,0:T(8,128)(2,1)} %broadcast_in_dim.5), calls=%async_computation.3 | async-start | bytes 3145728 | tf_op jit(solution)/shard_map/all_to_all | solution.py:786
  125.5 2.0 %shard_map.197 = (f32[128,1024]{1,0:T(8,128)}, f32[128,1024]{1,0:T(8,128)}, f32[1,1024]{1,0:T(1,128)}, f32[1,1024]{1,0:T(1,128)}, f32[1,512]{1,0:T(1,128)}) custom-call(bf16[128,2176]{1,0:T(8,128)(2,1)S(1)} %constant_dynamic-update-slice_fusion.all_ref), custom_call_target="tpu_custom_call" | custom-call | bytes 8388608 | tf_op jit(solution)/shard_map/pallas_call | solution.py:761
  127.5 4.8 %shard_map.196 = bf16[4,512,512]{2,1,0:T(8,128)(2,1)} custom-call(s32[4,3]{1,0:T(4,128)S(1)} %copy-done.1, bf16[4,512,512]{2,1,0:T(8,128)(2,1)} %og_hbm.5, bf16[4,512,512]{2,1,0:T(8,128)(2,1)} %get-tuple-element.105.da_hbm, bf16[4,512,512]{2,1,0:T(8,128)(2,1)} %tok_hbm.6, f32[4,8,512]{2,1,0:T(8,128)S(1)} %get-tuple-element.68.st_ref, ...), custom_call_target="tpu_custom_call" | custom-call | bytes 8388608 | tf_op jit(solution)/shard_map/pallas_call | solution.py:761
  132.3 10.1 %all-to-all-done.3 = bf16[4,4,96,512]{3,2,1,0:T(8,128)(2,1)S(1)} async-done(((bf16[4,4,96,512]{3,2,1,0:T(8,128)(2,1)}), bf16[4,4,96,512]{3,2,1,0:T(8,128)(2,1)S(1)}, u32[]{:S(2)}, u32[]{:S(2)}) %all-to-all-start.3) | async-done | bytes 1572896 | tf_op jit(solution)/shard_map/all_to_all | solution.py:786
  142.5 1.8 %shard_map.198 = (f32[3,512,512]{2,1,0:T(8,128)}, f32[3,512,512]{2,1,0:T(8,128)}) custom-call(bf16[4,4,2,48,512]{4,3,2,1,0:T(8,128)(2,1)S(1)} %bitcast.25), custom_call_target="tpu_custom_call" | custom-call | bytes 8388608 | tf_op jit(solution)/shard_map/pallas_call | solution.py:761
  145.9 1.8 %shard_map.199 = (f32[3,512,512]{2,1,0:T(8,128)}, f32[3,512,512]{2,1,0:T(8,128)}) custom-call(bf16[4,4,2,48,512]{4,3,2,1,0:T(8,128)(2,1)S(1)} %collective-permute-done.17.half_ref, f32[3,512,512]{2,1,0:T(8,128)} %get-tuple-element.117.refs_0_, f32[3,512,512]{2,1,0:T(8,128)} %get-tuple-element.118.refs_1_), custom_call_target="tpu_custom_call", output_to_operand_aliasing={{0}: (1, {}), {1}: (2, {})} | custom-call | bytes 8388608 | tf_op jit(solution)/shard_map/pallas_call | solution.py:761
  (66 shorter events, 15.6 us)
Async XLA Ops:
  0.6 9.5 %copy-start = (bf16[128,1024]{1,0:T(8,128)(2,1)S(1)}, bf16[128,1024]{1,0:T(8,128)(2,1)}, u32[]{:S(2)}) copy-start(bf16[128,1024]{1,0:T(8,128)(2,1)} %param.14) | copy-start | bytes 786436
  0.7 9.5 %copy-start.4 = (bf16[1024]{0:T(1024)(128)(2,1)S(1)}, bf16[1024]{0:T(1024)(128)(2,1)}, u32[]{:S(2)}) copy-start(bf16[1024]{0:T(1024)(128)(2,1)} %param.15) | copy-start | bytes 6148
  0.7 9.5 %copy-start.5 = (bf16[1024]{0:T(1024)(128)(2,1)S(1)}, bf16[1024]{0:T(1024)(128)(2,1)}, u32[]{:S(2)}) copy-start(bf16[1024]{0:T(1024)(128)(2,1)} %param.18) | copy-start | bytes 6148
  0.7 9.5 %copy-start.3 = (bf16[4,3,128]{2,0,1:T(4,128)(2,1)S(1)}, bf16[4,3,128]{2,0,1:T(4,128)(2,1)}, u32[]{:S(2)}) copy-start(bf16[4,3,128]{2,0,1:T(4,128)(2,1)} %param.13) | copy-start | bytes 9220
  0.7 9.7 %copy-start.2 = (bf16[128,1024]{1,0:T(8,128)(2,1)S(1)}, bf16[128,1024]{1,0:T(8,128)(2,1)}, u32[]{:S(2)}) copy-start(bf16[128,1024]{1,0:T(8,128)(2,1)} %param.17) | copy-start | bytes 786436
  0.7 15.3 %copy-start.1 = (s32[4,3]{1,0:T(4,128)S(1)}, s32[4,3]{1,0:T(4,128)}, u32[]{:S(2)}) copy-start(s32[4,3]{1,0:T(4,128)} %len_ref.15) | copy-start | bytes 148
  4.2 6.4 %collective-permute-start = (f32[24,512]{1,0:T(8,128)S(1)}, f32[24,512]{1,0:T(8,128)S(1)}, u32[]{:S(2)}, u32[]{:S(2)}) collective-permute-start(f32[24,512]{1,0:T(8,128)S(1)} %get-tuple-element.70), channel_id=1, source_target_pairs={{0,1},{1,0},{2,3},{3,2},{4,5},{5,4},{6,7},{7,6},{8,9},{9,8},{10,11... | collective-permute-start | bytes 147464 | tf_op jit(solution)/shard_map/ppermute | solution.py:790
  7.2 5.9 %collective-permute-start.1 = (f32[24,512]{1,0:T(8,128)S(1)}, f32[24,512]{1,0:T(8,128)S(1)}, u32[]{:S(2)}, u32[]{:S(2)}) collective-permute-start(f32[24,512]{1,0:T(8,128)S(1)} %get-tuple-element.71), channel_id=1, source_target_pairs={{0,2},{1,3},{2,0},{3,1},{4,6},{5,7},{6,4},{7,5},{8,10},{9,11},{10,... | collective-permute-start | bytes 147464 | tf_op jit(solution)/shard_map/ppermute | solution.py:790
  10.1 5.9 %collective-permute-start.2 = (f32[24,512]{1,0:T(8,128)S(1)}, f32[24,512]{1,0:T(8,128)S(1)}, u32[]{:S(2)}, u32[]{:S(2)}) collective-permute-start(f32[24,512]{1,0:T(8,128)S(1)} %get-tuple-element.72), channel_id=1, source_target_pairs={{0,3},{1,2},{2,1},{3,0},{4,7},{5,6},{6,5},{7,4},{8,11},{9,10},{10,... | collective-permute-start | bytes 147464 | tf_op jit(solution)/shard_map/ppermute | solution.py:790
  23.6 11.8 %collective-permute-start.3 = (f32[8,512]{1,0:T(8,128)S(1)}, f32[8,512]{1,0:T(8,128)S(1)}, u32[]{:S(2)}, u32[]{:S(2)}) collective-permute-start(f32[8,512]{1,0:T(8,128)S(1)} %get-tuple-element.79.rx_ref_0_), channel_id=1, source_target_pairs={{0,1},{1,0},{2,3},{3,2},{4,5},{5,4},{6,7},{7,6},{8,9},{9,8},{10,11... | collective-permute-start | bytes 49160 | tf_op jit(solution)/shard_map/ppermute | solution.py:790
  23.7 11.7 %collective-permute-start.4 = (f32[8,512]{1,0:T(8,128)S(1)}, f32[8,512]{1,0:T(8,128)S(1)}, u32[]{:S(2)}, u32[]{:S(2)}) collective-permute-start(f32[8,512]{1,0:T(8,128)S(1)} %get-tuple-element.79.rx_ref_0_), channel_id=1, source_target_pairs={{0,2},{1,3},{2,0},{3,1},{4,6},{5,7},{6,4},{7,5},{8,10},{9,11},{10,... | collective-permute-start | bytes 49160 | tf_op jit(solution)/shard_map/ppermute | solution.py:790
  25.6 9.8 %collective-permute-start.5 = (f32[8,512]{1,0:T(8,128)S(1)}, f32[8,512]{1,0:T(8,128)S(1)}, u32[]{:S(2)}, u32[]{:S(2)}) collective-permute-start(f32[8,512]{1,0:T(8,128)S(1)} %get-tuple-element.79.rx_ref_0_), channel_id=1, source_target_pairs={{0,3},{1,2},{2,1},{3,0},{4,7},{5,6},{6,5},{7,4},{8,11},{9,10},{10,... | collective-permute-start | bytes 49160 | tf_op jit(solution)/shard_map/ppermute | solution.py:790
  42.2 8.4 %collective-permute-start.6 = (bf16[768,512]{1,0:T(8,128)(2,1)S(1)}, bf16[768,512]{1,0:T(8,128)(2,1)S(1)}, u32[]{:S(2)}, u32[]{:S(2)}) collective-permute-start(bf16[768,512]{1,0:T(8,128)(2,1)S(1)} %get-tuple-element.83), channel_id=1, source_target_pairs={{0,4},{4,0},{1,5},{5,1},{2,6},{6,2},{3,7},{7,3},{8,12},{12,8},{9,1... | collective-permute-start | bytes 2359304 | tf_op jit(solution)/shard_map/ppermute | solution.py:790
  42.2 7.0 %collective-permute-start.7 = (f32[8,512]{1,0:T(8,128)S(1)}, f32[8,512]{1,0:T(8,128)S(1)}, u32[]{:S(2)}, u32[]{:S(2)}) collective-permute-start(f32[8,512]{1,0:T(8,128)S(1)} %get-tuple-element.85.grx_ref_0_), channel_id=1, source_target_pairs={{0,1},{1,0},{2,3},{3,2},{4,5},{5,4},{6,7},{7,6},{8,9},{9,8},{10,11... | collective-permute-start | bytes 49160 | tf_op jit(solution)/shard_map/ppermute | solution.py:790
  42.3 6.9 %collective-permute-start.8 = (f32[8,512]{1,0:T(8,128)S(1)}, f32[8,512]{1,0:T(8,128)S(1)}, u32[]{:S(2)}, u32[]{:S(2)}) collective-permute-start(f32[8,512]{1,0:T(8,128)S(1)} %get-tuple-element.85.grx_ref_0_), channel_id=1, source_target_pairs={{0,2},{1,3},{2,0},{3,1},{4,6},{5,7},{6,4},{7,5},{8,10},{9,11},{10,... | collective-permute-start | bytes 49160 | tf_op jit(solution)/shard_map/ppermute | solution.py:790
  45.1 5.5 %collective-permute-start.9 = (f32[8,512]{1,0:T(8,128)S(1)}, f32[8,512]{1,0:T(8,128)S(1)}, u32[]{:S(2)}, u32[]{:S(2)}) collective-permute-start(f32[8,512]{1,0:T(8,128)S(1)} %get-tuple-element.85.grx_ref_0_), channel_id=1, source_target_pairs={{0,3},{1,2},{2,1},{3,0},{4,7},{5,6},{6,5},{7,4},{8,11},{9,10},{10,... | collective-permute-start | bytes 49160 | tf_op jit(solution)/shard_map/ppermute | solution.py:790
  57.2 2.6 %collective-permute-start.10 = (bf16[768,512]{1,0:T(8,128)(2,1)S(1)}, bf16[768,512]{1,0:T(8,128)(2,1)S(1)}, u32[]{:S(2)}, u32[]{:S(2)}) collective-permute-start(bf16[768,512]{1,0:T(8,128)(2,1)S(1)} %get-tuple-element.91), channel_id=1, source_target_pairs={{0,4},{4,0},{1,5},{5,1},{2,6},{6,2},{3,7},{7,3},{8,12},{12,8},{9,1... | collective-permute-start | bytes 2359304 | tf_op jit(solution)/shard_map/ppermute | solution.py:790
  61.4 24.3 %all-to-all-start = ((bf16[4,384,512]{2,1,0:T(8,128)(2,1)}), bf16[4,384,512]{2,1,0:T(8,128)(2,1)S(1)}, u32[]{:S(2)}, u32[]{:S(2)}) async-start(bf16[4,384,512]{2,1,0:T(8,128)(2,1)} %bitcast.26), calls=%async_computation | async-start | bytes 3145728 | tf_op jit(solution)/shard_map/all_to_all | solution.py:782
  76.2 16.3 %copy-start.6 = (bf16[512]{0:T(512)(128)(2,1)S(1)}, bf16[512]{0:T(512)(128)(2,1)}, u32[]{:S(2)}) copy-start(bf16[512]{0:T(512)(128)(2,1)} %param.20) | copy-start | bytes 3076
  76.2 6.7 %collective-permute-start.13 = (bf16[16,2048]{1,0:T(8,128)(2,1)S(1)}, bf16[16,2048]{1,0:T(8,128)(2,1)S(1)}, u32[]{:S(2)}, u32[]{:S(2)}) collective-permute-start(bf16[16,2048]{1,0:T(8,128)(2,1)S(1)} %get-tuple-element.99), channel_id=1, source_target_pairs={{0,3},{1,2},{2,1},{3,0},{4,7},{5,6},{6,5},{7,4},{8,11},{9,10},{10,... | collective-permute-start | bytes 196616 | tf_op jit(solution)/shard_map/ppermute | solution.py:790
  79.3 6.2 %collective-permute-start.12 = (bf16[16,2048]{1,0:T(8,128)(2,1)S(1)}, bf16[16,2048]{1,0:T(8,128)(2,1)S(1)}, u32[]{:S(2)}, u32[]{:S(2)}) collective-permute-start(bf16[16,2048]{1,0:T(8,128)(2,1)S(1)} %get-tuple-element.99), channel_id=1, source_target_pairs={{0,1},{1,0},{2,3},{3,2},{4,5},{5,4},{6,7},{7,6},{8,9},{9,8},{10,11... | collective-permute-start | bytes 196616 | tf_op jit(solution)/shard_map/ppermute | solution.py:790
  79.3 6.2 %collective-permute-start.11 = (bf16[16,2048]{1,0:T(8,128)(2,1)S(1)}, bf16[16,2048]{1,0:T(8,128)(2,1)S(1)}, u32[]{:S(2)}, u32[]{:S(2)}) collective-permute-start(bf16[16,2048]{1,0:T(8,128)(2,1)S(1)} %get-tuple-element.99), channel_id=1, source_target_pairs={{0,2},{1,3},{2,0},{3,1},{4,6},{5,7},{6,4},{7,5},{8,10},{9,11},{10,... | collective-permute-start | bytes 196616 | tf_op jit(solution)/shard_map/ppermute | solution.py:790
  85.6 5.2 %collective-permute-start.14 = (bf16[16,2176]{1,0:T(8,128)(2,1)S(1)}, bf16[16,2176]{1,0:T(8,128)(2,1)S(1)}, u32[]{:S(2)}, u32[]{:S(2)}) collective-permute-start(bf16[16,2176]{1,0:T(8,128)(2,1)S(1)} %pad_maximum_fusion.3), channel_id=1, source_target_pairs={{0,4},{4,0},{1,5},{5,1},{2,6},{6,2},{3,7},{7,3},{8,12},{12,8},{9,1... | collective-permute-start | bytes 208904 | tf_op jit(solution)/shard_map/ppermute | solution.py:790
  86.7 16.4 %all-to-all-start.1 = ((bf16[4,96,512]{2,1,0:T(8,128)(2,1)}), bf16[4,96,512]{2,1,0:T(8,128)(2,1)S(1)}, u32[]{:S(2)}, u32[]{:S(2)}) async-start(bf16[4,96,512]{2,1,0:T(8,128)(2,1)} %bitcast.9), calls=%async_computation.1 | async-start | bytes 786432 | tf_op jit(solution)/shard_map/all_to_all | solution.py:782
  90.8 5.9 %collective-permute-start.15 = (bf16[32,2176]{1,0:T(8,128)(2,1)S(1)}, bf16[32,2176]{1,0:T(8,128)(2,1)S(1)}, u32[]{:S(2)}, u32[]{:S(2)}) collective-permute-start(bf16[32,2176]{1,0:T(8,128)(2,1)S(1)} %pad_maximum_fusion.2), channel_id=1, source_target_pairs={{0,8},{8,0},{16,24},{24,16},{1,9},{9,1},{17,25},{25,17},{2,10},{10... | collective-permute-start | bytes 417800 | tf_op jit(solution)/shard_map/ppermute | solution.py:790
  103.2 14.4 %collective-permute-start.16 = (bf16[64,2176]{1,0:T(8,128)(2,1)S(1)}, bf16[64,2176]{1,0:T(8,128)(2,1)S(1)}, u32[]{:S(2)}, u32[]{:S(2)}) collective-permute-start(bf16[64,2176]{1,0:T(8,128)(2,1)S(1)} %pad_maximum_fusion.1), channel_id=1, source_target_pairs={{0,16},{8,24},{16,0},{24,8},{1,17},{9,25},{17,1},{25,9},{2,18},{10... | collective-permute-start | bytes 835592 | tf_op jit(solution)/shard_map/ppermute | solution.py:790
  105.5 14.7 %all-to-all-start.2 = ((bf16[4,96,512]{2,1,0:T(8,128)(2,1)}), bf16[4,96,512]{2,1,0:T(8,128)(2,1)S(1)}, u32[]{:S(2)}, u32[]{:S(2)}) async-start(bf16[4,96,512]{2,1,0:T(8,128)(2,1)} %broadcast_in_dim.4), calls=%async_computation.2 | async-start | bytes 786432 | tf_op jit(solution)/shard_map/all_to_all | solution.py:786
  121.5 21.0 %all-to-all-start.3 = ((bf16[4,4,96,512]{3,2,1,0:T(8,128)(2,1)}), bf16[4,4,96,512]{3,2,1,0:T(8,128)(2,1)S(1)}, u32[]{:S(2)}, u32[]{:S(2)}) async-start(bf16[4,4,96,512]{3,2,1,0:T(8,128)(2,1)} %broadcast_in_dim.5), calls=%async_computation.3 | async-start | bytes 3145728 | tf_op jit(solution)/shard_map/all_to_all | solution.py:786
  142.5 3.4 %collective-permute-start.17 = (bf16[4,4,2,48,512]{4,3,2,1,0:T(8,128)(2,1)S(1)}, bf16[4,4,2,48,512]{4,3,2,1,0:T(8,128)(2,1)S(1)}, u32[]{:S(2)}, u32[]{:S(2)}) collective-permute-start(bf16[4,4,2,48,512]{4,3,2,1,0:T(8,128)(2,1)S(1)} %bitcast.24), channel_id=1, source_target_pairs={{0,4},{4,0},{1,5},{5,1},{2,6},{6,2},{3,7},{7,3},{8,12},{12,8},{9,1... | collective-permute-start | bytes 4718600 | tf_op jit(solution)/shard_map/ppermute | solution.py:790
